TPU v7x, 32 devices: a whole 2x2x4 slice. The times are simulated.
32 devices in a mesh: tile: 8 (over y, x, core), spec: 4 (over z).
Axes of the slice: x: 2, y: 2, z: 4, core: 2. Of those that a mesh axis runs over, the one named last changes fastest.
Arguments:
- concentrations: float32 [32, 512, 256], P('spec', 'tile'), may hold values from 0.1 to 4
- courant: float32 [512, 256], P('tile'), may hold values from 0.05 to 0.95
- first_weight: bfloat16 [32, 512], replicated, may hold values from -1 to 1
- middle_weight: bfloat16 [512, 512], replicated, may hold values from -0.25 to 0.25
- last_weight: bfloat16 [512, 32], replicated, may hold values from -0.25 to 0.25
- active_blocks: int32 [8, 4, 16], P('tile', 'spec'), may hold values from 0 to 32, as said below
- dest_tile: int32 [8, 4, 16], P('tile', 'spec'), may hold values from 0 to 7, as said below
Outputs:
- chemistry_out: bfloat16 [32, 131072], P(None, ('tile', 'spec'))
- load_share: float32 [8, 4], P('tile', 'spec')
Inputs may be any that keep to these rules, and one draw needn't show every extreme that they name: `active_blocks`: each device's entries name distinct blocks of its own 32; the value 32 marks an empty slot. `dest_tile`: A listed block's tile lies within 2 tiles of its home tile along the periodic order of tiles; an empty slot names the home tile. At most 2 blocks of one device name one other tile, and at most 8 listed blocks over all devices of one spec index name one tile; both bounds are reached in every draw.
All inputs are finite; a program needn't handle non-finite values.
Results may differ from a plain program's by a relative error of at most 0.0035.
Values may be sent and summed in bfloat16 or wider, within the bound.
No kernel may reach another device: no remote copies, remote signals or barrier semaphores. Data moves between devices by JAX's collectives and lax.ppermute only.
A program may use at most 64 MiB of HBM per device.

v0:
```python
import jax
import jax.numpy as jnp
from jax import lax
from jax.sharding import PartitionSpec as P

BLK = 128
NB = 32
RECV = 8
NBR = 2


def from_behind(value, axis, steps):
    count = lax.axis_size(axis)
    pairs = [(source, (source + steps) % count) for source in range(count)]
    return lax.ppermute(value, axis, pairs)


def extended(x, sides, width):
    for axis, dim in sides:
        devices, length = (lax.axis_size(axis), x.shape[dim])
        up = [(i, (i + 1) % devices) for i in range(devices)]
        down = [(j, i) for i, j in up]
        last = lax.slice_in_dim(x, length - width, length, axis=dim)
        initial = lax.slice_in_dim(x, 0, width, axis=dim)
        before = lax.ppermute(last, axis, up)
        after = lax.ppermute(initial, axis, down)
        x = jnp.concatenate([before, x, after], axis=dim)
    return x


def advect(values, courants):
    centre = values[:, 1:-1]
    left_diff = centre - values[:, :-2]
    right_diff = values[:, 2:] - centre
    slopes = jnp.where(
        left_diff * right_diff > 0,
        jnp.sign(left_diff) * jnp.minimum(jnp.abs(left_diff), jnp.abs(right_diff)),
        0.0,
    )
    fluxes = courants * (centre + 0.5 * (1.0 - courants) * slopes)
    return centre[:, 1:] - fluxes[:, 1:] + fluxes[:, :-1]


def surrogate(inputs, first_weight, middle_weight, last_weight):
    first_layer = jax.nn.silu(
        jnp.dot(first_weight.T, inputs, preferred_element_type=jnp.float32)
    ).astype(jnp.bfloat16)
    second = jax.nn.silu(
        jnp.dot(middle_weight.T, first_layer, preferred_element_type=jnp.float32)
    ).astype(jnp.bfloat16)
    change = jnp.dot(last_weight.T, second, preferred_element_type=jnp.float32)
    return (inputs.astype(jnp.float32) + change).astype(jnp.bfloat16)


def shards(
    concentrations, courant, first_weight, middle_weight, last_weight, active_blocks, dest_tile
):
    species_dev, shard_len, level_cols = concentrations.shape
    before = from_behind(courant[shard_len - 1 :], "tile", 1)
    rates_ext = jnp.concatenate([before, courant], axis=0)
    swept_field = concentrations
    for repeat in range(2):
        padded = extended(swept_field, (("tile", 1),), 2)
        swept_field = advect(padded[:, : shard_len + 3], rates_ext)
    advected = swept_field.astype(jnp.bfloat16).reshape(species_dev, shard_len * level_cols)
    regrouped = lax.all_to_all(advected, "spec", split_axis=1, concat_axis=0, tiled=True)
    species = regrouped.shape[0]
    grid_cell_block_list = regrouped.reshape(species, NB, BLK)
    listing = active_blocks.reshape(-1)
    targets = dest_tile.reshape(-1)
    slot_total = listing.shape[0]
    is_valid = listing < NB
    select_table = listing[:, None] == jnp.arange(NB, dtype=jnp.int32)[None, :]
    tiles_total = lax.axis_size("tile")
    home_tile = lax.axis_index("tile")
    offsets = (targets - home_tile + tiles_total // 2) % tiles_total - tiles_total // 2
    distances = [step_by for step_by in range(1, NBR + 1)] + [
        -step_by for step_by in range(1, NBR + 1)
    ]
    resident_selection = select_table.astype(jnp.bfloat16)
    picked = jnp.einsum(
        "au,cud->cad", resident_selection, grid_cell_block_list, preferred_element_type=jnp.float32
    ).astype(jnp.bfloat16)
    refreshed_state = surrogate(
        picked.reshape(species, slot_total * BLK), first_weight, middle_weight, last_weight
    )
    refreshed_state = refreshed_state.reshape(species, slot_total, BLK)
    assigned_blocks = jnp.einsum(
        "zu,xzi->xui", resident_selection, refreshed_state, preferred_element_type=jnp.float32
    )
    covered = jnp.sum(resident_selection.astype(jnp.float32), axis=0)
    own_total = jnp.sum((is_valid & (offsets == 0)).astype(jnp.float32)).reshape(1)
    for distance in distances:
        named_count = jnp.sum((is_valid & (offsets == distance)).astype(jnp.float32)).reshape(1)
        own_total = own_total + from_behind(named_count, "tile", distance)
    load_share = (own_total / RECV).reshape(1, 1)
    new_blocks = jnp.where(
        covered[None, :, None] > 0.5, assigned_blocks.astype(jnp.bfloat16), grid_cell_block_list
    )
    return (new_blocks.reshape(species, NB * BLK), load_share)


def solution(mesh):
    in_specs = (
        P("spec", "tile", None),
        P("tile", None),
        P(),
        P(),
        P(),
        P("tile", "spec", None),
        P("tile", "spec", None),
    )
    out_specs = (P(None, ("tile", "spec")), P("tile", "spec"))
    return jax.shard_map(shards, mesh=mesh, in_specs=in_specs, out_specs=out_specs, check_vma=False)
```

profile of v0, /device:TPU:0, one launch (start us, length us, event | category | flops | bytes accessed | tf_op | source)
XLA Modules:
  0.0 37.6 jit_solution(18423801778446919984)
XLA Ops:
  0.6 0.0 copy-start
  0.6 0.8 %slice.63 = f32[1,256]{1,0:T(1,128)S(1)} slice(f32[64,256]{1,0:T(8,128)} %param.8), slice={[63:64], [0:256]} | slice | bytes 2048 | tf_op jit(solution)/shard_map/slice | solution.py:59
  1.4 0.5 %collective-permute-start = (f32[1,256]{1,0:T(1,128)S(1)}, f32[1,256]{1,0:T(1,128)S(1)}, u32[]{:S(2)}, u32[]{:S(2)}) collective-permute-start(f32[1,256]{1,0:T(1,128)S(1)} %slice.63), channel_id=1, source_target_pairs={{0,4},{4,8},{8,12},{12,16},{16,20},{20,24},{24,28},{28,0},{1,5},{5... | collective-permute-start | bytes 3080 | tf_op jit(solution)/shard_map/ppermute | solution.py:15
  1.9 0.9 %fusion.40 = (f32[8,2,256]{2,1,0:T(2,128)S(1)}, f32[8,2,256]{2,1,0:T(2,128)S(1)}) fusion(f32[8,64,256]{2,1,0:T(8,128)} %param.7), kind=kLoop, calls=%fused_computation.70 | loop fusion | bytes 65536 | tf_op jit(solution)/shard_map/slice | solution.py:24
  2.7 2.7 %collective-permute-start.1 = (f32[8,2,256]{2,1,0:T(2,128)S(1)}, f32[8,2,256]{2,1,0:T(2,128)S(1)}, u32[]{:S(2)}, u32[]{:S(2)}) collective-permute-start(f32[8,2,256]{2,1,0:T(2,128)S(1)} %get-tuple-element.10), channel_id=1, source_target_pairs={{0,4},{4,8},{8,12},{12,16},{16,20},{20,24},{24,28},{28,0},{1,5},{5... | collective-permute-start | bytes 49160 | tf_op jit(solution)/shard_map/ppermute | solution.py:25
  5.4 0.3 collective-permute-start.2
  5.7 0.2 collective-permute-done
  6.0 0.9 %pad_maximum_fusion.4 = (f32[65,256]{1,0:T(8,128)S(1)}, f32[65,256]{1,0:T(8,128)S(1)}) fusion(f32[64,256]{1,0:T(8,128)} %param.8, f32[1,256]{1,0:T(1,128)S(1)} %collective-permute-done), kind=kLoop, calls=%fused_computation.43 | loop fusion | flops 49920 | bytes 199680 | tf_op jit(solution)/shard_map/concatenate | solution.py:60
  6.8 0.3 collective-permute-done.1
  7.1 0.1 collective-permute-done.2
  7.2 2.1 %add_multiply_fusion.1 = f32[8,65,256]{2,1,0:T(8,128)S(1)} fusion(f32[8,64,256]{2,1,0:T(8,128)} %param.7, f32[8,2,256]{2,1,0:T(2,128)S(1)} %collective-permute-done.1, f32[8,2,256]{2,1,0:T(2,128)S(1)} %collective-permute-done.2, f32[65,256]{1,0:T(8,128)S(1)} %get-tuple-element.12, f32[65,256]{1,0:T(8,128)S(1)} %get-tuple-element.11), kind=kLoop, calls=%fused_computation.33 | loop fusion | flops 2129920 | bytes 1222656 | tf_op jit(solution)/shard_map/mul | solution.py:40
  9.3 1.1 %slice_add_fusion.1 = f32[8,64,256]{2,1,0:T(8,128)S(1)} fusion(f32[8,65,256]{2,1,0:T(8,128)S(1)} %add_multiply_fusion.1, f32[8,64,256]{2,1,0:T(8,128)} %param.7), kind=kLoop, calls=%fused_computation.38 | loop fusion | flops 262144 | bytes 2097152 | tf_op jit(solution)/shard_map/add | solution.py:41
  10.4 1.5 %collective-permute-start.3 = (f32[8,2,256]{2,1,0:T(2,128)S(1)}, f32[8,2,256]{2,1,0:T(2,128)S(1)}, u32[]{:S(2)}, u32[]{:S(2)}) collective-permute-start(f32[8,2,256]{2,1,0:T(2,128)S(1)} %get-tuple-element.8), channel_id=1, source_target_pairs={{0,4},{4,8},{8,12},{12,16},{16,20},{20,24},{24,28},{28,0},{1,5},{5... | collective-permute-start | bytes 49160 | tf_op jit(solution)/shard_map/ppermute | solution.py:25
  11.9 1.2 %collective-permute-start.4 = (f32[8,2,256]{2,1,0:T(2,128)S(1)}, f32[8,2,256]{2,1,0:T(2,128)S(1)}, u32[]{:S(2)}, u32[]{:S(2)}) collective-permute-start(f32[8,2,256]{2,1,0:T(2,128)S(1)} %get-tuple-element.7), channel_id=1, source_target_pairs={{4,0},{8,4},{12,8},{16,12},{20,16},{24,20},{28,24},{0,28},{5,1},{9... | collective-permute-start | bytes 49160 | tf_op jit(solution)/shard_map/ppermute | solution.py:26
  13.2 0.0 copy-start.1
  13.2 0.0 copy-start.2
  13.2 1.4 %collective-permute-done.3 = f32[8,2,256]{2,1,0:T(2,128)S(1)} collective-permute-done((f32[8,2,256]{2,1,0:T(2,128)S(1)}, f32[8,2,256]{2,1,0:T(2,128)S(1)}, u32[]{:S(2)}, u32[]{:S(2)}) %collective-permute-start.3) | collective-permute-done | bytes 16416 | tf_op jit(solution)/shard_map/ppermute | solution.py:25
  14.5 0.1 collective-permute-done.4
  14.6 0.5 %add_multiply_fusion = f32[8,65,256]{2,1,0:T(8,128)S(1)} fusion(f32[8,64,256]{2,1,0:T(8,128)S(1)} %slice_add_fusion.1, f32[8,2,256]{2,1,0:T(2,128)S(1)} %collective-permute-done.3, f32[8,2,256]{2,1,0:T(2,128)S(1)} %collective-permute-done.4, f32[65,256]{1,0:T(8,128)S(1)} %get-tuple-element.12, f32[65,256]{1,0:T(8,128)S(1)} %get-tuple-element.11), kind=kLoop, calls=%fused_computation.31 | loop fusion | flops 2129920 | bytes 1222656 | tf_op jit(solution)/shard_map/mul | solution.py:40
  15.1 0.0 copy-start.3
  15.1 0.1 fusion.22
  15.2 0.2 all_to_all.12
  15.4 0.9 %copy.9 = bf16[8,4,4096]{2,0,1:T(8,128)(2,1)} copy(bf16[8,4,4096]{2,1,0:T(4,128)(2,1)S(1)} %all_to_all.12) | data formatting | bytes 524288 | tf_op jit(solution)/shard_map/all_to_all | solution.py:66
  16.2 5.6 %all-to-all-start = ((bf16[8,4,4096]{2,0,1:T(8,128)(2,1)}), bf16[8,4,4096]{2,0,1:T(8,128)(2,1)S(1)}, u32[]{:S(2)}, u32[]{:S(2)}) async-start(bf16[8,4,4096]{2,0,1:T(8,128)(2,1)} %copy.9), calls=%async_computation | async-start | bytes 524288 | tf_op jit(solution)/shard_map/all_to_all | solution.py:66
  21.8 0.0 copy-done.1
  21.8 0.0 copy-done.2
  21.8 0.7 %fusion.36 = (f32[]{:T(128)}, f32[]{:T(128)}, f32[]{:T(128)}, f32[]{:T(128)}, f32[]{:T(128)}) fusion(s32[1,1,16]{2,1,0:T(1,128)S(1)} %copy-done.1, s32[1,1,16]{2,1,0:T(1,128)S(1)} %copy-done.2, s32[]{:T(128)S(6)} %axis_index.15), kind=kLoop, calls=%fused_computation.64 | loop fusion | flops 555 | bytes 152 | tf_op jit(solution)/shard_map/reduce_sum | solution.py:94
  22.5 0.2 collective-permute-start.5
  22.7 2.6 %collective-permute-start.6 = (f32[1]{0:T(128)}, f32[1]{0:T(128)}, u32[]{:S(2)}, u32[]{:S(2)}) collective-permute-start(f32[1]{0:T(128)} %bitcast.11), channel_id=1, source_target_pairs={{0,8},{4,12},{8,16},{12,20},{16,24},{20,28},{24,0},{28,4},{1,9},{5... | collective-permute-start | bytes 20 | tf_op jit(solution)/shard_map/ppermute | solution.py:15
  25.3 0.0 collective-permute-start.7
  25.3 1.6 %collective-permute-start.8 = (f32[1]{0:T(128)}, f32[1]{0:T(128)}, u32[]{:S(2)}, u32[]{:S(2)}) collective-permute-start(f32[1]{0:T(128)} %bitcast.13), channel_id=1, source_target_pairs={{0,24},{4,28},{8,0},{12,4},{16,8},{20,12},{24,16},{28,20},{1,25},{... | collective-permute-start | bytes 20 | tf_op jit(solution)/shard_map/ppermute | solution.py:15
  26.9 0.1 convert_reduce_fusion
  27.0 0.0 collective-permute-done.5
  28.2 0.0 collective-permute-done.6
  28.9 0.0 collective-permute-done.7
  29.6 0.0 collective-permute-done.8
  30.2 1.2 %all-to-all-done = bf16[8,4,4096]{2,0,1:T(8,128)(2,1)S(1)} async-done(((bf16[8,4,4096]{2,0,1:T(8,128)(2,1)}), bf16[8,4,4096]{2,0,1:T(8,128)(2,1)S(1)}, u32[]{:S(2)}, u32[]{:S(2)}) %all-to-all-start) | async-done | bytes 262176 | tf_op jit(solution)/shard_map/all_to_all | solution.py:66
  31.4 0.2 convolution_convert_fusion.1
  31.6 0.0 copy-done.3
  31.6 0.0 copy-start.4
  31.7 1.3 %fusion.6 = bf16[512,2048]{0,1:T(8,128)(2,1)S(1)} fusion(bf16[32,512]{1,0:T(8,128)(2,1)S(1)} %copy-done.3, bf16[4,8,16,128]{3,2,1,0:T(8,128)(2,1)S(1)} %bitcast.94), kind=kOutput, calls=%fused_computation.10 | convolution fusion | flops 72351744 | bytes 2260992 | tf_op jit(solution)/shard_map/dot_general | solution.py:46
  33.0 0.0 copy-done
  33.0 0.0 copy-done.4
  33.0 2.3 %fusion.15 = bf16[4,8,16,128]{3,1,2,0:T(8,128)(2,1)S(1)} fusion(bf16[512,32]{0,1:T(8,128)(2,1)S(1)} %copy-done.4, bf16[512,2048]{0,1:T(8,128)(2,1)S(1)} %fusion.6, bf16[512,512]{1,0:T(8,128)(2,1)S(1)} %copy-done, bf16[4,8,16,128]{3,2,1,0:T(8,128)(2,1)S(1)} %bitcast.95), kind=kOutput, calls=%fused_computation.20 | convolution fusion | flops 1146290176 | bytes 2916352 | tf_op jit(solution)/shard_map/dot_general | solution.py:51
  35.3 0.3 fusion.14
  35.6 0.8 %copy.20 = bf16[4,8,32,128]{3,1,2,0:T(8,128)(2,1)} copy(bf16[4,8,32,128]{3,2,1,0:T(8,128)(2,1)S(1)} %bitcast.90) | data formatting | bytes 524288
  (4 shorter events, 0.1 us)
Async XLA Ops:
  0.6 32.3 %copy-start = (bf16[512,512]{1,0:T(8,128)(2,1)S(1)}, bf16[512,512]{1,0:T(8,128)(2,1)}, u32[]{:S(2)}) copy-start(bf16[512,512]{1,0:T(8,128)(2,1)} %param.10) | copy-start | bytes 1572868
  1.4 4.6 %collective-permute-start = (f32[1,256]{1,0:T(1,128)S(1)}, f32[1,256]{1,0:T(1,128)S(1)}, u32[]{:S(2)}, u32[]{:S(2)}) collective-permute-start(f32[1,256]{1,0:T(1,128)S(1)} %slice.63), channel_id=1, source_target_pairs={{0,4},{4,8},{8,12},{12,16},{16,20},{20,24},{24,28},{28,0},{1,5},{5... | collective-permute-start | bytes 3080 | tf_op jit(solution)/shard_map/ppermute | solution.py:15
  2.7 4.4 %collective-permute-start.1 = (f32[8,2,256]{2,1,0:T(2,128)S(1)}, f32[8,2,256]{2,1,0:T(2,128)S(1)}, u32[]{:S(2)}, u32[]{:S(2)}) collective-permute-start(f32[8,2,256]{2,1,0:T(2,128)S(1)} %get-tuple-element.10), channel_id=1, source_target_pairs={{0,4},{4,8},{8,12},{12,16},{16,20},{20,24},{24,28},{28,0},{1,5},{5... | collective-permute-start | bytes 49160 | tf_op jit(solution)/shard_map/ppermute | solution.py:25
  5.4 1.8 %collective-permute-start.2 = (f32[8,2,256]{2,1,0:T(2,128)S(1)}, f32[8,2,256]{2,1,0:T(2,128)S(1)}, u32[]{:S(2)}, u32[]{:S(2)}) collective-permute-start(f32[8,2,256]{2,1,0:T(2,128)S(1)} %get-tuple-element.9), channel_id=1, source_target_pairs={{4,0},{8,4},{12,8},{16,12},{20,16},{24,20},{28,24},{0,28},{5,1},{9... | collective-permute-start | bytes 49160 | tf_op jit(solution)/shard_map/ppermute | solution.py:26
  10.4 4.1 %collective-permute-start.3 = (f32[8,2,256]{2,1,0:T(2,128)S(1)}, f32[8,2,256]{2,1,0:T(2,128)S(1)}, u32[]{:S(2)}, u32[]{:S(2)}) collective-permute-start(f32[8,2,256]{2,1,0:T(2,128)S(1)} %get-tuple-element.8), channel_id=1, source_target_pairs={{0,4},{4,8},{8,12},{12,16},{16,20},{20,24},{24,28},{28,0},{1,5},{5... | collective-permute-start | bytes 49160 | tf_op jit(solution)/shard_map/ppermute | solution.py:25
  11.9 2.7 %collective-permute-start.4 = (f32[8,2,256]{2,1,0:T(2,128)S(1)}, f32[8,2,256]{2,1,0:T(2,128)S(1)}, u32[]{:S(2)}, u32[]{:S(2)}) collective-permute-start(f32[8,2,256]{2,1,0:T(2,128)S(1)} %get-tuple-element.7), channel_id=1, source_target_pairs={{4,0},{8,4},{12,8},{16,12},{20,16},{24,20},{28,24},{0,28},{5,1},{9... | collective-permute-start | bytes 49160 | tf_op jit(solution)/shard_map/ppermute | solution.py:26
  13.2 8.7 %copy-start.1 = (s32[1,1,16]{2,1,0:T(1,128)S(1)}, s32[1,1,16]{2,1,0:T(1,128)}, u32[]{:S(2)}) copy-start(s32[1,1,16]{2,1,0:T(1,128)} %param.12) | copy-start | bytes 196
  13.2 8.7 %copy-start.2 = (s32[1,1,16]{2,1,0:T(1,128)S(1)}, s32[1,1,16]{2,1,0:T(1,128)}, u32[]{:S(2)}) copy-start(s32[1,1,16]{2,1,0:T(1,128)} %param.13) | copy-start | bytes 196
  15.1 16.6 %copy-start.3 = (bf16[32,512]{1,0:T(8,128)(2,1)S(1)}, bf16[32,512]{1,0:T(8,128)(2,1)}, u32[]{:S(2)}) copy-start(bf16[32,512]{1,0:T(8,128)(2,1)} %param.9) | copy-start | bytes 98308
  16.2 15.1 %all-to-all-start = ((bf16[8,4,4096]{2,0,1:T(8,128)(2,1)}), bf16[8,4,4096]{2,0,1:T(8,128)(2,1)S(1)}, u32[]{:S(2)}, u32[]{:S(2)}) async-start(bf16[8,4,4096]{2,0,1:T(8,128)(2,1)} %copy.9), calls=%async_computation | async-start | bytes 524288 | tf_op jit(solution)/shard_map/all_to_all | solution.py:66
  22.5 4.5 %collective-permute-start.5 = (f32[1]{0:T(128)}, f32[1]{0:T(128)}, u32[]{:S(2)}, u32[]{:S(2)}) collective-permute-start(f32[1]{0:T(128)} %bitcast.10), channel_id=1, source_target_pairs={{0,4},{4,8},{8,12},{12,16},{16,20},{20,24},{24,28},{28,0},{1,5},{5... | collective-permute-start | bytes 20 | tf_op jit(solution)/shard_map/ppermute | solution.py:15
  22.7 5.5 %collective-permute-start.6 = (f32[1]{0:T(128)}, f32[1]{0:T(128)}, u32[]{:S(2)}, u32[]{:S(2)}) collective-permute-start(f32[1]{0:T(128)} %bitcast.11), channel_id=1, source_target_pairs={{0,8},{4,12},{8,16},{12,20},{16,24},{20,28},{24,0},{28,4},{1,9},{5... | collective-permute-start | bytes 20 | tf_op jit(solution)/shard_map/ppermute | solution.py:15
  25.3 3.6 %collective-permute-start.7 = (f32[1]{0:T(128)}, f32[1]{0:T(128)}, u32[]{:S(2)}, u32[]{:S(2)}) collective-permute-start(f32[1]{0:T(128)} %bitcast.12), channel_id=1, source_target_pairs={{0,28},{4,0},{8,4},{12,8},{16,12},{20,16},{24,20},{28,24},{1,29},{... | collective-permute-start | bytes 20 | tf_op jit(solution)/shard_map/ppermute | solution.py:15
  25.3 4.3 %collective-permute-start.8 = (f32[1]{0:T(128)}, f32[1]{0:T(128)}, u32[]{:S(2)}, u32[]{:S(2)}) collective-permute-start(f32[1]{0:T(128)} %bitcast.13), channel_id=1, source_target_pairs={{0,24},{4,28},{8,0},{12,4},{16,8},{20,12},{24,16},{28,20},{1,25},{... | collective-permute-start | bytes 20 | tf_op jit(solution)/shard_map/ppermute | solution.py:15
  31.6 1.3 %copy-start.4 = (bf16[512,32]{0,1:T(8,128)(2,1)S(1)}, bf16[512,32]{0,1:T(8,128)(2,1)}, u32[]{:S(2)}) copy-start(bf16[512,32]{0,1:T(8,128)(2,1)} %param.11) | copy-start | bytes 98308
where the time goes:
time: 38 us; the launch traced here: 37.6 us
  starting transfers between devices  16.2 us (43%)
  other arithmetic  5.37 us (14%)
  between operations  5.04 us (13%)
  matrix products  4.14 us (11%)
  local copies, waits for them, and re-layouts  3.59 us (9%)
  waiting for transfers between devices  3.22 us (8%)
    all_to_all x1, starting transfers between devices, shards(): lax.all_to_all(advected, 'spec', split_axis=1, concat_axis=0, tiled=True)  5.63 us
    ppermute x5, starting transfers between devices, from_behind(): return lax.ppermute(value, axis, pairs)  4.84 us
    ppermute x2, starting transfers between devices, extended(): before = lax.ppermute(last, axis, up)  4.14 us
    mul x2, other arithmetic, advect(): fluxes = courants * (centre + 0.5 * (1.0 - courants) * slopes)  2.54 us
    dot_general x1, matrix products, surrogate(): change = jnp.dot(last_weight.T, second, preferred_element_type=jnp.float32)  2.27 us
    ppermute x2, waiting for transfers between devices, extended(): before = lax.ppermute(last, axis, up)  1.63 us
    ppermute x2, starting transfers between devices, extended(): after = lax.ppermute(initial, axis, down)  1.6 us
    dot_general x1, matrix products, surrogate(): jnp.dot(first_weight.T, inputs, preferred_element_type=jnp.float32)  1.31 us
  transfers between devices with their start and end apart: 10, of which 6 were waited for; matrix products, arithmetic and copies ran while one was open for 7% of the time, Pallas kernels for 0%

commit v1 on v0

v1 whole, which is shorter than its diff:
```python
import functools

import jax
import jax.numpy as jnp
from jax import lax
from jax.experimental import pallas as pl
from jax.experimental.pallas import tpu as pltpu
from jax.sharding import PartitionSpec as P

BLK = 128
RECV = 8
BEHIND = 4
AHEAD = 2
VMEM_BYTES = 16 * 1024 * 1024


def silu(v):
    half = 0.5 * v
    return half + half * jnp.tanh(half)


def sweep_rows(rows, rates):
    diffs = [b - a for a, b in zip(rows[:-1], rows[1:])]
    fluxes = []
    for at in range(1, len(rows) - 1):
        left, right = diffs[at - 1], diffs[at]
        slope = jnp.maximum(jnp.minimum(left, right), 0.0) + jnp.minimum(
            jnp.maximum(left, right), 0.0
        )
        rate, damp = rates[at]
        fluxes.append(rate * (rows[at] + damp * slope))
    return [rows[at] - fluxes[at - 1] + fluxes[at - 2] for at in range(2, len(rows) - 1)]


def two_sweeps(rows, rates):
    once = sweep_rows(rows, rates)
    return sweep_rows(once, rates[2:-1])


def with_damp(rate, shape):
    rate = jnp.broadcast_to(rate, shape)
    return rate, 0.5 - 0.5 * rate


def inner_kernel(dests, length, q_ref, courant_ref, up_ref, down_ref, context_ref, *refs):
    *out_refs, held_ref, rates_ref, arrived = refs
    species = q_ref.shape[0] // length
    cols = q_ref.shape[1]
    share = length // dests
    reach = BEHIND + AHEAD
    me = lax.axis_index("spec")
    lanes = held_ref.shape[2]
    copies = [
        [
            pltpu.make_async_copy(
                source.at[:, h * lanes : (h + 1) * lanes], target.at[h], arrived.at[h, i]
            )
            for i, (source, target) in enumerate([(courant_ref, rates_ref), (q_ref, held_ref)])
        ]
        for h in range(cols // lanes)
    ]
    for pair in copies:
        for copy in pair:
            copy.start()
    for h, pair in enumerate(copies):
        here = slice(h * lanes, (h + 1) * lanes)

        def row(at):
            return held_ref[h, pl.ds(at, species, stride=length), :]

        def rate_row(at):
            return with_damp(rates_ref[h, pl.ds(at, 1), :], (species, lanes))

        for copy in pair:
            copy.wait()
        up_ref[BEHIND * species :, here] = rates_ref[h, length - 8 :, :]
        down_ref[AHEAD * species :, here] = rates_ref[h, 0:8, :]
        for j in range(BEHIND):
            up_ref[j * species : (j + 1) * species, here] = row(length - BEHIND + j)
        for j in range(AHEAD):
            down_ref[j * species : (j + 1) * species, here] = row(j)
        for j in range(reach):
            context_ref[j * species : (j + 1) * species, here] = row(j)
            context_ref[(reach + j) * species : (reach + j + 1) * species, here] = row(
                length - reach + j
            )
        for k in range(dests):
            first = lax.rem(me + k, dests) * share
            places = [
                jnp.clip(first + at, 0, length - 1) for at in range(-BEHIND, share + AHEAD)
            ]
            done = two_sweeps([row(at) for at in places], [rate_row(at) for at in places])
            for at, value in enumerate(done):
                start = at * cols + h * lanes
                out_refs[k][:, start : start + lanes] = value.astype(jnp.bfloat16)


def edge_kernel(dests, length, up_ref, down_ref, context_ref, courant_ref, *out_refs):
    species = out_refs[0].shape[0]
    cols = courant_ref.shape[1]
    me = lax.axis_index("spec")
    reach = BEHIND + AHEAD

    def part(ref, at):
        return ref[at * species : (at + 1) * species, :]

    def rate_rows(ref, start, count):
        return [with_damp(ref[at : at + 1, :], (species, cols)) for at in range(start, start + count)]

    behind = [part(up_ref, j) for j in range(BEHIND)]
    ahead = [part(down_ref, j) for j in range(AHEAD)]
    lowest = [part(context_ref, j) for j in range(reach)]
    highest = [part(context_ref, reach + j) for j in range(reach)]
    top = two_sweeps(
        behind + lowest,
        rate_rows(up_ref, BEHIND * species + 8 - BEHIND, BEHIND) + rate_rows(courant_ref, 0, reach),
    )
    bottom = two_sweeps(
        highest + ahead,
        rate_rows(courant_ref, length - reach, reach)
        + rate_rows(down_ref, AHEAD * species, AHEAD),
    )
    fill = [jnp.zeros_like(bottom[0])] * (BEHIND - AHEAD)
    for k in range(dests):
        for j, (one, other) in enumerate(zip(top, fill + bottom)):
            out_refs[k][:, j * cols : (j + 1) * cols] = jnp.where(me == k, one, other).astype(
                jnp.bfloat16
            )


def chemistry_kernel(groups, slots, list_ref, w1_ref, w2_ref, w3_ref, *refs):
    parts, edges = refs[:groups], refs[groups : 2 * groups]
    out_ref, picked_ref, fresh_ref = refs[2 * groups :]
    species, cells = out_ref.shape[1:]
    blocks = cells // BLK
    wide = edges[0].shape[1]
    narrow = wide // BEHIND * AHEAD
    me = lax.axis_index("spec")
    for k in range(groups):
        out_ref[lax.rem(me - k + groups, groups)] = parts[k][...]

    @pl.when(me == 0)
    def _():
        for k in range(groups):
            out_ref[k, :, 0:wide] = edges[k][...]

    @pl.when(me == groups - 1)
    def _():
        for k in range(groups):
            out_ref[groups - 1 - k, :, cells - narrow :] = edges[k][:, wide - narrow :]

    def place(j):
        return pl.ds(pl.multiple_of(jnp.minimum(list_ref[j], blocks - 1) * BLK, BLK), BLK)

    for j in range(slots):
        for g in range(groups):
            picked_ref[g * species : (g + 1) * species, j * BLK : (j + 1) * BLK] = out_ref[
                g, :, place(j)
            ].astype(jnp.float32)
    width = 4 * BLK
    for start in range(0, slots * BLK, width):
        x = picked_ref[:, start : start + width]
        hidden = jnp.dot(w1_ref[...], x.astype(jnp.bfloat16), preferred_element_type=jnp.float32)
        hidden = silu(hidden).astype(jnp.bfloat16)
        hidden = jnp.dot(w2_ref[...], hidden, preferred_element_type=jnp.float32)
        hidden = silu(hidden).astype(jnp.bfloat16)
        fresh_ref[:, start : start + width] = x + jnp.dot(
            w3_ref[...], hidden, preferred_element_type=jnp.float32
        )
    for j in range(slots):

        @pl.when(list_ref[j] < blocks)
        def _():
            for g in range(groups):
                out_ref[g, :, place(j)] = fresh_ref[
                    g * species : (g + 1) * species, j * BLK : (j + 1) * BLK
                ].astype(jnp.bfloat16)


def vmem():
    return pl.BlockSpec(memory_space=pltpu.VMEM)


def shards(
    concentrations, courant, first_weight, middle_weight, last_weight, active_blocks, dest_tile
):
    species, length, cols = concentrations.shape
    dests = lax.axis_size("spec")
    tiles = lax.axis_size("tile")
    cells = length // dests * cols
    slots = active_blocks.shape[-1]
    params = pltpu.CompilerParams(vmem_limit_bytes=VMEM_BYTES)
    reach = BEHIND + AHEAD
    f32, bf16 = jnp.float32, jnp.bfloat16

    up, down, context, *blocks = pl.pallas_call(
        functools.partial(inner_kernel, dests, length),
        out_shape=[
            jax.ShapeDtypeStruct((BEHIND * species + 8, cols), f32),
            jax.ShapeDtypeStruct((AHEAD * species + 8, cols), f32),
            jax.ShapeDtypeStruct((2 * reach * species, cols), f32),
        ]
        + [jax.ShapeDtypeStruct((species, cells), bf16)] * dests,
        in_specs=[pl.BlockSpec(memory_space=pltpu.HBM)] * 2,
        out_specs=[vmem()] * (3 + dests),
        scratch_shapes=[
            pltpu.VMEM((cols // BLK, species * length, BLK), f32),
            pltpu.VMEM((cols // BLK, length, BLK), f32),
            pltpu.SemaphoreType.DMA((cols // BLK, 2)),
        ],
        compiler_params=params,
        name="inner_rows",
    )(concentrations.reshape(species * length, cols), courant)

    forward = [(t, (t + 1) % tiles) for t in range(tiles)]
    backward = [(b, a) for a, b in forward]
    received = [blocks[0]] + [
        lax.ppermute(blocks[k], "spec", [(s, (s + k) % dests) for s in range(dests)])
        for k in range(1, dests)
    ]
    behind = lax.ppermute(up, "tile", forward)
    ahead = lax.ppermute(down, "tile", backward)
    edges = pl.pallas_call(
        functools.partial(edge_kernel, dests, length),
        out_shape=[jax.ShapeDtypeStruct((species, BEHIND * cols), bf16)] * dests,
        in_specs=[vmem()] * 4,
        out_specs=[vmem()] * dests,
        compiler_params=params,
        name="edge_rows",
    )(behind, ahead, context, courant)
    edges = [edges[0]] + [
        lax.ppermute(edges[k], "spec", [(k, 0), (dests - 1 - k, dests - 1)])
        for k in range(1, dests)
    ]

    listing = active_blocks.reshape(-1)
    hits = (dest_tile.reshape(-1)[None, :] == jnp.arange(tiles, dtype=jnp.int32)[:, None]) & (
        listing < cells // BLK
    )[None, :]
    share = lax.psum_scatter(
        jnp.sum(hits.astype(f32), axis=1), "tile", scatter_dimension=0, tiled=True
    )
    load_share = (share / RECV).reshape(1, 1)

    out = pl.pallas_call(
        functools.partial(chemistry_kernel, dests, slots),
        out_shape=jax.ShapeDtypeStruct((dests, species, cells), bf16),
        in_specs=[pl.BlockSpec(memory_space=pltpu.SMEM)] + [vmem()] * (3 + 2 * dests),
        out_specs=vmem(),
        scratch_shapes=[
            pltpu.VMEM((dests * species, slots * BLK), f32),
            pltpu.VMEM((dests * species, slots * BLK), f32),
        ],
        compiler_params=params,
        name="chemistry",
    )(listing, first_weight.T, middle_weight.T, last_weight.T, *received, *edges)
    return out.reshape(dests * species, cells), load_share


def solution(mesh):
    in_specs = (
        P("spec", "tile", None),
        P("tile", None),
        P(),
        P(),
        P(),
        P("tile", "spec", None),
        P("tile", "spec", None),
    )
    out_specs = (P(None, ("tile", "spec")), P("tile", "spec"))
    return jax.shard_map(shards, mesh=mesh, in_specs=in_specs, out_specs=out_specs, check_vma=False)
```

time: 38 us -> 44.6 us (1.17)
  blocking collectives: 0 us -> 12.9 us
  Pallas kernels: 0 us -> 5.58 us
  other arithmetic: 5.37 us -> 0.12 us
  matrix products: 4.14 us -> 0 us
  between operations: 5.04 us -> 2.57 us
  local copies, waits for them, and re-layouts: 3.59 us -> 5.08 us
  starting transfers between devices: 16.2 us -> 14.8 us
    unnamed x0 -> x1, blocking collectives: none -> 12.9 us
    all_to_all x1 -> x0, starting transfers between devices: 5.63 us -> none  [shards(): lax.all_to_all(advected, 'spec', split_axis=1, concat_axis=0, tiled=True)]
    pallas_call x0 -> x3, Pallas kernels: none -> 5.58 us  [the longest x1 4.47 us: shards(): pl.pallas_call(functools.partial(chemistry_kernel, dests, slots), out_sha...]
    ppermute x9 -> x8, starting transfers between devices: 10.6 us -> 14.8 us  [the longest x3 6.21 us: shards(): lax.ppermute(blocks[k], 'spec', [(s, (s + k) % dests) for s in range(dest...]
    unnamed x13 -> x20, local copies, waits for them, and re-layouts: 0.9 us -> 5.08 us
    dot_general x4 -> x0, matrix products: 4.14 us -> none  [the longest x1 2.27 us: surrogate(): change = jnp.dot(last_weight.T, second, preferred_element_type=jnp.float32)]
    mul x2 -> x0, other arithmetic: 2.54 us -> none  [advect(): fluxes = courants * (centre + 0.5 * (1.0 - courants) * slopes)]
    slice x3 -> x0, local copies, waits for them, and re-layouts: 1.66 us -> none  [the longest x2 0.9 us: extended(): initial = lax.slice_in_dim(x, 0, width, axis=dim)]
  transfers between devices with their start and end apart: 10 -> 8, of which waited for: 6 -> 1; matrix products, arithmetic and copies ran while one was open for 7% -> 5% of each run, Pallas kernels for 0% -> 0%
where the time goes in v1:
time: 44.6 us; the launch traced here: 44.1 us
  starting transfers between devices  14.8 us (33%)
  blocking collectives  12.9 us (29%)
  Pallas kernels  5.58 us (13%)
  local copies, waits for them, and re-layouts  5.08 us (11%)
  waiting for transfers between devices  3.03 us (7%)
  between operations  2.57 us (6%)
    unnamed x1, blocking collectives  12.9 us
    ppermute x3, starting transfers between devices, shards(): lax.ppermute(blocks[k], 'spec', [(s, (s + k) % dests) for s in range(dest...  6.21 us
    ppermute x3, starting transfers between devices, shards(): lax.ppermute(edges[k], 'spec', [(k, 0), (dests - 1 - k, dests - 1)])  5.11 us
    unnamed x20, local copies, waits for them, and re-layouts  5.08 us
    pallas_call x1, Pallas kernels, shards(): pl.pallas_call(functools.partial(chemistry_kernel, dests, slots), out_sha...  4.47 us
    ppermute x3, waiting for transfers between devices, shards(): lax.ppermute(edges[k], 'spec', [(k, 0), (dests - 1 - k, dests - 1)])  3.02 us
    ppermute x1, starting transfers between devices, shards(): ahead = lax.ppermute(down, 'tile', backward)  2.95 us
    pallas_call x1, Pallas kernels, shards(): pl.pallas_call(functools.partial(inner_kernel, dests, length), out_shape=...  1.02 us
  transfers between devices with their start and end apart: 8, of which 1 were waited for; matrix products, arithmetic and copies ran while one was open for 5% of the time, Pallas kernels for 0%

profile of v1, /device:TPU:0, one launch (start us, length us, event | category | flops | bytes accessed | tf_op | source)
XLA Modules:
  0.0 44.1 jit_solution(3697168449381568084)
XLA Ops:
  0.6 0.0 copy-start
  0.6 1.0 %copy-done = f32[8,64,256]{2,1,0:T(8,128)S(1)} copy-done((f32[8,64,256]{2,1,0:T(8,128)S(1)}, f32[8,64,256]{2,1,0:T(8,128)}, u32[]{:S(2)}) %copy-start) | copy-done | bytes 524312
  1.7 0.0 copy-start.1
  1.7 0.8 %copy-done.1 = f32[64,256]{1,0:T(8,128)S(1)} copy-done((f32[64,256]{1,0:T(8,128)S(1)}, f32[64,256]{1,0:T(8,128)}, u32[]{:S(2)}) %copy-start.1) | copy-done | bytes 65560
  2.5 0.0 copy-start.4
  2.5 1.0 %inner_rows.1 = (f32[40,256]{1,0:T(8,128)S(1)}, f32[24,256]{1,0:T(8,128)S(1)}, f32[96,256]{1,0:T(8,128)S(1)}, bf16[8,4096]{1,0:T(8,128)(2,1)S(1)}, bf16[8,4096]{...) custom-call(f32[512,256]{1,0:T(8,128)S(1)} %bitcast.12, f32[64,256]{1,0:T(8,128)S(1)} %copy-done.1), custom_call_target="tpu_custom_call" | custom-call | tf_op jit(solution)/shard_map/inner_rows/pallas_call | solution.py:196
  3.5 0.5 %collective-permute-start.3 = (f32[40,256]{1,0:T(8,128)S(1)}, f32[40,256]{1,0:T(8,128)S(1)}, u32[]{:S(2)}, u32[]{:S(2)}) collective-permute-start(f32[40,256]{1,0:T(8,128)S(1)} %get-tuple-element.17), channel_id=1, source_target_pairs={{0,4},{4,8},{8,12},{12,16},{16,20},{20,24},{24,28},{28,0},{1,5},{5... | collective-permute-start | bytes 122888 | tf_op jit(solution)/shard_map/ppermute | solution.py:221
  4.1 2.9 %collective-permute-start.4 = (f32[24,256]{1,0:T(8,128)S(1)}, f32[24,256]{1,0:T(8,128)S(1)}, u32[]{:S(2)}, u32[]{:S(2)}) collective-permute-start(f32[24,256]{1,0:T(8,128)S(1)} %get-tuple-element.18), channel_id=1, source_target_pairs={{4,0},{8,4},{12,8},{16,12},{20,16},{24,20},{28,24},{0,28},{5,1},{9... | collective-permute-start | bytes 73736 | tf_op jit(solution)/shard_map/ppermute | solution.py:222
  7.0 2.3 %collective-permute-start = (bf16[8,4096]{1,0:T(8,128)(2,1)S(1)}, bf16[8,4096]{1,0:T(8,128)(2,1)S(1)}, u32[]{:S(2)}, u32[]{:S(2)}) collective-permute-start(bf16[8,4096]{1,0:T(8,128)(2,1)S(1)} %get-tuple-element.14), channel_id=1, source_target_pairs={{0,1},{1,2},{2,3},{3,0},{4,5},{5,6},{6,7},{7,4},{8,9},{9,10},{10,1... | collective-permute-start | bytes 196616 | tf_op jit(solution)/shard_map/ppermute | solution.py:218
  9.3 2.6 %collective-permute-start.1 = (bf16[8,4096]{1,0:T(8,128)(2,1)S(1)}, bf16[8,4096]{1,0:T(8,128)(2,1)S(1)}, u32[]{:S(2)}, u32[]{:S(2)}) collective-permute-start(bf16[8,4096]{1,0:T(8,128)(2,1)S(1)} %get-tuple-element.15), channel_id=1, source_target_pairs={{0,2},{1,3},{2,0},{3,1},{4,6},{5,7},{6,4},{7,5},{8,10},{9,11},{10,... | collective-permute-start | bytes 196616 | tf_op jit(solution)/shard_map/ppermute | solution.py:218
  11.9 1.3 %collective-permute-start.2 = (bf16[8,4096]{1,0:T(8,128)(2,1)S(1)}, bf16[8,4096]{1,0:T(8,128)(2,1)S(1)}, u32[]{:S(2)}, u32[]{:S(2)}) collective-permute-start(bf16[8,4096]{1,0:T(8,128)(2,1)S(1)} %get-tuple-element.16), channel_id=1, source_target_pairs={{0,3},{1,0},{2,1},{3,2},{4,7},{5,4},{6,5},{7,6},{8,11},{9,8},{10,9... | collective-permute-start | bytes 196616 | tf_op jit(solution)/shard_map/ppermute | solution.py:218
  13.2 0.0 collective-permute-done.4.down_ref
  13.2 0.0 collective-permute-done.3.up_ref
  13.2 0.1 edge_rows.1
  13.3 0.0 copy-start.3
  13.3 1.3 %collective-permute-start.5 = (bf16[8,1024]{1,0:T(8,128)(2,1)S(1)}, bf16[8,1024]{1,0:T(8,128)(2,1)S(1)}, u32[]{:S(2)}, u32[]{:S(2)}) collective-permute-start(bf16[8,1024]{1,0:T(8,128)(2,1)S(1)} %get-tuple-element.21), channel_id=1, source_target_pairs={{1,0},{2,3},{5,4},{6,7},{9,8},{10,11},{13,12},{14,15},{17,16},{18,... | collective-permute-start | bytes 49160 | tf_op jit(solution)/shard_map/ppermute | solution.py:232
  14.6 0.0 copy-done.3
  14.6 1.3 %collective-permute-start.6 = (bf16[8,1024]{1,0:T(8,128)(2,1)S(1)}, bf16[8,1024]{1,0:T(8,128)(2,1)S(1)}, u32[]{:S(2)}, u32[]{:S(2)}) collective-permute-start(bf16[8,1024]{1,0:T(8,128)(2,1)S(1)} %get-tuple-element.22), channel_id=1, source_target_pairs={{2,0},{1,3},{6,4},{5,7},{10,8},{9,11},{14,12},{13,15},{18,16},{17,... | collective-permute-start | bytes 49160 | tf_op jit(solution)/shard_map/ppermute | solution.py:232
  15.9 3.0 %collective-permute-done.5.refs_5_ = bf16[8,1024]{1,0:T(8,128)(2,1)S(1)} collective-permute-done((bf16[8,1024]{1,0:T(8,128)(2,1)S(1)}, bf16[8,1024]{1,0:T(8,128)(2,1)S(1)}, u32[]{:S(2)}, u32[]{:S(2)}) %collective-permute-start.5) | collective-permute-done | bytes 16416 | tf_op jit(solution)/shard_map/ppermute | solution.py:232
  18.9 0.0 copy-start.6
  19.0 2.5 %collective-permute-start.7 = (bf16[8,1024]{1,0:T(8,128)(2,1)S(1)}, bf16[8,1024]{1,0:T(8,128)(2,1)S(1)}, u32[]{:S(2)}, u32[]{:S(2)}) collective-permute-start(bf16[8,1024]{1,0:T(8,128)(2,1)S(1)} %get-tuple-element.23), channel_id=1, source_target_pairs={{3,0},{0,3},{7,4},{4,7},{11,8},{8,11},{15,12},{12,15},{19,16},{16,... | collective-permute-start | bytes 49160 | tf_op jit(solution)/shard_map/ppermute | solution.py:232
  21.5 0.0 copy-done.6
  21.5 0.1 convert_reduce_fusion
  21.6 12.9 %all-reduce = f32[8]{0:T(128)S(1)} all-reduce(f32[8]{0:T(128)S(1)} %convert_reduce_fusion), channel_id=2, replica_groups=mesh['tile'=8,'spec'=4] {'tile'}, use_global_device_ids=true, to_apply=%region_1.0.clone | all-reduce | flops 8 | bytes 64
  34.6 0.0 copy-done.4
  34.6 0.0 copy-start.5
  34.6 0.2 copy.14
  34.8 0.5 %copy-done.5 = bf16[32,512]{1,0:T(8,128)(2,1)S(1)} copy-done((bf16[32,512]{1,0:T(8,128)(2,1)S(1)}, bf16[32,512]{1,0:T(8,128)(2,1)}, u32[]{:S(2)}) %copy-start.5) | copy-done | bytes 32792
  35.3 0.0 copy-start.7
  35.3 0.1 copy.13
  35.4 0.0 copy-start.2
  35.5 0.5 %copy-done.7 = u32[32]{0:T(128)S(1)} copy-done((u32[32]{0:T(128)S(1)}, u32[32]{0:T(128)}, u32[]{:S(2)}) %copy-start.7) | copy-done | bytes 152
  36.0 0.6 %dynamic-slice = u32[1]{0:T(128)} dynamic-slice(u32[32]{0:T(128)S(1)} %copy-done.7, u32[]{:T(128)S(6)} %add.3), dynamic_slice_sizes={1} | dynamic-slice | bytes 12
  36.6 1.2 %dynamic-slice.1 = f32[1]{0:T(128)} dynamic-slice(f32[8]{0:T(128)S(1)} %all-reduce, u32[]{:T(128)} %bitcast.7), dynamic_slice_sizes={1} | dynamic-slice | bytes 12
  38.4 0.0 collective-permute-done.6.refs_6_
  38.5 0.0 collective-permute-done.7.refs_7_
  38.5 0.0 collective-permute-done.refs_1_
  38.5 0.0 collective-permute-done.1.refs_2_
  38.5 0.0 collective-permute-done.2.refs_3_
  38.5 0.0 copy-done.2
  38.5 4.5 %chemistry.1 = bf16[4,8,4096]{2,1,0:T(8,128)(2,1)} custom-call(s32[16]{0:T(128)S(1)} %bitcast.14, bf16[512,32]{1,0:T(8,128)(2,1)S(1)} %bitcast.11, bf16[512,512]{1,0:T(8,128)(2,1)S(1)} %bitcast.10, bf16[32,512]{1,0:T(8,128)(2,1)S(1)} %bitcast.13, bf16[8,4096]{1,0:T(8,128)(2,1)S(1)} %get-tuple-element.13.refs_0_, ...), custom_call_target="tpu_custom_call" | custom-call | tf_op jit(solution)/shard_map/chemistry/pallas_call | solution.py:245
  (1 shorter events, 0.0 us)
Async XLA Ops:
  0.6 1.0 %copy-start = (f32[8,64,256]{2,1,0:T(8,128)S(1)}, f32[8,64,256]{2,1,0:T(8,128)}, u32[]{:S(2)}) copy-start(f32[8,64,256]{2,1,0:T(8,128)} %param.7) | copy-start | bytes 1572868
  1.7 0.8 %copy-start.1 = (f32[64,256]{1,0:T(8,128)S(1)}, f32[64,256]{1,0:T(8,128)}, u32[]{:S(2)}) copy-start(f32[64,256]{1,0:T(8,128)} %courant_ref.3) | copy-start | bytes 196612
  2.5 32.0 %copy-start.4 = (bf16[512,512]{1,0:T(8,128)(2,1)S(1)}, bf16[512,512]{1,0:T(8,128)(2,1)}, u32[]{:S(2)}) copy-start(bf16[512,512]{1,0:T(8,128)(2,1)} %param.10) | copy-start | bytes 1572868
  3.5 9.7 %collective-permute-start.3 = (f32[40,256]{1,0:T(8,128)S(1)}, f32[40,256]{1,0:T(8,128)S(1)}, u32[]{:S(2)}, u32[]{:S(2)}) collective-permute-start(f32[40,256]{1,0:T(8,128)S(1)} %get-tuple-element.17), channel_id=1, source_target_pairs={{0,4},{4,8},{8,12},{12,16},{16,20},{20,24},{24,28},{28,0},{1,5},{5... | collective-permute-start | bytes 122888 | tf_op jit(solution)/shard_map/ppermute | solution.py:221
  4.1 9.2 %collective-permute-start.4 = (f32[24,256]{1,0:T(8,128)S(1)}, f32[24,256]{1,0:T(8,128)S(1)}, u32[]{:S(2)}, u32[]{:S(2)}) collective-permute-start(f32[24,256]{1,0:T(8,128)S(1)} %get-tuple-element.18), channel_id=1, source_target_pairs={{4,0},{8,4},{12,8},{16,12},{20,16},{24,20},{28,24},{0,28},{5,1},{9... | collective-permute-start | bytes 73736 | tf_op jit(solution)/shard_map/ppermute | solution.py:222
  7.0 31.5 %collective-permute-start = (bf16[8,4096]{1,0:T(8,128)(2,1)S(1)}, bf16[8,4096]{1,0:T(8,128)(2,1)S(1)}, u32[]{:S(2)}, u32[]{:S(2)}) collective-permute-start(bf16[8,4096]{1,0:T(8,128)(2,1)S(1)} %get-tuple-element.14), channel_id=1, source_target_pairs={{0,1},{1,2},{2,3},{3,0},{4,5},{5,6},{6,7},{7,4},{8,9},{9,10},{10,1... | collective-permute-start | bytes 196616 | tf_op jit(solution)/shard_map/ppermute | solution.py:218
  9.3 29.2 %collective-permute-start.1 = (bf16[8,4096]{1,0:T(8,128)(2,1)S(1)}, bf16[8,4096]{1,0:T(8,128)(2,1)S(1)}, u32[]{:S(2)}, u32[]{:S(2)}) collective-permute-start(bf16[8,4096]{1,0:T(8,128)(2,1)S(1)} %get-tuple-element.15), channel_id=1, source_target_pairs={{0,2},{1,3},{2,0},{3,1},{4,6},{5,7},{6,4},{7,5},{8,10},{9,11},{10,... | collective-permute-start | bytes 196616 | tf_op jit(solution)/shard_map/ppermute | solution.py:218
  11.9 26.6 %collective-permute-start.2 = (bf16[8,4096]{1,0:T(8,128)(2,1)S(1)}, bf16[8,4096]{1,0:T(8,128)(2,1)S(1)}, u32[]{:S(2)}, u32[]{:S(2)}) collective-permute-start(bf16[8,4096]{1,0:T(8,128)(2,1)S(1)} %get-tuple-element.16), channel_id=1, source_target_pairs={{0,3},{1,0},{2,1},{3,2},{4,7},{5,4},{6,5},{7,6},{8,11},{9,8},{10,9... | collective-permute-start | bytes 196616 | tf_op jit(solution)/shard_map/ppermute | solution.py:218
  13.3 1.3 %copy-start.3 = (s32[1,1,16]{2,1,0:T(1,128)S(1)}, s32[1,1,16]{2,1,0:T(1,128)}, u32[]{:S(2)}) copy-start(s32[1,1,16]{2,1,0:T(1,128)} %param.12) | copy-start | bytes 196
  13.3 5.6 %collective-permute-start.5 = (bf16[8,1024]{1,0:T(8,128)(2,1)S(1)}, bf16[8,1024]{1,0:T(8,128)(2,1)S(1)}, u32[]{:S(2)}, u32[]{:S(2)}) collective-permute-start(bf16[8,1024]{1,0:T(8,128)(2,1)S(1)} %get-tuple-element.21), channel_id=1, source_target_pairs={{1,0},{2,3},{5,4},{6,7},{9,8},{10,11},{13,12},{14,15},{17,16},{18,... | collective-permute-start | bytes 49160 | tf_op jit(solution)/shard_map/ppermute | solution.py:232
  14.6 23.8 %collective-permute-start.6 = (bf16[8,1024]{1,0:T(8,128)(2,1)S(1)}, bf16[8,1024]{1,0:T(8,128)(2,1)S(1)}, u32[]{:S(2)}, u32[]{:S(2)}) collective-permute-start(bf16[8,1024]{1,0:T(8,128)(2,1)S(1)} %get-tuple-element.22), channel_id=1, source_target_pairs={{2,0},{1,3},{6,4},{5,7},{10,8},{9,11},{14,12},{13,15},{18,16},{17,... | collective-permute-start | bytes 49160 | tf_op jit(solution)/shard_map/ppermute | solution.py:232
  18.9 2.5 %copy-start.6 = (s32[1,1,16]{2,1,0:T(1,128)S(1)}, s32[1,1,16]{2,1,0:T(1,128)}, u32[]{:S(2)}) copy-start(s32[1,1,16]{2,1,0:T(1,128)} %param.13) | copy-start | bytes 196
  19.0 19.5 %collective-permute-start.7 = (bf16[8,1024]{1,0:T(8,128)(2,1)S(1)}, bf16[8,1024]{1,0:T(8,128)(2,1)S(1)}, u32[]{:S(2)}, u32[]{:S(2)}) collective-permute-start(bf16[8,1024]{1,0:T(8,128)(2,1)S(1)} %get-tuple-element.23), channel_id=1, source_target_pairs={{3,0},{0,3},{7,4},{4,7},{11,8},{8,11},{15,12},{12,15},{19,16},{16,... | collective-permute-start | bytes 49160 | tf_op jit(solution)/shard_map/ppermute | solution.py:232
  34.6 0.8 %copy-start.5 = (bf16[32,512]{1,0:T(8,128)(2,1)S(1)}, bf16[32,512]{1,0:T(8,128)(2,1)}, u32[]{:S(2)}) copy-start(bf16[32,512]{1,0:T(8,128)(2,1)} %param.9) | copy-start | bytes 98308
  35.3 0.7 %copy-start.7 = (u32[32]{0:T(128)S(1)}, u32[32]{0:T(128)}, u32[]{:S(2)}) copy-start(u32[32]{0:T(128)} %constant.11) | copy-start | bytes 388
  35.4 3.0 %copy-start.2 = (bf16[512,32]{0,1:T(8,128)(2,1)S(1)}, bf16[512,32]{0,1:T(8,128)(2,1)}, u32[]{:S(2)}) copy-start(bf16[512,32]{0,1:T(8,128)(2,1)} %param.11) | copy-start | bytes 98308

commit v2 on v0

v2 whole, which is shorter than its diff:
```python
import functools

import jax
import jax.numpy as jnp
from jax import lax
from jax.experimental import pallas as pl
from jax.experimental.pallas import tpu as pltpu
from jax.sharding import PartitionSpec as P

BLK = 128
RECV = 8
LANES = 128
SUB = 8
BEHIND = 4
AHEAD = 2
VMEM_BYTES = 16 * 1024 * 1024


def silu_of_half(half):
    return half + half * jnp.tanh(half)


def sweep_rows(rows, rates):
    diffs = [b - a for a, b in zip(rows[:-1], rows[1:])]
    fluxes = []
    for at in range(1, len(rows) - 1):
        left, right = diffs[at - 1], diffs[at]
        slope = jnp.maximum(jnp.minimum(left, right), 0.0) + jnp.minimum(
            jnp.maximum(left, right), 0.0
        )
        rate, damp = rates[at]
        fluxes.append(rate * (rows[at] + damp * slope))
    return [rows[at] - fluxes[at - 1] + fluxes[at - 2] for at in range(2, len(rows) - 1)]


def two_sweeps(rows, rates):
    once = sweep_rows(rows, rates)
    return sweep_rows(once, rates[2:-1])


def with_damp(rate, shape):
    rate = jnp.broadcast_to(rate, shape)
    return rate, 0.5 - 0.5 * rate


def tiled(x, halves):
    lead, (rows, cols) = x.shape[:-2], x.shape[-2:]
    x = x.reshape(lead + (rows // SUB, SUB, halves, LANES))
    axes = tuple(range(len(lead)))
    x = x.transpose(axes + tuple(len(lead) + a for a in (0, 2, 1, 3)))
    return x.reshape(lead + (rows * halves, LANES))


def spot(at, half, halves):
    return (at // SUB * halves + half) * SUB + at % SUB


def pack_kernel(
    length, halves, blocks, q_in, rates_in, list_in, dest_in,
    even_ref, odd_ref, hits_ref, q_ref, rates_ref, list_ref, dest_ref, arrived,
):
    pairs = [(q_in, q_ref), (rates_in, rates_ref), (list_in, list_ref), (dest_in, dest_ref)]
    copies = [
        pltpu.make_async_copy(source, target, arrived.at[i])
        for i, (source, target) in enumerate(pairs)
    ]
    for copy in copies:
        copy.start()
    species = q_ref.shape[0] // (length * halves)
    part = BEHIND * species + SUB

    def row(at, half):
        return q_ref[pl.ds(spot(at, half, halves), species, stride=length * halves), :]

    copies[2].wait()
    copies[3].wait()
    lane = lax.broadcasted_iota(jnp.int32, (SUB, LANES), 1)
    hits = jnp.zeros((SUB, LANES), jnp.float32)
    for j in range(list_ref.shape[0]):
        target = jnp.where(list_ref[j] < blocks, dest_ref[j], -1)
        hits = hits + jnp.where(lane == target, 1.0, 0.0)
    hits_ref[...] = hits
    copies[1].wait()
    copies[0].wait()

    def write(up_ref, down_ref):
        for half in range(halves):
            start = half * part
            for j in range(BEHIND):
                up_ref[start + j * species : start + (j + 1) * species, :] = row(
                    length - BEHIND + j, half
                )
            for j in range(AHEAD):
                down_ref[start + j * species : start + (j + 1) * species, :] = row(j, half)
            for j in range(AHEAD, BEHIND):
                down_ref[start + j * species : start + (j + 1) * species, :] = jnp.zeros(
                    (species, LANES), jnp.float32
                )
            high, low = spot(length - SUB, half, halves), spot(0, half, halves)
            up_ref[start + BEHIND * species : start + part, :] = rates_ref[high : high + SUB, :]
            down_ref[start + BEHIND * species : start + part, :] = rates_ref[low : low + SUB, :]
        up_ref[halves * part :, :] = hits
        down_ref[halves * part :, :] = hits

    even = lax.rem(lax.axis_index("tile"), 2) == 0

    @pl.when(even)
    def _():
        write(even_ref, odd_ref)

    @pl.when(jnp.logical_not(even))
    def _():
        write(odd_ref, even_ref)


def inner_kernel(dests, length, halves, q_ref, rates_ref, *out_refs):
    species = out_refs[0].shape[0]
    share = length // dests
    me = lax.axis_index("spec")
    for k in range(dests):
        first = lax.rem(me + k, dests) * share
        below = jnp.maximum(first - SUB, 0)
        above = jnp.minimum(first + share, length - SUB)
        for half in range(halves):

            def start(at):
                if at < 0:
                    return below * halves + spot(at + SUB, half, halves)
                if at >= share:
                    return above * halves + spot(at - share, half, halves)
                return first * halves + spot(at, half, halves)

            reach = range(-BEHIND, share + AHEAD)
            rows = [q_ref[pl.ds(start(at), species, stride=length * halves), :] for at in reach]
            rates = [
                with_damp(rates_ref[pl.ds(start(at), 1), :], (species, LANES)) for at in reach
            ]
            for at, value in enumerate(two_sweeps(rows, rates)):
                place = (at * halves + half) * LANES
                out_refs[k][:, place : place + LANES] = value.astype(jnp.bfloat16)


def edge_kernel(dests, length, halves, even_ref, odd_ref, hits_ref, q_ref, rates_ref, *refs):
    out_refs = refs[dests : 2 * dests]
    to_even_ref, to_odd_ref, known_ref = refs[2 * dests :]
    species, cells = out_refs[0].shape
    part = BEHIND * species + SUB
    reach = BEHIND + AHEAD
    me = lax.axis_index("spec")
    even = lax.rem(lax.axis_index("tile"), 2) == 0
    own, from_even, from_odd = hits_ref[...], even_ref[halves * part :, :], odd_ref[halves * part :, :]
    known_ref[...] = own + from_even + from_odd
    to_even_ref[...] = from_odd
    to_odd_ref[...] = from_even

    def message(behind, at, size):
        a, b = odd_ref[at : at + size, :], even_ref[at : at + size, :]
        return jnp.where(even, a, b) if behind else jnp.where(even, b, a)

    def row(at, half):
        return q_ref[pl.ds(spot(at, half, halves), species, stride=length * halves), :]

    def rates_of(values):
        return [with_damp(value, (species, LANES)) for value in values]

    tops, bottoms = [], []
    for half in range(halves):
        base = half * part
        behind = [message(True, base + j * species, species) for j in range(BEHIND)]
        ahead = [message(False, base + j * species, species) for j in range(AHEAD)]
        before = message(True, base + BEHIND * species, SUB)
        after = message(False, base + BEHIND * species, SUB)

        def own_rates(first):
            places = [spot(first + j, half, halves) for j in range(reach)]
            return [rates_ref[at : at + 1, :] for at in places]

        tops.append(
            two_sweeps(
                behind + [row(j, half) for j in range(reach)],
                rates_of([before[SUB - BEHIND + j :][:1] for j in range(BEHIND)] + own_rates(0)),
            )
        )
        bottoms.append(
            two_sweeps(
                [row(length - reach + j, half) for j in range(reach)] + ahead,
                rates_of(own_rates(length - reach) + [after[j : j + 1] for j in range(AHEAD)]),
            )
        )
    top = [tops[half][j].astype(jnp.bfloat16) for j in range(BEHIND) for half in range(halves)]
    bottom = [bottoms[half][j].astype(jnp.bfloat16) for j in range(AHEAD) for half in range(halves)]
    for k in range(dests):
        dest = lax.rem(me + k, dests)

        @pl.when(dest == 0)
        def _():
            for j, value in enumerate(top):
                out_refs[k][:, j * LANES : (j + 1) * LANES] = value

        @pl.when(dest == dests - 1)
        def _():
            for j, value in enumerate(bottom):
                at = cells + (j - len(bottom)) * LANES
                out_refs[k][:, at : at + LANES] = value


def weight_kernel(w1_ref, w2_ref, after_ref, w1_out, w2_out):
    w1_out[...] = (0.5 * w1_ref[...].astype(jnp.float32)).T.astype(jnp.bfloat16)
    w2_out[...] = (0.5 * w2_ref[...].astype(jnp.float32)).T.astype(jnp.bfloat16)


def chemistry_kernel(groups, list_in, w1_ref, w2_ref, w3_ref, known_ref, even_ref, odd_ref, *refs):
    parts = refs[:groups]
    out_ref, share_ref, list_ref, state_ref, picked_ref, fresh_ref, done = refs[groups:]
    species, cells = state_ref.shape[1:]
    slots = list_ref.shape[0]
    blocks = cells // BLK
    me = lax.axis_index("spec")
    listing = pltpu.make_async_copy(list_in, list_ref, done.at[0])
    listing.start()
    for k in range(groups):
        state_ref[lax.rem(me - k + groups, groups)] = parts[k][...]
    whole = pltpu.make_async_copy(state_ref, out_ref, done.at[1])
    whole.start()
    hits = known_ref[...] + even_ref[...] + odd_ref[...]
    lane = lax.broadcasted_iota(jnp.int32, hits.shape, 1)
    mine = jnp.where(lane == lax.axis_index("tile"), hits, 0.0)
    share_ref[...] = jnp.sum(mine[0:1], axis=1, keepdims=True) / RECV
    listing.wait()

    def place(j):
        return pl.ds(pl.multiple_of(jnp.minimum(list_ref[j], blocks - 1) * BLK, BLK), BLK)

    for j in range(slots):
        for g in range(groups):
            picked_ref[g * species : (g + 1) * species, j * BLK : (j + 1) * BLK] = state_ref[
                g, :, place(j)
            ].astype(jnp.float32)

    def result(j):
        return pltpu.make_async_copy(fresh_ref.at[j], out_ref.at[:, :, place(j)], done.at[2 + j])

    each = 4
    for first in range(0, slots, each):
        x = picked_ref[:, first * BLK : (first + each) * BLK]
        hidden = jnp.dot(w1_ref[...], x.astype(jnp.bfloat16), preferred_element_type=jnp.float32)
        hidden = silu_of_half(hidden).astype(jnp.bfloat16)
        hidden = jnp.dot(w2_ref[...], hidden, preferred_element_type=jnp.float32)
        hidden = silu_of_half(hidden).astype(jnp.bfloat16)
        y = x + jnp.dot(w3_ref[...], hidden, preferred_element_type=jnp.float32)
        for j in range(first, first + each):
            for g in range(groups):
                fresh_ref[j, g] = y[
                    g * species : (g + 1) * species, (j - first) * BLK : (j - first + 1) * BLK
                ].astype(jnp.bfloat16)
        if first == 0:
            whole.wait()
        for j in range(first, first + each):

            @pl.when(list_ref[j] < blocks)
            def _():
                result(j).start()

    for j in range(slots):

        @pl.when(list_ref[j] < blocks)
        def _():
            result(j).wait()


def vmem():
    return pl.BlockSpec(memory_space=pltpu.VMEM)


def anywhere():
    return pl.BlockSpec(memory_space=pl.ANY)


def from_hbm(x):
    return pltpu.with_memory_space_constraint(x, pltpu.HBM)


def cost(us):
    return pl.CostEstimate(flops=int(us * 1e9), bytes_accessed=int(us * 3e6), transcendentals=0)


def shards(
    concentrations, courant, first_weight, middle_weight, last_weight, active_blocks, dest_tile
):
    species, length, cols = concentrations.shape
    dests = lax.axis_size("spec")
    tiles = lax.axis_size("tile")
    cells = length // dests * cols
    slots = active_blocks.shape[-1]
    halves = cols // LANES
    f32, bf16 = jnp.float32, jnp.bfloat16
    params = pltpu.CompilerParams(vmem_limit_bytes=VMEM_BYTES)
    listing = active_blocks.reshape(-1)
    size = halves * (BEHIND * species + SUB) + SUB
    flag = jax.ShapeDtypeStruct((SUB, LANES), f32)
    block = jax.ShapeDtypeStruct((species, cells), bf16)

    to_even, to_odd, hits, field, rates = pl.pallas_call(
        functools.partial(pack_kernel, length, halves, cells // BLK),
        out_shape=[jax.ShapeDtypeStruct((size, LANES), f32)] * 2
        + [
            flag,
            jax.ShapeDtypeStruct((species * length * halves, LANES), f32),
            jax.ShapeDtypeStruct((length * halves, LANES), f32),
        ],
        in_specs=[anywhere()] * 4,
        out_specs=[vmem()] * 5,
        scratch_shapes=[
            pltpu.SMEM((slots,), jnp.int32),
            pltpu.SMEM((slots,), jnp.int32),
            pltpu.SemaphoreType.DMA((4,)),
        ],
        compiler_params=params,
        cost_estimate=cost(1.0),
        name="pack_edges",
    )(
        from_hbm(tiled(concentrations, halves).reshape(species * length * halves, LANES)),
        from_hbm(tiled(courant, halves)),
        from_hbm(listing),
        from_hbm(dest_tile.reshape(-1)),
    )
    evens = [(t, t ^ 1) for t in range(tiles)]
    odds = [(t, ((t + 1) ^ 1) - 1) for t in range(tiles)]
    odds = [(t, other % tiles) for t, other in odds]
    from_even = lax.ppermute(to_even, "tile", evens)
    from_odd = lax.ppermute(to_odd, "tile", odds)
    blocks = pl.pallas_call(
        functools.partial(inner_kernel, dests, length, halves),
        out_shape=[block] * dests,
        in_specs=[vmem()] * 2,
        out_specs=[vmem()] * dests,
        compiler_params=params,
        cost_estimate=cost(1.0),
        name="inner_rows",
    )(field, rates)
    *blocks, to_even, to_odd, known = pl.pallas_call(
        functools.partial(edge_kernel, dests, length, halves),
        out_shape=[block] * dests + [flag] * 3,
        in_specs=[vmem()] * (5 + dests),
        out_specs=[vmem()] * (dests + 3),
        input_output_aliases={5 + k: k for k in range(dests)},
        compiler_params=params,
        cost_estimate=cost(0.1),
        name="edge_rows",
    )(from_even, from_odd, hits, field, rates, *blocks)
    received = [blocks[0]] + [
        lax.ppermute(blocks[k], "spec", [(s, (s + k) % dests) for s in range(dests)])
        for k in range(1, dests)
    ]
    from_even = lax.ppermute(to_even, "tile", evens)
    from_odd = lax.ppermute(to_odd, "tile", odds)
    w1, w2 = pl.pallas_call(
        weight_kernel,
        out_shape=[jax.ShapeDtypeStruct(w.shape[::-1], bf16) for w in (first_weight, middle_weight)],
        in_specs=[vmem(), vmem(), anywhere()],
        out_specs=[vmem()] * 2,
        compiler_params=params,
        cost_estimate=cost(0.5),
        name="halved_weights",
    )(first_weight, middle_weight, known)
    out, load_share = pl.pallas_call(
        functools.partial(chemistry_kernel, dests),
        out_shape=[
            jax.ShapeDtypeStruct((dests, species, cells), bf16),
            jax.ShapeDtypeStruct((1, 1), f32),
        ],
        in_specs=[anywhere()] + [vmem()] * (6 + dests),
        out_specs=[anywhere(), vmem()],
        scratch_shapes=[
            pltpu.SMEM((slots,), jnp.int32),
            pltpu.VMEM((dests, species, cells), bf16),
            pltpu.VMEM((dests * species, slots * BLK), f32),
            pltpu.VMEM((slots, dests, species, BLK), bf16),
            pltpu.SemaphoreType.DMA((2 + slots,)),
        ],
        compiler_params=params,
        cost_estimate=cost(4.0),
        name="chemistry",
    )(
        from_hbm(listing),
        w1,
        w2,
        last_weight.T,
        known,
        from_even,
        from_odd,
        *received,
    )
    return out.reshape(dests * species, cells), load_share


def solution(mesh):
    in_specs = (
        P("spec", "tile", None),
        P("tile", None),
        P(),
        P(),
        P(),
        P("tile", "spec", None),
        P("tile", "spec", None),
    )
    out_specs = (P(None, ("tile", "spec")), P("tile", "spec"))
    return jax.shard_map(shards, mesh=mesh, in_specs=in_specs, out_specs=out_specs, check_vma=False)
```

time: 38 us -> 22.4 us (0.59)
  Pallas kernels: 0 us -> 7 us
  other arithmetic: 5.37 us -> 0 us
  starting transfers between devices: 16.2 us -> 11.5 us
  between operations: 5.04 us -> 0.7 us
  matrix products: 4.14 us -> 0 us
  local copies, waits for them, and re-layouts: 3.59 us -> 0.01 us
    pallas_call x0 -> x5, Pallas kernels: none -> 7 us  [the longest x1 4.81 us: shards(): pl.pallas_call(functools.partial(chemistry_kernel, dests), out_shape=[jax...]
    all_to_all x1 -> x0, starting transfers between devices: 5.63 us -> none  [shards(): lax.all_to_all(advected, 'spec', split_axis=1, concat_axis=0, tiled=True)]
    dot_general x4 -> x0, matrix products: 4.14 us -> none  [the longest x1 2.27 us: surrogate(): change = jnp.dot(last_weight.T, second, preferred_element_type=jnp.float32)]
    mul x2 -> x0, other arithmetic: 2.54 us -> none  [advect(): fluxes = courants * (centre + 0.5 * (1.0 - courants) * slopes)]
    slice x3 -> x0, local copies, waits for them, and re-layouts: 1.66 us -> none  [the longest x2 0.9 us: extended(): initial = lax.slice_in_dim(x, 0, width, axis=dim)]
    all_to_all x1 -> x0, waiting for transfers between devices: 1.19 us -> none  [shards(): lax.all_to_all(advected, 'spec', split_axis=1, concat_axis=0, tiled=True)]
    add x1 -> x0, other arithmetic: 1.12 us -> none  [advect(): return centre[:, 1:] - fluxes[:, 1:] + fluxes[:, :-1]]
    all_to_all x2 -> x0, local copies, waits for them, and re-layouts: 1.03 us -> none  [shards(): lax.all_to_all(advected, 'spec', split_axis=1, concat_axis=0, tiled=True)]
  transfers between devices with their start and end apart: 10 -> 7, of which waited for: 6 -> 2; matrix products, arithmetic and copies ran while one was open for 7% -> 0% of each run, Pallas kernels for 0% -> 4%
where the time goes in v2:
time: 22.4 us; the launch traced here: 22.2 us
  starting transfers between devices  11.5 us (51%)
  Pallas kernels  7 us (31%)
  waiting for transfers between devices  3.04 us (14%)
  between operations  0.7 us (3%)
    ppermute x3, starting transfers between devices, shards(): lax.ppermute(blocks[k], 'spec', [(s, (s + k) % dests) for s in range(dest...  5.72 us
    ppermute x2, starting transfers between devices, shards(): from_odd = lax.ppermute(to_odd, 'tile', odds)  5.22 us
    pallas_call x1, Pallas kernels, shards(): pl.pallas_call(functools.partial(chemistry_kernel, dests), out_shape=[jax...  4.81 us
    ppermute x2, waiting for transfers between devices, shards(): from_odd = lax.ppermute(to_odd, 'tile', odds)  3.03 us
    pallas_call x1, Pallas kernels, shards(): pl.pallas_call(functools.partial(pack_kernel, length, halves, cells // BL...  1.11 us
    pallas_call x1, Pallas kernels, shards(): pl.pallas_call(functools.partial(inner_kernel, dests, length, halves), ou...  0.67 us
    ppermute x2, starting transfers between devices, shards(): from_even = lax.ppermute(to_even, 'tile', evens)  0.52 us
  transfers between devices with their start and end apart: 7, of which 2 were waited for; matrix products, arithmetic and copies ran while one was open for 0% of the time, Pallas kernels for 4%

profile of v2, /device:TPU:0, one launch (start us, length us, event | category | flops | bytes accessed | tf_op | source)
XLA Modules:
  0.0 22.2 jit_solution(13183646606456157908)
XLA Ops:
  0.6 1.1 %pack_edges.1 = (f32[88,128]{1,0:T(8,128)S(1)}, f32[88,128]{1,0:T(8,128)S(1)}, f32[8,128]{1,0:T(8,128)S(1)}, f32[1024,128]{1,0:T(8,128)S(1)}, f32[128,128]{1,0:T(8,128)S(1)}) custom-call(f32[1024,128]{1,0:T(8,128)} %bitcast.15, f32[128,128]{1,0:T(8,128)} %bitcast.16, s32[16]{0:T(128)} %bitcast.18, s32[16]{0:T(128)} %bitcast.17), custom_call_target="tpu_custom_call" | custom-call | flops 1000000000 | bytes 3000000 | tf_op jit(solution)/shard_map/pack_edges/pallas_call | solution.py:303
  1.8 0.5 %collective-permute-start = (f32[88,128]{1,0:T(8,128)S(1)}, f32[88,128]{1,0:T(8,128)S(1)}, u32[]{:S(2)}, u32[]{:S(2)}) collective-permute-start(f32[88,128]{1,0:T(8,128)S(1)} %get-tuple-element.22), channel_id=1, source_target_pairs={{0,4},{4,0},{8,12},{12,8},{16,20},{20,16},{24,28},{28,24},{1,5},{5... | collective-permute-start | bytes 135176 | tf_op jit(solution)/shard_map/ppermute | solution.py:330
  2.3 3.6 %collective-permute-start.1 = (f32[88,128]{1,0:T(8,128)S(1)}, f32[88,128]{1,0:T(8,128)S(1)}, u32[]{:S(2)}, u32[]{:S(2)}) collective-permute-start(f32[88,128]{1,0:T(8,128)S(1)} %get-tuple-element.23), channel_id=1, source_target_pairs={{0,28},{4,8},{8,4},{12,16},{16,12},{20,24},{24,20},{28,0},{1,29},{... | collective-permute-start | bytes 135176 | tf_op jit(solution)/shard_map/ppermute | solution.py:331
  5.8 0.7 %inner_rows.1 = (bf16[8,4096]{1,0:T(8,128)(2,1)S(1)}, bf16[8,4096]{1,0:T(8,128)(2,1)S(1)}, bf16[8,4096]{1,0:T(8,128)(2,1)S(1)}, bf16[8,4096]{1,0:T(8,128)(2,1)S(1)}) custom-call(f32[1024,128]{1,0:T(8,128)S(1)} %get-tuple-element.25.q_ref, f32[128,128]{1,0:T(8,128)S(1)} %get-tuple-element.26.rates_ref), custom_call_target="tpu_custom_call" | custom-call | flops 1000000000 | bytes 3000000 | tf_op jit(solution)/shard_map/inner_rows/pallas_call | solution.py:332
  6.5 0.0 copy-start
  6.5 0.0 collective-permute-done.even_ref
  6.5 1.0 %collective-permute-done.1.odd_ref = f32[88,128]{1,0:T(8,128)S(1)} collective-permute-done((f32[88,128]{1,0:T(8,128)S(1)}, f32[88,128]{1,0:T(8,128)S(1)}, u32[]{:S(2)}, u32[]{:S(2)}) %collective-permute-start.1) | collective-permute-done | bytes 45088 | tf_op jit(solution)/shard_map/ppermute | solution.py:331
  7.6 0.0 copy-start.1
  7.6 0.2 edge_rows.1
  7.7 1.8 %collective-permute-start.4 = (bf16[8,4096]{1,0:T(8,128)(2,1)S(1)}, bf16[8,4096]{1,0:T(8,128)(2,1)S(1)}, u32[]{:S(2)}, u32[]{:S(2)}) collective-permute-start(bf16[8,4096]{1,0:T(8,128)(2,1)S(1)} %get-tuple-element.37), channel_id=1, source_target_pairs={{0,1},{1,2},{2,3},{3,0},{4,5},{5,6},{6,7},{7,4},{8,9},{9,10},{10,1... | collective-permute-start | bytes 196616 | tf_op jit(solution)/shard_map/ppermute | solution.py:352
  9.5 2.6 %collective-permute-start.5 = (bf16[8,4096]{1,0:T(8,128)(2,1)S(1)}, bf16[8,4096]{1,0:T(8,128)(2,1)S(1)}, u32[]{:S(2)}, u32[]{:S(2)}) collective-permute-start(bf16[8,4096]{1,0:T(8,128)(2,1)S(1)} %get-tuple-element.38), channel_id=1, source_target_pairs={{0,2},{1,3},{2,0},{3,1},{4,6},{5,7},{6,4},{7,5},{8,10},{9,11},{10,... | collective-permute-start | bytes 196616 | tf_op jit(solution)/shard_map/ppermute | solution.py:352
  12.1 1.3 %collective-permute-start.6 = (bf16[8,4096]{1,0:T(8,128)(2,1)S(1)}, bf16[8,4096]{1,0:T(8,128)(2,1)S(1)}, u32[]{:S(2)}, u32[]{:S(2)}) collective-permute-start(bf16[8,4096]{1,0:T(8,128)(2,1)S(1)} %get-tuple-element.39), channel_id=1, source_target_pairs={{0,3},{1,0},{2,1},{3,2},{4,7},{5,4},{6,5},{7,6},{8,11},{9,8},{10,9... | collective-permute-start | bytes 196616 | tf_op jit(solution)/shard_map/ppermute | solution.py:352
  13.4 0.0 collective-permute-start.2
  13.4 1.7 %collective-permute-start.3 = (f32[8,128]{1,0:T(8,128)S(1)}, f32[8,128]{1,0:T(8,128)S(1)}, u32[]{:S(2)}, u32[]{:S(2)}) collective-permute-start(f32[8,128]{1,0:T(8,128)S(1)} %get-tuple-element.35), channel_id=1, source_target_pairs={{0,28},{4,8},{8,4},{12,16},{16,12},{20,24},{24,20},{28,0},{1,29},{... | collective-permute-start | bytes 12296 | tf_op jit(solution)/shard_map/ppermute | solution.py:356
  15.1 0.0 copy-done
  15.1 0.0 copy-done.1
  15.1 0.0 copy-start.2
  15.1 0.2 %halved_weights.1 = (bf16[512,32]{1,0:T(8,128)(2,1)S(1)}, bf16[512,512]{1,0:T(8,128)(2,1)S(1)}) custom-call(bf16[32,512]{1,0:T(8,128)(2,1)S(1)} %copy-done.1, bf16[512,512]{1,0:T(8,128)(2,1)S(1)} %copy-done, f32[8,128]{1,0:T(8,128)S(1)} %get-tuple-element.31.after_ref.known_ref), custom_call_target="tpu_custom_call" | custom-call | flops 500000000 | bytes 1500000 | tf_op jit(solution)/shard_map/halved_weights/pallas_call | solution.py:357
  15.4 0.0 collective-permute-done.2.even_ref
  15.4 2.0 %collective-permute-done.3.odd_ref = f32[8,128]{1,0:T(8,128)S(1)} collective-permute-done((f32[8,128]{1,0:T(8,128)S(1)}, f32[8,128]{1,0:T(8,128)S(1)}, u32[]{:S(2)}, u32[]{:S(2)}) %collective-permute-start.3) | collective-permute-done | bytes 4128 | tf_op jit(solution)/shard_map/ppermute | solution.py:356
  17.4 0.0 collective-permute-done.4.refs_1_
  17.4 0.0 collective-permute-done.5.refs_2_
  17.4 0.0 collective-permute-done.6.refs_3_
  17.4 0.0 copy-done.2
  17.4 4.8 %chemistry.1 = (bf16[4,8,4096]{2,1,0:T(8,128)(2,1)}, f32[1,1]{1,0:T(1,128)}) custom-call(s32[16]{0:T(128)} %bitcast.19, bf16[512,32]{1,0:T(8,128)(2,1)S(1)} %get-tuple-element.32.w1_ref, bf16[512,512]{1,0:T(8,128)(2,1)S(1)} %get-tuple-element.33.w2_ref, bf16[32,512]{1,0:T(8,128)(2,1)S(1)} %bitcast.14, f32[8,128]{1,0:T(8,128)S(1)} %get-tuple-element.31.after_ref.known_ref, ...), custom_call_target="tpu_custom_call" | custom-call | flops 4000000000 | bytes 12000000 | tf_op jit(solution)/shard_map/chemistry/pallas_call | solution.py:366
Async XLA Ops:
  1.8 4.8 %collective-permute-start = (f32[88,128]{1,0:T(8,128)S(1)}, f32[88,128]{1,0:T(8,128)S(1)}, u32[]{:S(2)}, u32[]{:S(2)}) collective-permute-start(f32[88,128]{1,0:T(8,128)S(1)} %get-tuple-element.22), channel_id=1, source_target_pairs={{0,4},{4,0},{8,12},{12,8},{16,20},{20,16},{24,28},{28,24},{1,5},{5... | collective-permute-start | bytes 135176 | tf_op jit(solution)/shard_map/ppermute | solution.py:330
  2.3 5.3 %collective-permute-start.1 = (f32[88,128]{1,0:T(8,128)S(1)}, f32[88,128]{1,0:T(8,128)S(1)}, u32[]{:S(2)}, u32[]{:S(2)}) collective-permute-start(f32[88,128]{1,0:T(8,128)S(1)} %get-tuple-element.23), channel_id=1, source_target_pairs={{0,28},{4,8},{8,4},{12,16},{16,12},{20,24},{24,20},{28,0},{1,29},{... | collective-permute-start | bytes 135176 | tf_op jit(solution)/shard_map/ppermute | solution.py:331
  6.5 8.6 %copy-start = (bf16[512,512]{1,0:T(8,128)(2,1)S(1)}, bf16[512,512]{1,0:T(8,128)(2,1)}, u32[]{:S(2)}) copy-start(bf16[512,512]{1,0:T(8,128)(2,1)} %w2_ref.1) | copy-start | bytes 1572868
  7.6 7.6 %copy-start.1 = (bf16[32,512]{1,0:T(8,128)(2,1)S(1)}, bf16[32,512]{1,0:T(8,128)(2,1)}, u32[]{:S(2)}) copy-start(bf16[32,512]{1,0:T(8,128)(2,1)} %w1_ref.1) | copy-start | bytes 98308
  7.7 9.7 %collective-permute-start.4 = (bf16[8,4096]{1,0:T(8,128)(2,1)S(1)}, bf16[8,4096]{1,0:T(8,128)(2,1)S(1)}, u32[]{:S(2)}, u32[]{:S(2)}) collective-permute-start(bf16[8,4096]{1,0:T(8,128)(2,1)S(1)} %get-tuple-element.37), channel_id=1, source_target_pairs={{0,1},{1,2},{2,3},{3,0},{4,5},{5,6},{6,7},{7,4},{8,9},{9,10},{10,1... | collective-permute-start | bytes 196616 | tf_op jit(solution)/shard_map/ppermute | solution.py:352
  9.5 7.9 %collective-permute-start.5 = (bf16[8,4096]{1,0:T(8,128)(2,1)S(1)}, bf16[8,4096]{1,0:T(8,128)(2,1)S(1)}, u32[]{:S(2)}, u32[]{:S(2)}) collective-permute-start(bf16[8,4096]{1,0:T(8,128)(2,1)S(1)} %get-tuple-element.38), channel_id=1, source_target_pairs={{0,2},{1,3},{2,0},{3,1},{4,6},{5,7},{6,4},{7,5},{8,10},{9,11},{10,... | collective-permute-start | bytes 196616 | tf_op jit(solution)/shard_map/ppermute | solution.py:352
  12.1 5.3 %collective-permute-start.6 = (bf16[8,4096]{1,0:T(8,128)(2,1)S(1)}, bf16[8,4096]{1,0:T(8,128)(2,1)S(1)}, u32[]{:S(2)}, u32[]{:S(2)}) collective-permute-start(bf16[8,4096]{1,0:T(8,128)(2,1)S(1)} %get-tuple-element.39), channel_id=1, source_target_pairs={{0,3},{1,0},{2,1},{3,2},{4,7},{5,4},{6,5},{7,6},{8,11},{9,8},{10,9... | collective-permute-start | bytes 196616 | tf_op jit(solution)/shard_map/ppermute | solution.py:352
  13.4 1.9 %collective-permute-start.2 = (f32[8,128]{1,0:T(8,128)S(1)}, f32[8,128]{1,0:T(8,128)S(1)}, u32[]{:S(2)}, u32[]{:S(2)}) collective-permute-start(f32[8,128]{1,0:T(8,128)S(1)} %get-tuple-element.34), channel_id=1, source_target_pairs={{0,4},{4,0},{8,12},{12,8},{16,20},{20,16},{24,28},{28,24},{1,5},{5... | collective-permute-start | bytes 12296 | tf_op jit(solution)/shard_map/ppermute | solution.py:355
  13.4 3.9 %collective-permute-start.3 = (f32[8,128]{1,0:T(8,128)S(1)}, f32[8,128]{1,0:T(8,128)S(1)}, u32[]{:S(2)}, u32[]{:S(2)}) collective-permute-start(f32[8,128]{1,0:T(8,128)S(1)} %get-tuple-element.35), channel_id=1, source_target_pairs={{0,28},{4,8},{8,4},{12,16},{16,12},{20,24},{24,20},{28,0},{1,29},{... | collective-permute-start | bytes 12296 | tf_op jit(solution)/shard_map/ppermute | solution.py:356
  15.1 2.3 %copy-start.2 = (bf16[512,32]{0,1:T(8,128)(2,1)S(1)}, bf16[512,32]{0,1:T(8,128)(2,1)}, u32[]{:S(2)}) copy-start(bf16[512,32]{0,1:T(8,128)(2,1)} %param.11) | copy-start | bytes 98308

commit v3 on v2

--- a/solution.py
+++ b/solution.py
@@ -140,9 +140,11 @@
                 out_refs[k][:, place : place + LANES] = value.astype(jnp.bfloat16)
 
 
-def edge_kernel(dests, length, halves, even_ref, odd_ref, hits_ref, q_ref, rates_ref, *refs):
-    out_refs = refs[dests : 2 * dests]
-    to_even_ref, to_odd_ref, known_ref = refs[2 * dests :]
+def edge_kernel(
+    dests, early, late, length, halves, even_ref, odd_ref, hits_ref, q_ref, rates_ref, *refs
+):
+    out_refs, refs = refs[len(late) : 2 * len(late)], refs[2 * len(late) :]
+    small_refs, (to_even_ref, to_odd_ref, known_ref) = refs[: len(early)], refs[len(early) :]
     species, cells = out_refs[0].shape
     part = BEHIND * species + SUB
     reach = BEHIND + AHEAD
@@ -187,21 +189,29 @@
                 rates_of(own_rates(length - reach) + [after[j : j + 1] for j in range(AHEAD)]),
             )
         )
-    top = [tops[half][j].astype(jnp.bfloat16) for j in range(BEHIND) for half in range(halves)]
-    bottom = [bottoms[half][j].astype(jnp.bfloat16) for j in range(AHEAD) for half in range(halves)]
-    for k in range(dests):
+    top = [tops[half][j] for j in range(BEHIND) for half in range(halves)]
+    bottom = [bottoms[half][j] for j in range(AHEAD) for half in range(halves)]
+    for k, small_ref in zip(early, small_refs):
+        low = lax.rem(me + k, dests) == 0
+        skip = len(top) - len(bottom)
+        for j, value in enumerate(top):
+            other = bottom[j - skip] if j >= skip else value
+            small_ref[:, j * LANES : (j + 1) * LANES] = jnp.where(low, value, other).astype(
+                jnp.bfloat16
+            )
+    for k, out_ref in zip(late, out_refs):
         dest = lax.rem(me + k, dests)
 
         @pl.when(dest == 0)
         def _():
             for j, value in enumerate(top):
-                out_refs[k][:, j * LANES : (j + 1) * LANES] = value
+                out_ref[:, j * LANES : (j + 1) * LANES] = value.astype(jnp.bfloat16)
 
         @pl.when(dest == dests - 1)
         def _():
             for j, value in enumerate(bottom):
                 at = cells + (j - len(bottom)) * LANES
-                out_refs[k][:, at : at + LANES] = value
+                out_ref[:, at : at + LANES] = value.astype(jnp.bfloat16)
 
 
 def weight_kernel(w1_ref, w2_ref, after_ref, w1_out, w2_out):
@@ -209,24 +219,40 @@
     w2_out[...] = (0.5 * w2_ref[...].astype(jnp.float32)).T.astype(jnp.bfloat16)
 
 
-def chemistry_kernel(groups, list_in, w1_ref, w2_ref, w3_ref, known_ref, even_ref, odd_ref, *refs):
-    parts = refs[:groups]
-    out_ref, share_ref, list_ref, state_ref, picked_ref, fresh_ref, done = refs[groups:]
+def chemistry_kernel(
+    groups, early, list_ref, w1_ref, w2_ref, w3_ref, known_ref, even_ref, odd_ref, *refs
+):
+    parts, edges, refs = refs[:groups], refs[groups : groups + len(early)], refs[groups + len(early) :]
+    out_ref, share_ref, state_ref, picked_ref, held_ref, done = refs
     species, cells = state_ref.shape[1:]
     slots = list_ref.shape[0]
     blocks = cells // BLK
     me = lax.axis_index("spec")
-    listing = pltpu.make_async_copy(list_in, list_ref, done.at[0])
-    listing.start()
+
+    def source(k):
+        return lax.rem(me - k + groups, groups)
+
     for k in range(groups):
-        state_ref[lax.rem(me - k + groups, groups)] = parts[k][...]
-    whole = pltpu.make_async_copy(state_ref, out_ref, done.at[1])
-    whole.start()
+        state_ref[source(k)] = parts[k][...]
+    wide = edges[0].shape[1]
+    narrow = wide // BEHIND * AHEAD
+
+    @pl.when(me == 0)
+    def _():
+        for k, edge in zip(early, edges):
+            state_ref[source(k), :, 0:wide] = edge[...]
+
+    @pl.when(me == groups - 1)
+    def _():
+        for k, edge in zip(early, edges):
+            state_ref[source(k), :, cells - narrow :] = edge[:, wide - narrow :]
+
     hits = known_ref[...] + even_ref[...] + odd_ref[...]
     lane = lax.broadcasted_iota(jnp.int32, hits.shape, 1)
     mine = jnp.where(lane == lax.axis_index("tile"), hits, 0.0)
-    share_ref[...] = jnp.sum(mine[0:1], axis=1, keepdims=True) / RECV
-    listing.wait()
+    held_ref[...] = jnp.sum(mine[0:1], axis=1, keepdims=True) / RECV
+    share = pltpu.make_async_copy(held_ref, share_ref, done.at[0])
+    share.start()
 
     def place(j):
         return pl.ds(pl.multiple_of(jnp.minimum(list_ref[j], blocks - 1) * BLK, BLK), BLK)
@@ -236,10 +262,6 @@
             picked_ref[g * species : (g + 1) * species, j * BLK : (j + 1) * BLK] = state_ref[
                 g, :, place(j)
             ].astype(jnp.float32)
-
-    def result(j):
-        return pltpu.make_async_copy(fresh_ref.at[j], out_ref.at[:, :, place(j)], done.at[2 + j])
-
     each = 4
     for first in range(0, slots, each):
         x = picked_ref[:, first * BLK : (first + each) * BLK]
@@ -247,25 +269,19 @@
         hidden = silu_of_half(hidden).astype(jnp.bfloat16)
         hidden = jnp.dot(w2_ref[...], hidden, preferred_element_type=jnp.float32)
         hidden = silu_of_half(hidden).astype(jnp.bfloat16)
-        y = x + jnp.dot(w3_ref[...], hidden, preferred_element_type=jnp.float32)
-        for j in range(first, first + each):
-            for g in range(groups):
-                fresh_ref[j, g] = y[
-                    g * species : (g + 1) * species, (j - first) * BLK : (j - first + 1) * BLK
-                ].astype(jnp.bfloat16)
-        if first == 0:
-            whole.wait()
-        for j in range(first, first + each):
-
-            @pl.when(list_ref[j] < blocks)
-            def _():
-                result(j).start()
-
+        picked_ref[:, first * BLK : (first + each) * BLK] = x + jnp.dot(
+            w3_ref[...], hidden, preferred_element_type=jnp.float32
+        )
     for j in range(slots):
-
-        @pl.when(list_ref[j] < blocks)
-        def _():
-            result(j).wait()
+        valid = list_ref[j] < blocks
+        for g in range(groups):
+            fresh = picked_ref[g * species : (g + 1) * species, j * BLK : (j + 1) * BLK]
+            now = state_ref[g, :, place(j)].astype(jnp.float32)
+            state_ref[g, :, place(j)] = jnp.where(valid, fresh, now).astype(jnp.bfloat16)
+    whole = pltpu.make_async_copy(state_ref, out_ref, done.at[1])
+    whole.start()
+    share.wait()
+    whole.wait()
 
 
 def vmem():
@@ -295,23 +311,22 @@
     halves = cols // LANES
     f32, bf16 = jnp.float32, jnp.bfloat16
     params = pltpu.CompilerParams(vmem_limit_bytes=VMEM_BYTES)
-    listing = active_blocks.reshape(-1)
     size = halves * (BEHIND * species + SUB) + SUB
     flag = jax.ShapeDtypeStruct((SUB, LANES), f32)
     block = jax.ShapeDtypeStruct((species, cells), bf16)
 
-    to_even, to_odd, hits, field, rates = pl.pallas_call(
+    to_even, to_odd, hits, field, rates, listing = pl.pallas_call(
         functools.partial(pack_kernel, length, halves, cells // BLK),
         out_shape=[jax.ShapeDtypeStruct((size, LANES), f32)] * 2
         + [
             flag,
             jax.ShapeDtypeStruct((species * length * halves, LANES), f32),
             jax.ShapeDtypeStruct((length * halves, LANES), f32),
+            jax.ShapeDtypeStruct((slots,), jnp.int32),
         ],
         in_specs=[anywhere()] * 4,
-        out_specs=[vmem()] * 5,
+        out_specs=[vmem()] * 5 + [pl.BlockSpec(memory_space=pltpu.SMEM)],
         scratch_shapes=[
-            pltpu.SMEM((slots,), jnp.int32),
             pltpu.SMEM((slots,), jnp.int32),
             pltpu.SemaphoreType.DMA((4,)),
         ],
@@ -321,7 +336,7 @@
     )(
         from_hbm(tiled(concentrations, halves).reshape(species * length * halves, LANES)),
         from_hbm(tiled(courant, halves)),
-        from_hbm(listing),
+        from_hbm(active_blocks.reshape(-1)),
         from_hbm(dest_tile.reshape(-1)),
     )
     evens = [(t, t ^ 1) for t in range(tiles)]
@@ -338,20 +353,26 @@
         cost_estimate=cost(1.0),
         name="inner_rows",
     )(field, rates)
-    *blocks, to_even, to_odd, known = pl.pallas_call(
-        functools.partial(edge_kernel, dests, length, halves),
-        out_shape=[block] * dests + [flag] * 3,
-        in_specs=[vmem()] * (5 + dests),
+    def ring(k, x):
+        return lax.ppermute(x, "spec", [(s, (s + k) % dests) for s in range(dests)])
+
+    order = [k for k in (2, 1) if k < dests] + list(range(3, dests))
+    early, late = order[: dests // 2], [0] + order[dests // 2 :]
+    received = {k: ring(k, blocks[k]) for k in early}
+    edge = jax.ShapeDtypeStruct((species, BEHIND * cols), bf16)
+    outs = pl.pallas_call(
+        functools.partial(edge_kernel, dests, early, late, length, halves),
+        out_shape=[block] * len(late) + [edge] * len(early) + [flag] * 3,
+        in_specs=[vmem()] * (5 + len(late)),
         out_specs=[vmem()] * (dests + 3),
-        input_output_aliases={5 + k: k for k in range(dests)},
+        input_output_aliases={5 + i: i for i in range(len(late))},
         compiler_params=params,
         cost_estimate=cost(0.1),
         name="edge_rows",
-    )(from_even, from_odd, hits, field, rates, *blocks)
-    received = [blocks[0]] + [
-        lax.ppermute(blocks[k], "spec", [(s, (s + k) % dests) for s in range(dests)])
-        for k in range(1, dests)
-    ]
+    )(from_even, from_odd, hits, field, rates, *[blocks[k] for k in late])
+    full, edges, (to_even, to_odd, known) = outs[: len(late)], outs[len(late) : dests], outs[dests:]
+    received |= {k: ring(k, x) if k else x for k, x in zip(late, full)}
+    edges = [ring(k, x) for k, x in zip(early, edges)]
     from_even = lax.ppermute(to_even, "tile", evens)
     from_odd = lax.ppermute(to_odd, "tile", odds)
     w1, w2 = pl.pallas_call(
@@ -364,32 +385,32 @@
         name="halved_weights",
     )(first_weight, middle_weight, known)
     out, load_share = pl.pallas_call(
-        functools.partial(chemistry_kernel, dests),
+        functools.partial(chemistry_kernel, dests, early),
         out_shape=[
             jax.ShapeDtypeStruct((dests, species, cells), bf16),
             jax.ShapeDtypeStruct((1, 1), f32),
         ],
-        in_specs=[anywhere()] + [vmem()] * (6 + dests),
-        out_specs=[anywhere(), vmem()],
+        in_specs=[pl.BlockSpec(memory_space=pltpu.SMEM)] + [vmem()] * (6 + dests + len(early)),
+        out_specs=[anywhere()] * 2,
         scratch_shapes=[
-            pltpu.SMEM((slots,), jnp.int32),
             pltpu.VMEM((dests, species, cells), bf16),
             pltpu.VMEM((dests * species, slots * BLK), f32),
-            pltpu.VMEM((slots, dests, species, BLK), bf16),
-            pltpu.SemaphoreType.DMA((2 + slots,)),
+            pltpu.VMEM((1, 1), f32),
+            pltpu.SemaphoreType.DMA((2,)),
         ],
         compiler_params=params,
         cost_estimate=cost(4.0),
         name="chemistry",
     )(
-        from_hbm(listing),
+        listing,
         w1,
         w2,
         last_weight.T,
         known,
         from_even,
         from_odd,
-        *received,
+        *[received[k] for k in range(dests)],
+        *edges,
     )
     return out.reshape(dests * species, cells), load_share
 

time: 22.4 us -> 26.6 us (1.19)
  waiting for transfers between devices: 3.04 us -> 7.05 us
  starting transfers between devices: 11.5 us -> 11.9 us
    ppermute x3 -> x5, waiting for transfers between devices: 0.01 us -> 4.61 us  [ring(): return lax.ppermute(x, 'spec', [(s, (s + k) % dests) for s in range(dests)])]
    pallas_call x2, Pallas kernels: 4.97 us -> 4.22 us  [the longest x1 4.08 us: shards(): pl.pallas_call(functools.partial(chemistry_kernel, dests, early), out_sha...]
    ppermute x3 -> x5, starting transfers between devices: 5.72 us -> 6.37 us  [ring(): return lax.ppermute(x, 'spec', [(s, (s + k) % dests) for s in range(dests)])]
    ppermute x2, waiting for transfers between devices: 3.03 us -> 2.43 us  [shards(): from_odd = lax.ppermute(to_odd, 'tile', odds)]
    pallas_call x1, Pallas kernels: 1.11 us -> 1.7 us  [shards(): pl.pallas_call(functools.partial(pack_kernel, length, halves, cells // BL...]
  transfers between devices with their start and end apart: 7 -> 9, of which waited for: 2 -> 3; matrix products, arithmetic and copies ran while one was open for 0% -> 0% of each run, Pallas kernels for 4% -> 4%
where the time goes in v3:
time: 26.6 us; the launch traced here: 26.5 us
  starting transfers between devices  11.9 us (45%)
  waiting for transfers between devices  7.05 us (27%)
  Pallas kernels  6.84 us (26%)
  between operations  0.69 us (3%)
    ppermute x5, starting transfers between devices, ring(): return lax.ppermute(x, 'spec', [(s, (s + k) % dests) for s in range(dests)])  6.37 us
    ppermute x2, starting transfers between devices, shards(): from_odd = lax.ppermute(to_odd, 'tile', odds)  4.98 us
    ppermute x5, waiting for transfers between devices, ring(): return lax.ppermute(x, 'spec', [(s, (s + k) % dests) for s in range(dests)])  4.61 us
    pallas_call x1, Pallas kernels, shards(): pl.pallas_call(functools.partial(chemistry_kernel, dests, early), out_sha...  4.08 us
    ppermute x2, waiting for transfers between devices, shards(): from_odd = lax.ppermute(to_odd, 'tile', odds)  2.43 us
    pallas_call x1, Pallas kernels, shards(): pl.pallas_call(functools.partial(pack_kernel, length, halves, cells // BL...  1.7 us
    pallas_call x1, Pallas kernels, shards(): pl.pallas_call(functools.partial(inner_kernel, dests, length, halves), ou...  0.67 us
  transfers between devices with their start and end apart: 9, of which 3 were waited for; matrix products, arithmetic and copies ran while one was open for 0% of the time, Pallas kernels for 4%

profile of v3, /device:TPU:0, one launch (start us, length us, event | category | flops | bytes accessed | tf_op | source)
XLA Modules:
  0.0 26.5 jit_solution(9800713437987833364)
XLA Ops:
  0.6 1.7 %pack_edges.1 = (f32[88,128]{1,0:T(8,128)S(1)}, f32[88,128]{1,0:T(8,128)S(1)}, f32[8,128]{1,0:T(8,128)S(1)}, f32[1024,128]{1,0:T(8,128)S(1)}, f32[128,128]{1,0:T(8,128)S(1)}, /*index=5*/s32[16]{0:T(128)S(1)}) custom-call(f32[1024,128]{1,0:T(8,128)} %bitcast.15, f32[128,128]{1,0:T(8,128)} %bitcast.16, s32[16]{0:T(128)} %bitcast.17, s32[16]{0:T(128)} %bitcast.18), custom_call_target="tpu_custom_call" | custom-call | flops 1000000000 | bytes 3000000 | tf_op jit(solution)/shard_map/pack_edges/pallas_call | solution.py:318
  2.3 0.5 %collective-permute-start = (f32[88,128]{1,0:T(8,128)S(1)}, f32[88,128]{1,0:T(8,128)S(1)}, u32[]{:S(2)}, u32[]{:S(2)}) collective-permute-start(f32[88,128]{1,0:T(8,128)S(1)} %get-tuple-element.24), channel_id=1, source_target_pairs={{0,4},{4,0},{8,12},{12,8},{16,20},{20,16},{24,28},{28,24},{1,5},{5... | collective-permute-start | bytes 135176 | tf_op jit(solution)/shard_map/ppermute | solution.py:345
  2.9 3.6 %collective-permute-start.1 = (f32[88,128]{1,0:T(8,128)S(1)}, f32[88,128]{1,0:T(8,128)S(1)}, u32[]{:S(2)}, u32[]{:S(2)}) collective-permute-start(f32[88,128]{1,0:T(8,128)S(1)} %get-tuple-element.25), channel_id=1, source_target_pairs={{0,28},{4,8},{8,4},{12,16},{16,12},{20,24},{24,20},{28,0},{1,29},{... | collective-permute-start | bytes 135176 | tf_op jit(solution)/shard_map/ppermute | solution.py:346
  6.4 0.7 %inner_rows.1 = (bf16[8,4096]{1,0:T(8,128)(2,1)S(1)}, bf16[8,4096]{1,0:T(8,128)(2,1)S(1)}, bf16[8,4096]{1,0:T(8,128)(2,1)S(1)}, bf16[8,4096]{1,0:T(8,128)(2,1)S(1)}) custom-call(f32[1024,128]{1,0:T(8,128)S(1)} %get-tuple-element.27.q_ref, f32[128,128]{1,0:T(8,128)S(1)} %get-tuple-element.28.rates_ref), custom_call_target="tpu_custom_call" | custom-call | flops 1000000000 | bytes 3000000 | tf_op jit(solution)/shard_map/inner_rows/pallas_call | solution.py:347
  7.1 0.0 copy-start
  7.1 1.6 %collective-permute-start.4 = (bf16[8,4096]{1,0:T(8,128)(2,1)S(1)}, bf16[8,4096]{1,0:T(8,128)(2,1)S(1)}, u32[]{:S(2)}, u32[]{:S(2)}) collective-permute-start(bf16[8,4096]{1,0:T(8,128)(2,1)S(1)} %get-tuple-element.37), channel_id=1, source_target_pairs={{0,1},{1,2},{2,3},{3,0},{4,5},{5,6},{6,7},{7,4},{8,9},{9,10},{10,1... | collective-permute-start | bytes 196616 | tf_op jit(solution)/shard_map/ppermute | solution.py:357
  8.7 2.6 %collective-permute-start.5 = (bf16[8,4096]{1,0:T(8,128)(2,1)S(1)}, bf16[8,4096]{1,0:T(8,128)(2,1)S(1)}, u32[]{:S(2)}, u32[]{:S(2)}) collective-permute-start(bf16[8,4096]{1,0:T(8,128)(2,1)S(1)} %get-tuple-element.38), channel_id=1, source_target_pairs={{0,2},{1,3},{2,0},{3,1},{4,6},{5,7},{6,4},{7,5},{8,10},{9,11},{10,... | collective-permute-start | bytes 196616 | tf_op jit(solution)/shard_map/ppermute | solution.py:357
  11.3 0.0 collective-permute-done.even_ref
  11.3 0.0 collective-permute-done.1.odd_ref
  11.3 0.0 copy-start.1
  11.3 0.1 edge_rows.1
  11.5 1.4 %collective-permute-start.6 = (bf16[8,4096]{1,0:T(8,128)(2,1)S(1)}, bf16[8,4096]{1,0:T(8,128)(2,1)S(1)}, u32[]{:S(2)}, u32[]{:S(2)}) collective-permute-start(bf16[8,4096]{1,0:T(8,128)(2,1)S(1)} %get-tuple-element.39), channel_id=1, source_target_pairs={{0,3},{1,0},{2,1},{3,2},{4,7},{5,4},{6,5},{7,6},{8,11},{9,8},{10,9... | collective-permute-start | bytes 196616 | tf_op jit(solution)/shard_map/ppermute | solution.py:357
  12.9 0.0 collective-permute-start.2
  12.9 1.4 %collective-permute-start.3 = (f32[8,128]{1,0:T(8,128)S(1)}, f32[8,128]{1,0:T(8,128)S(1)}, u32[]{:S(2)}, u32[]{:S(2)}) collective-permute-start(f32[8,128]{1,0:T(8,128)S(1)} %get-tuple-element.35), channel_id=1, source_target_pairs={{0,28},{4,8},{8,4},{12,16},{16,12},{20,24},{24,20},{28,0},{1,29},{... | collective-permute-start | bytes 12296 | tf_op jit(solution)/shard_map/ppermute | solution.py:377
  14.3 0.0 collective-permute-done.2.even_ref
  14.3 0.1 collective-permute-start.7
  14.4 2.4 %collective-permute-done.3.odd_ref = f32[8,128]{1,0:T(8,128)S(1)} collective-permute-done((f32[8,128]{1,0:T(8,128)S(1)}, f32[8,128]{1,0:T(8,128)S(1)}, u32[]{:S(2)}, u32[]{:S(2)}) %collective-permute-start.3) | collective-permute-done | bytes 4128 | tf_op jit(solution)/shard_map/ppermute | solution.py:377
  16.8 0.7 %collective-permute-start.8 = (bf16[8,1024]{1,0:T(8,128)(2,1)S(1)}, bf16[8,1024]{1,0:T(8,128)(2,1)S(1)}, u32[]{:S(2)}, u32[]{:S(2)}) collective-permute-start(bf16[8,1024]{1,0:T(8,128)(2,1)S(1)} %get-tuple-element.41), channel_id=1, source_target_pairs={{0,1},{1,2},{2,3},{3,0},{4,5},{5,6},{6,7},{7,4},{8,9},{9,10},{10,1... | collective-permute-start | bytes 49160 | tf_op jit(solution)/shard_map/ppermute | solution.py:357
  17.5 0.0 copy-done
  17.5 0.0 copy-done.1
  17.5 0.0 copy-start.2
  17.5 0.2 halved_weights.1
  17.8 1.2 %collective-permute-done.7.refs_4_ = bf16[8,1024]{1,0:T(8,128)(2,1)S(1)} collective-permute-done((bf16[8,1024]{1,0:T(8,128)(2,1)S(1)}, bf16[8,1024]{1,0:T(8,128)(2,1)S(1)}, u32[]{:S(2)}, u32[]{:S(2)}) %collective-permute-start.7) | collective-permute-done | bytes 16416 | tf_op jit(solution)/shard_map/ppermute | solution.py:357
  19.0 3.4 %collective-permute-done.8.refs_5_ = bf16[8,1024]{1,0:T(8,128)(2,1)S(1)} collective-permute-done((bf16[8,1024]{1,0:T(8,128)(2,1)S(1)}, bf16[8,1024]{1,0:T(8,128)(2,1)S(1)}, u32[]{:S(2)}, u32[]{:S(2)}) %collective-permute-start.8) | collective-permute-done | bytes 16416 | tf_op jit(solution)/shard_map/ppermute | solution.py:357
  22.4 0.0 collective-permute-done.4.refs_1_
  22.4 0.0 collective-permute-done.5.refs_2_
  22.4 0.0 collective-permute-done.6.refs_3_
  22.4 0.0 copy-done.2
  22.4 4.1 %chemistry.1 = (bf16[4,8,4096]{2,1,0:T(8,128)(2,1)}, f32[1,1]{1,0:T(1,128)}) custom-call(s32[16]{0:T(128)S(1)} %get-tuple-element.23.list_ref, bf16[512,32]{1,0:T(8,128)(2,1)S(1)} %get-tuple-element.32.w1_ref, bf16[512,512]{1,0:T(8,128)(2,1)S(1)} %get-tuple-element.33.w2_ref, bf16[32,512]{1,0:T(8,128)(2,1)S(1)} %bitcast.14, ...), custom_call_target="tpu_custom_call" | custom-call | flops 4000000000 | bytes 12000000 | tf_op jit(solution)/shard_map/chemistry/pallas_call | solution.py:387
Async XLA Ops:
  2.3 9.0 %collective-permute-start = (f32[88,128]{1,0:T(8,128)S(1)}, f32[88,128]{1,0:T(8,128)S(1)}, u32[]{:S(2)}, u32[]{:S(2)}) collective-permute-start(f32[88,128]{1,0:T(8,128)S(1)} %get-tuple-element.24), channel_id=1, source_target_pairs={{0,4},{4,0},{8,12},{12,8},{16,20},{20,16},{24,28},{28,24},{1,5},{5... | collective-permute-start | bytes 135176 | tf_op jit(solution)/shard_map/ppermute | solution.py:345
  2.9 8.5 %collective-permute-start.1 = (f32[88,128]{1,0:T(8,128)S(1)}, f32[88,128]{1,0:T(8,128)S(1)}, u32[]{:S(2)}, u32[]{:S(2)}) collective-permute-start(f32[88,128]{1,0:T(8,128)S(1)} %get-tuple-element.25), channel_id=1, source_target_pairs={{0,28},{4,8},{8,4},{12,16},{16,12},{20,24},{24,20},{28,0},{1,29},{... | collective-permute-start | bytes 135176 | tf_op jit(solution)/shard_map/ppermute | solution.py:346
  7.1 10.4 %copy-start = (bf16[512,512]{1,0:T(8,128)(2,1)S(1)}, bf16[512,512]{1,0:T(8,128)(2,1)}, u32[]{:S(2)}) copy-start(bf16[512,512]{1,0:T(8,128)(2,1)} %w2_ref.1) | copy-start | bytes 1572868
  7.1 15.3 %collective-permute-start.4 = (bf16[8,4096]{1,0:T(8,128)(2,1)S(1)}, bf16[8,4096]{1,0:T(8,128)(2,1)S(1)}, u32[]{:S(2)}, u32[]{:S(2)}) collective-permute-start(bf16[8,4096]{1,0:T(8,128)(2,1)S(1)} %get-tuple-element.37), channel_id=1, source_target_pairs={{0,1},{1,2},{2,3},{3,0},{4,5},{5,6},{6,7},{7,4},{8,9},{9,10},{10,1... | collective-permute-start | bytes 196616 | tf_op jit(solution)/shard_map/ppermute | solution.py:357
  8.7 13.6 %collective-permute-start.5 = (bf16[8,4096]{1,0:T(8,128)(2,1)S(1)}, bf16[8,4096]{1,0:T(8,128)(2,1)S(1)}, u32[]{:S(2)}, u32[]{:S(2)}) collective-permute-start(bf16[8,4096]{1,0:T(8,128)(2,1)S(1)} %get-tuple-element.38), channel_id=1, source_target_pairs={{0,2},{1,3},{2,0},{3,1},{4,6},{5,7},{6,4},{7,5},{8,10},{9,11},{10,... | collective-permute-start | bytes 196616 | tf_op jit(solution)/shard_map/ppermute | solution.py:357
  11.3 6.2 %copy-start.1 = (bf16[32,512]{1,0:T(8,128)(2,1)S(1)}, bf16[32,512]{1,0:T(8,128)(2,1)}, u32[]{:S(2)}) copy-start(bf16[32,512]{1,0:T(8,128)(2,1)} %w1_ref.1) | copy-start | bytes 98308
  11.5 10.9 %collective-permute-start.6 = (bf16[8,4096]{1,0:T(8,128)(2,1)S(1)}, bf16[8,4096]{1,0:T(8,128)(2,1)S(1)}, u32[]{:S(2)}, u32[]{:S(2)}) collective-permute-start(bf16[8,4096]{1,0:T(8,128)(2,1)S(1)} %get-tuple-element.39), channel_id=1, source_target_pairs={{0,3},{1,0},{2,1},{3,2},{4,7},{5,4},{6,5},{7,6},{8,11},{9,8},{10,9... | collective-permute-start | bytes 196616 | tf_op jit(solution)/shard_map/ppermute | solution.py:357
  12.9 1.4 %collective-permute-start.2 = (f32[8,128]{1,0:T(8,128)S(1)}, f32[8,128]{1,0:T(8,128)S(1)}, u32[]{:S(2)}, u32[]{:S(2)}) collective-permute-start(f32[8,128]{1,0:T(8,128)S(1)} %get-tuple-element.34), channel_id=1, source_target_pairs={{0,4},{4,0},{8,12},{12,8},{16,20},{20,16},{24,28},{28,24},{1,5},{5... | collective-permute-start | bytes 12296 | tf_op jit(solution)/shard_map/ppermute | solution.py:376
  12.9 3.9 %collective-permute-start.3 = (f32[8,128]{1,0:T(8,128)S(1)}, f32[8,128]{1,0:T(8,128)S(1)}, u32[]{:S(2)}, u32[]{:S(2)}) collective-permute-start(f32[8,128]{1,0:T(8,128)S(1)} %get-tuple-element.35), channel_id=1, source_target_pairs={{0,28},{4,8},{8,4},{12,16},{16,12},{20,24},{24,20},{28,0},{1,29},{... | collective-permute-start | bytes 12296 | tf_op jit(solution)/shard_map/ppermute | solution.py:377
  14.3 4.7 %collective-permute-start.7 = (bf16[8,1024]{1,0:T(8,128)(2,1)S(1)}, bf16[8,1024]{1,0:T(8,128)(2,1)S(1)}, u32[]{:S(2)}, u32[]{:S(2)}) collective-permute-start(bf16[8,1024]{1,0:T(8,128)(2,1)S(1)} %get-tuple-element.40), channel_id=1, source_target_pairs={{0,2},{1,3},{2,0},{3,1},{4,6},{5,7},{6,4},{7,5},{8,10},{9,11},{10,... | collective-permute-start | bytes 49160 | tf_op jit(solution)/shard_map/ppermute | solution.py:357
  16.8 5.5 %collective-permute-start.8 = (bf16[8,1024]{1,0:T(8,128)(2,1)S(1)}, bf16[8,1024]{1,0:T(8,128)(2,1)S(1)}, u32[]{:S(2)}, u32[]{:S(2)}) collective-permute-start(bf16[8,1024]{1,0:T(8,128)(2,1)S(1)} %get-tuple-element.41), channel_id=1, source_target_pairs={{0,1},{1,2},{2,3},{3,0},{4,5},{5,6},{6,7},{7,4},{8,9},{9,10},{10,1... | collective-permute-start | bytes 49160 | tf_op jit(solution)/shard_map/ppermute | solution.py:357
  17.5 4.9 %copy-start.2 = (bf16[512,32]{0,1:T(8,128)(2,1)S(1)}, bf16[512,32]{0,1:T(8,128)(2,1)}, u32[]{:S(2)}) copy-start(bf16[512,32]{0,1:T(8,128)(2,1)} %param.11) | copy-start | bytes 98308

commit v4 on v3

--- a/solution.py
+++ b/solution.py
@@ -113,42 +113,30 @@
         write(odd_ref, even_ref)
 
 
-def inner_kernel(dests, length, halves, q_ref, rates_ref, *out_refs):
-    species = out_refs[0].shape[0]
+def inner_kernel(dests, length, halves, q_ref, rates_ref, out_ref):
+    species = out_ref.shape[1]
     share = length // dests
-    me = lax.axis_index("spec")
-    for k in range(dests):
-        first = lax.rem(me + k, dests) * share
-        below = jnp.maximum(first - SUB, 0)
-        above = jnp.minimum(first + share, length - SUB)
+    for dest in range(dests):
+        places = [
+            min(max(dest * share + at, 0), length - 1) for at in range(-BEHIND, share + AHEAD)
+        ]
         for half in range(halves):
-
-            def start(at):
-                if at < 0:
-                    return below * halves + spot(at + SUB, half, halves)
-                if at >= share:
-                    return above * halves + spot(at - share, half, halves)
-                return first * halves + spot(at, half, halves)
-
-            reach = range(-BEHIND, share + AHEAD)
-            rows = [q_ref[pl.ds(start(at), species, stride=length * halves), :] for at in reach]
-            rates = [
-                with_damp(rates_ref[pl.ds(start(at), 1), :], (species, LANES)) for at in reach
-            ]
+            starts = [spot(at, half, halves) for at in places]
+            rows = [q_ref[pl.ds(at, species, stride=length * halves), :] for at in starts]
+            rates = [with_damp(rates_ref[at : at + 1, :], (species, LANES)) for at in starts]
             for at, value in enumerate(two_sweeps(rows, rates)):
                 place = (at * halves + half) * LANES
-                out_refs[k][:, place : place + LANES] = value.astype(jnp.bfloat16)
+                out_ref[dest, :, place : place + LANES] = value.astype(jnp.bfloat16)
 
 
 def edge_kernel(
-    dests, early, late, length, halves, even_ref, odd_ref, hits_ref, q_ref, rates_ref, *refs
+    length, halves, even_ref, odd_ref, hits_ref, q_ref, rates_ref, inner_ref, out_ref,
+    to_even_ref, to_odd_ref, known_ref,
 ):
-    out_refs, refs = refs[len(late) : 2 * len(late)], refs[2 * len(late) :]
-    small_refs, (to_even_ref, to_odd_ref, known_ref) = refs[: len(early)], refs[len(early) :]
-    species, cells = out_refs[0].shape
+    dests, species, cells = out_ref.shape
+    out_ref[...] = inner_ref[...]
     part = BEHIND * species + SUB
     reach = BEHIND + AHEAD
-    me = lax.axis_index("spec")
     even = lax.rem(lax.axis_index("tile"), 2) == 0
     own, from_even, from_odd = hits_ref[...], even_ref[halves * part :, :], odd_ref[halves * part :, :]
     known_ref[...] = own + from_even + from_odd
@@ -189,64 +177,29 @@
                 rates_of(own_rates(length - reach) + [after[j : j + 1] for j in range(AHEAD)]),
             )
         )
-    top = [tops[half][j] for j in range(BEHIND) for half in range(halves)]
-    bottom = [bottoms[half][j] for j in range(AHEAD) for half in range(halves)]
-    for k, small_ref in zip(early, small_refs):
-        low = lax.rem(me + k, dests) == 0
-        skip = len(top) - len(bottom)
-        for j, value in enumerate(top):
-            other = bottom[j - skip] if j >= skip else value
-            small_ref[:, j * LANES : (j + 1) * LANES] = jnp.where(low, value, other).astype(
-                jnp.bfloat16
-            )
-    for k, out_ref in zip(late, out_refs):
-        dest = lax.rem(me + k, dests)
-
-        @pl.when(dest == 0)
-        def _():
-            for j, value in enumerate(top):
-                out_ref[:, j * LANES : (j + 1) * LANES] = value.astype(jnp.bfloat16)
-
-        @pl.when(dest == dests - 1)
-        def _():
-            for j, value in enumerate(bottom):
-                at = cells + (j - len(bottom)) * LANES
-                out_ref[:, at : at + LANES] = value.astype(jnp.bfloat16)
-
-
-def weight_kernel(w1_ref, w2_ref, after_ref, w1_out, w2_out):
+    for half in range(halves):
+        for j, value in enumerate(tops[half]):
+            at = (j * halves + half) * LANES
+            out_ref[0, :, at : at + LANES] = value.astype(jnp.bfloat16)
+        for j, value in enumerate(bottoms[half]):
+            at = cells + ((j - AHEAD) * halves + half) * LANES
+            out_ref[dests - 1, :, at : at + LANES] = value.astype(jnp.bfloat16)
+
+
+def weight_kernel(w1_ref, w2_ref, list_ref, after_ref, w1_out, w2_out, list_out):
+    list_out[...] = list_ref[...]
     w1_out[...] = (0.5 * w1_ref[...].astype(jnp.float32)).T.astype(jnp.bfloat16)
     w2_out[...] = (0.5 * w2_ref[...].astype(jnp.float32)).T.astype(jnp.bfloat16)
 
 
 def chemistry_kernel(
-    groups, early, list_ref, w1_ref, w2_ref, w3_ref, known_ref, even_ref, odd_ref, *refs
+    list_ref, w1_ref, w2_ref, w3_ref, known_ref, even_ref, odd_ref, cells_ref,
+    out_ref, share_ref, state_ref, picked_ref, held_ref, done,
 ):
-    parts, edges, refs = refs[:groups], refs[groups : groups + len(early)], refs[groups + len(early) :]
-    out_ref, share_ref, state_ref, picked_ref, held_ref, done = refs
-    species, cells = state_ref.shape[1:]
+    groups, species, cells = state_ref.shape
     slots = list_ref.shape[0]
     blocks = cells // BLK
-    me = lax.axis_index("spec")
-
-    def source(k):
-        return lax.rem(me - k + groups, groups)
-
-    for k in range(groups):
-        state_ref[source(k)] = parts[k][...]
-    wide = edges[0].shape[1]
-    narrow = wide // BEHIND * AHEAD
-
-    @pl.when(me == 0)
-    def _():
-        for k, edge in zip(early, edges):
-            state_ref[source(k), :, 0:wide] = edge[...]
-
-    @pl.when(me == groups - 1)
-    def _():
-        for k, edge in zip(early, edges):
-            state_ref[source(k), :, cells - narrow :] = edge[:, wide - narrow :]
-
+    state_ref[...] = cells_ref[...]
     hits = known_ref[...] + even_ref[...] + odd_ref[...]
     lane = lax.broadcasted_iota(jnp.int32, hits.shape, 1)
     mine = jnp.where(lane == lax.axis_index("tile"), hits, 0.0)
@@ -313,20 +266,19 @@
     params = pltpu.CompilerParams(vmem_limit_bytes=VMEM_BYTES)
     size = halves * (BEHIND * species + SUB) + SUB
     flag = jax.ShapeDtypeStruct((SUB, LANES), f32)
-    block = jax.ShapeDtypeStruct((species, cells), bf16)
-
-    to_even, to_odd, hits, field, rates, listing = pl.pallas_call(
+
+    to_even, to_odd, hits, field, rates = pl.pallas_call(
         functools.partial(pack_kernel, length, halves, cells // BLK),
         out_shape=[jax.ShapeDtypeStruct((size, LANES), f32)] * 2
         + [
             flag,
             jax.ShapeDtypeStruct((species * length * halves, LANES), f32),
             jax.ShapeDtypeStruct((length * halves, LANES), f32),
-            jax.ShapeDtypeStruct((slots,), jnp.int32),
         ],
         in_specs=[anywhere()] * 4,
-        out_specs=[vmem()] * 5 + [pl.BlockSpec(memory_space=pltpu.SMEM)],
+        out_specs=[vmem()] * 5,
         scratch_shapes=[
+            pltpu.SMEM((slots,), jnp.int32),
             pltpu.SMEM((slots,), jnp.int32),
             pltpu.SemaphoreType.DMA((4,)),
         ],
@@ -344,53 +296,42 @@
     odds = [(t, other % tiles) for t, other in odds]
     from_even = lax.ppermute(to_even, "tile", evens)
     from_odd = lax.ppermute(to_odd, "tile", odds)
-    blocks = pl.pallas_call(
+    every = jax.ShapeDtypeStruct((dests, species, cells), bf16)
+    inner = pl.pallas_call(
         functools.partial(inner_kernel, dests, length, halves),
-        out_shape=[block] * dests,
+        out_shape=every,
         in_specs=[vmem()] * 2,
-        out_specs=[vmem()] * dests,
+        out_specs=vmem(),
         compiler_params=params,
         cost_estimate=cost(1.0),
         name="inner_rows",
     )(field, rates)
-    def ring(k, x):
-        return lax.ppermute(x, "spec", [(s, (s + k) % dests) for s in range(dests)])
-
-    order = [k for k in (2, 1) if k < dests] + list(range(3, dests))
-    early, late = order[: dests // 2], [0] + order[dests // 2 :]
-    received = {k: ring(k, blocks[k]) for k in early}
-    edge = jax.ShapeDtypeStruct((species, BEHIND * cols), bf16)
-    outs = pl.pallas_call(
-        functools.partial(edge_kernel, dests, early, late, length, halves),
-        out_shape=[block] * len(late) + [edge] * len(early) + [flag] * 3,
-        in_specs=[vmem()] * (5 + len(late)),
-        out_specs=[vmem()] * (dests + 3),
-        input_output_aliases={5 + i: i for i in range(len(late))},
+    swept, to_even, to_odd, known = pl.pallas_call(
+        functools.partial(edge_kernel, length, halves),
+        out_shape=[every] + [flag] * 3,
+        in_specs=[vmem()] * 6,
+        out_specs=[vmem()] * 4,
         compiler_params=params,
         cost_estimate=cost(0.1),
         name="edge_rows",
-    )(from_even, from_odd, hits, field, rates, *[blocks[k] for k in late])
-    full, edges, (to_even, to_odd, known) = outs[: len(late)], outs[len(late) : dests], outs[dests:]
-    received |= {k: ring(k, x) if k else x for k, x in zip(late, full)}
-    edges = [ring(k, x) for k, x in zip(early, edges)]
+    )(from_even, from_odd, hits, field, rates, inner)
+    gathered = lax.all_to_all(swept, "spec", split_axis=0, concat_axis=0, tiled=True)
     from_even = lax.ppermute(to_even, "tile", evens)
     from_odd = lax.ppermute(to_odd, "tile", odds)
-    w1, w2 = pl.pallas_call(
+    w1, w2, listing = pl.pallas_call(
         weight_kernel,
-        out_shape=[jax.ShapeDtypeStruct(w.shape[::-1], bf16) for w in (first_weight, middle_weight)],
-        in_specs=[vmem(), vmem(), anywhere()],
-        out_specs=[vmem()] * 2,
+        out_shape=[jax.ShapeDtypeStruct(w.shape[::-1], bf16) for w in (first_weight, middle_weight)]
+        + [jax.ShapeDtypeStruct((1, slots), jnp.int32)],
+        in_specs=[vmem()] * 3 + [anywhere()],
+        out_specs=[vmem()] * 3,
         compiler_params=params,
         cost_estimate=cost(0.5),
         name="halved_weights",
-    )(first_weight, middle_weight, known)
+    )(first_weight, middle_weight, active_blocks.reshape(1, slots), known)
     out, load_share = pl.pallas_call(
-        functools.partial(chemistry_kernel, dests, early),
-        out_shape=[
-            jax.ShapeDtypeStruct((dests, species, cells), bf16),
-            jax.ShapeDtypeStruct((1, 1), f32),
-        ],
-        in_specs=[pl.BlockSpec(memory_space=pltpu.SMEM)] + [vmem()] * (6 + dests + len(early)),
+        chemistry_kernel,
+        out_shape=[every, jax.ShapeDtypeStruct((1, 1), f32)],
+        in_specs=[pl.BlockSpec(memory_space=pltpu.SMEM)] + [vmem()] * 7,
         out_specs=[anywhere()] * 2,
         scratch_shapes=[
             pltpu.VMEM((dests, species, cells), bf16),
@@ -402,15 +343,14 @@
         cost_estimate=cost(4.0),
         name="chemistry",
     )(
-        listing,
+        listing.reshape(-1),
         w1,
         w2,
         last_weight.T,
         known,
         from_even,
         from_odd,
-        *[received[k] for k in range(dests)],
-        *edges,
+        gathered,
     )
     return out.reshape(dests * species, cells), load_share
 

time: 26.6 us -> 27 us (1.015)
  local copies, waits for them, and re-layouts: 0.01 us -> 0.66 us
  starting transfers between devices: 11.9 us -> 11.4 us
    ppermute x5 -> x0, starting transfers between devices: 6.37 us -> none  [ring(): return lax.ppermute(x, 'spec', [(s, (s + k) % dests) for s in range(dests)])]
    all_to_all x0 -> x1, starting transfers between devices: none -> 5.16 us  [shards(): lax.all_to_all(swept, 'spec', split_axis=0, concat_axis=0, tiled=True)]
    all_to_all x0 -> x1, waiting for transfers between devices: none -> 5.11 us  [shards(): lax.all_to_all(swept, 'spec', split_axis=0, concat_axis=0, tiled=True)]
    ppermute x5 -> x0, waiting for transfers between devices: 4.61 us -> none  [ring(): return lax.ppermute(x, 'spec', [(s, (s + k) % dests) for s in range(dests)])]
    ppermute x2, starting transfers between devices: 4.98 us -> 5.76 us  [shards(): from_odd = lax.ppermute(to_odd, 'tile', odds)]
    pallas_call x2, Pallas kernels: 4.22 us -> 4.91 us  [the longest x1 4.08 us: shards(): pl.pallas_call(chemistry_kernel, out_shape=[every, jax.ShapeDtypeStruct((...]
    unnamed x6 -> x8, local copies, waits for them, and re-layouts: 0.01 us -> 0.66 us
    pallas_call x1, Pallas kernels: 1.7 us -> 1.11 us  [shards(): pl.pallas_call(functools.partial(pack_kernel, length, halves, cells // BL...]
  transfers between devices with their start and end apart: 9 -> 5, of which waited for: 3 -> 3; matrix products, arithmetic and copies ran while one was open for 0% -> 0% of each run, Pallas kernels for 4% -> 3%
where the time goes in v4:
time: 27 us; the launch traced here: 26.7 us
  starting transfers between devices  11.4 us (42%)
  waiting for transfers between devices  7 us (26%)
  Pallas kernels  6.91 us (26%)
  between operations  0.67 us (2%)
  local copies, waits for them, and re-layouts  0.66 us (2%)
    ppermute x2, starting transfers between devices, shards(): from_odd = lax.ppermute(to_odd, 'tile', odds)  5.76 us
    all_to_all x1, starting transfers between devices, shards(): lax.all_to_all(swept, 'spec', split_axis=0, concat_axis=0, tiled=True)  5.16 us
    all_to_all x1, waiting for transfers between devices, shards(): lax.all_to_all(swept, 'spec', split_axis=0, concat_axis=0, tiled=True)  5.11 us
    pallas_call x1, Pallas kernels, shards(): pl.pallas_call(chemistry_kernel, out_shape=[every, jax.ShapeDtypeStruct((...  4.08 us
    ppermute x2, waiting for transfers between devices, shards(): from_odd = lax.ppermute(to_odd, 'tile', odds)  1.88 us
    pallas_call x1, Pallas kernels, shards(): pl.pallas_call(functools.partial(pack_kernel, length, halves, cells // BL...  1.11 us
    pallas_call x1, Pallas kernels, shards(): pl.pallas_call(functools.partial(edge_kernel, length, halves), out_shape=...  0.84 us
    unnamed x8, local copies, waits for them, and re-layouts  0.66 us
  transfers between devices with their start and end apart: 5, of which 3 were waited for; matrix products, arithmetic and copies ran while one was open for 0% of the time, Pallas kernels for 3%

profile of v4, /device:TPU:0, one launch (start us, length us, event | category | flops | bytes accessed | tf_op | source)
XLA Modules:
  0.0 26.7 jit_solution(5557078561261941908)
XLA Ops:
  0.6 1.1 %pack_edges.1 = (f32[88,128]{1,0:T(8,128)S(1)}, f32[88,128]{1,0:T(8,128)S(1)}, f32[8,128]{1,0:T(8,128)S(1)}, f32[1024,128]{1,0:T(8,128)S(1)}, f32[128,128]{1,0:T(8,128)S(1)}) custom-call(f32[1024,128]{1,0:T(8,128)} %bitcast.20, f32[128,128]{1,0:T(8,128)} %bitcast.21, s32[16]{0:T(128)} %bitcast.17, s32[16]{0:T(128)} %bitcast.22), custom_call_target="tpu_custom_call" | custom-call | flops 1000000000 | bytes 3000000 | tf_op jit(solution)/shard_map/pack_edges/pallas_call | solution.py:270
  1.8 0.5 %collective-permute-start = (f32[88,128]{1,0:T(8,128)S(1)}, f32[88,128]{1,0:T(8,128)S(1)}, u32[]{:S(2)}, u32[]{:S(2)}) collective-permute-start(f32[88,128]{1,0:T(8,128)S(1)} %get-tuple-element.16), channel_id=1, source_target_pairs={{0,4},{4,0},{8,12},{12,8},{16,20},{20,16},{24,28},{28,24},{1,5},{5... | collective-permute-start | bytes 135176 | tf_op jit(solution)/shard_map/ppermute | solution.py:297
  2.3 3.6 %collective-permute-start.1 = (f32[88,128]{1,0:T(8,128)S(1)}, f32[88,128]{1,0:T(8,128)S(1)}, u32[]{:S(2)}, u32[]{:S(2)}) collective-permute-start(f32[88,128]{1,0:T(8,128)S(1)} %get-tuple-element.17), channel_id=1, source_target_pairs={{0,28},{4,8},{8,4},{12,16},{16,12},{20,24},{24,20},{28,0},{1,29},{... | collective-permute-start | bytes 135176 | tf_op jit(solution)/shard_map/ppermute | solution.py:298
  5.8 0.6 %inner_rows.1.inner_ref = bf16[4,8,4096]{2,1,0:T(8,128)(2,1)S(1)} custom-call(f32[1024,128]{1,0:T(8,128)S(1)} %get-tuple-element.19.q_ref, f32[128,128]{1,0:T(8,128)S(1)} %get-tuple-element.20.rates_ref), custom_call_target="tpu_custom_call" | custom-call | flops 1000000000 | bytes 3000000 | tf_op jit(solution)/shard_map/inner_rows/pallas_call | solution.py:300
  6.5 0.0 collective-permute-done.even_ref
  6.5 1.1 %collective-permute-done.1.odd_ref = f32[88,128]{1,0:T(8,128)S(1)} collective-permute-done((f32[88,128]{1,0:T(8,128)S(1)}, f32[88,128]{1,0:T(8,128)S(1)}, u32[]{:S(2)}, u32[]{:S(2)}) %collective-permute-start.1) | collective-permute-done | bytes 45088 | tf_op jit(solution)/shard_map/ppermute | solution.py:298
  7.6 0.0 copy-start
  7.6 0.8 %edge_rows.1 = (bf16[4,8,4096]{2,1,0:T(8,128)(2,1)}, f32[8,128]{1,0:T(8,128)S(1)}, f32[8,128]{1,0:T(8,128)S(1)}, f32[8,128]{1,0:T(8,128)S(1)}) custom-call(f32[88,128]{1,0:T(8,128)S(1)} %collective-permute-done.even_ref, f32[88,128]{1,0:T(8,128)S(1)} %collective-permute-done.1.odd_ref, f32[8,128]{1,0:T(8,128)S(1)} %get-tuple-element.18.hits_ref, ...), custom_call_target="tpu_custom_call" | custom-call | flops 100000000 | bytes 300000 | tf_op jit(solution)/shard_map/edge_rows/pallas_call | solution.py:309
  8.4 0.0 copy-start.1
  8.4 5.2 %all-to-all-start = ((bf16[4,8,4096]{2,1,0:T(8,128)(2,1)}), bf16[4,8,4096]{2,1,0:T(8,128)(2,1)S(1)}, u32[]{:S(2)}, u32[]{:S(2)}) async-start(bf16[4,8,4096]{2,1,0:T(8,128)(2,1)} %get-tuple-element.27), calls=%async_computation | async-start | bytes 524288 | tf_op jit(solution)/shard_map/all_to_all | solution.py:318
  13.6 0.0 collective-permute-start.2
  13.6 2.2 %collective-permute-start.3 = (f32[8,128]{1,0:T(8,128)S(1)}, f32[8,128]{1,0:T(8,128)S(1)}, u32[]{:S(2)}, u32[]{:S(2)}) collective-permute-start(f32[8,128]{1,0:T(8,128)S(1)} %get-tuple-element.26), channel_id=1, source_target_pairs={{0,28},{4,8},{8,4},{12,16},{16,12},{20,24},{24,20},{28,0},{1,29},{... | collective-permute-start | bytes 12296 | tf_op jit(solution)/shard_map/ppermute | solution.py:320
  15.8 0.0 copy-start.3
  15.8 0.0 copy-done
  15.8 0.0 copy-done.1
  15.8 0.6 %copy-done.3 = s32[1,1,16]{2,1,0:T(1,128)S(1)} copy-done((s32[1,1,16]{2,1,0:T(1,128)S(1)}, s32[1,1,16]{2,1,0:T(1,128)}, u32[]{:S(2)}) %copy-start.3) | copy-done | bytes 88
  16.4 0.0 copy-start.2
  16.4 0.2 halved_weights.1
  16.7 0.0 collective-permute-done.2.even_ref
  16.7 0.8 %collective-permute-done.3.odd_ref = f32[8,128]{1,0:T(8,128)S(1)} collective-permute-done((f32[8,128]{1,0:T(8,128)S(1)}, f32[8,128]{1,0:T(8,128)S(1)}, u32[]{:S(2)}, u32[]{:S(2)}) %collective-permute-start.3) | collective-permute-done | bytes 4128 | tf_op jit(solution)/shard_map/ppermute | solution.py:320
  17.5 5.1 %all-to-all-done.cells_ref = bf16[4,8,4096]{2,1,0:T(8,128)(2,1)S(1)} async-done(((bf16[4,8,4096]{2,1,0:T(8,128)(2,1)}), bf16[4,8,4096]{2,1,0:T(8,128)(2,1)S(1)}, u32[]{:S(2)}, u32[]{:S(2)}) %all-to-all-start) | async-done | bytes 262176 | tf_op jit(solution)/shard_map/all_to_all | solution.py:318
  22.6 0.0 copy-done.2
  22.6 4.1 %chemistry.1 = (bf16[4,8,4096]{2,1,0:T(8,128)(2,1)}, f32[1,1]{1,0:T(1,128)}) custom-call(s32[16]{0:T(128)S(1)} %bitcast.19, bf16[512,32]{1,0:T(8,128)(2,1)S(1)} %get-tuple-element.23.w1_ref, bf16[512,512]{1,0:T(8,128)(2,1)S(1)} %get-tuple-element.24.w2_ref, bf16[32,512]{1,0:T(8,128)(2,1)S(1)} %bitcast.16, ...), custom_call_target="tpu_custom_call" | custom-call | flops 4000000000 | bytes 12000000 | tf_op jit(solution)/shard_map/chemistry/pallas_call | solution.py:331
Async XLA Ops:
  1.8 4.7 %collective-permute-start = (f32[88,128]{1,0:T(8,128)S(1)}, f32[88,128]{1,0:T(8,128)S(1)}, u32[]{:S(2)}, u32[]{:S(2)}) collective-permute-start(f32[88,128]{1,0:T(8,128)S(1)} %get-tuple-element.16), channel_id=1, source_target_pairs={{0,4},{4,0},{8,12},{12,8},{16,20},{20,16},{24,28},{28,24},{1,5},{5... | collective-permute-start | bytes 135176 | tf_op jit(solution)/shard_map/ppermute | solution.py:297
  2.3 5.3 %collective-permute-start.1 = (f32[88,128]{1,0:T(8,128)S(1)}, f32[88,128]{1,0:T(8,128)S(1)}, u32[]{:S(2)}, u32[]{:S(2)}) collective-permute-start(f32[88,128]{1,0:T(8,128)S(1)} %get-tuple-element.17), channel_id=1, source_target_pairs={{0,28},{4,8},{8,4},{12,16},{16,12},{20,24},{24,20},{28,0},{1,29},{... | collective-permute-start | bytes 135176 | tf_op jit(solution)/shard_map/ppermute | solution.py:298
  7.6 8.2 %copy-start = (bf16[512,512]{1,0:T(8,128)(2,1)S(1)}, bf16[512,512]{1,0:T(8,128)(2,1)}, u32[]{:S(2)}) copy-start(bf16[512,512]{1,0:T(8,128)(2,1)} %w2_ref.1) | copy-start | bytes 1572868
  8.4 7.4 %copy-start.1 = (bf16[32,512]{1,0:T(8,128)(2,1)S(1)}, bf16[32,512]{1,0:T(8,128)(2,1)}, u32[]{:S(2)}) copy-start(bf16[32,512]{1,0:T(8,128)(2,1)} %w1_ref.1) | copy-start | bytes 98308
  8.4 14.2 %all-to-all-start = ((bf16[4,8,4096]{2,1,0:T(8,128)(2,1)}), bf16[4,8,4096]{2,1,0:T(8,128)(2,1)S(1)}, u32[]{:S(2)}, u32[]{:S(2)}) async-start(bf16[4,8,4096]{2,1,0:T(8,128)(2,1)} %get-tuple-element.27), calls=%async_computation | async-start | bytes 524288 | tf_op jit(solution)/shard_map/all_to_all | solution.py:318
  13.6 3.1 %collective-permute-start.2 = (f32[8,128]{1,0:T(8,128)S(1)}, f32[8,128]{1,0:T(8,128)S(1)}, u32[]{:S(2)}, u32[]{:S(2)}) collective-permute-start(f32[8,128]{1,0:T(8,128)S(1)} %get-tuple-element.25), channel_id=1, source_target_pairs={{0,4},{4,0},{8,12},{12,8},{16,20},{20,16},{24,28},{28,24},{1,5},{5... | collective-permute-start | bytes 12296 | tf_op jit(solution)/shard_map/ppermute | solution.py:319
  13.6 3.9 %collective-permute-start.3 = (f32[8,128]{1,0:T(8,128)S(1)}, f32[8,128]{1,0:T(8,128)S(1)}, u32[]{:S(2)}, u32[]{:S(2)}) collective-permute-start(f32[8,128]{1,0:T(8,128)S(1)} %get-tuple-element.26), channel_id=1, source_target_pairs={{0,28},{4,8},{8,4},{12,16},{16,12},{20,24},{24,20},{28,0},{1,29},{... | collective-permute-start | bytes 12296 | tf_op jit(solution)/shard_map/ppermute | solution.py:320
  15.8 0.7 %copy-start.3 = (s32[1,1,16]{2,1,0:T(1,128)S(1)}, s32[1,1,16]{2,1,0:T(1,128)}, u32[]{:S(2)}) copy-start(s32[1,1,16]{2,1,0:T(1,128)} %param.12) | copy-start | bytes 196
  16.4 6.2 %copy-start.2 = (bf16[512,32]{0,1:T(8,128)(2,1)S(1)}, bf16[512,32]{0,1:T(8,128)(2,1)}, u32[]{:S(2)}) copy-start(bf16[512,32]{0,1:T(8,128)(2,1)} %param.11) | copy-start | bytes 98308

commit v5 on v4

--- a/solution.py
+++ b/solution.py
@@ -113,28 +113,41 @@
         write(odd_ref, even_ref)
 
 
-def inner_kernel(dests, length, halves, q_ref, rates_ref, out_ref):
-    species = out_ref.shape[1]
+def inner_kernel(dests, length, halves, q_ref, rates_ref, *out_refs):
+    species = out_refs[0].shape[0]
     share = length // dests
-    for dest in range(dests):
-        places = [
-            min(max(dest * share + at, 0), length - 1) for at in range(-BEHIND, share + AHEAD)
-        ]
+    me = lax.axis_index("spec")
+    for k in range(dests):
+        first = lax.rem(me + k, dests) * share
+        below = jnp.maximum(first - SUB, 0)
+        above = jnp.minimum(first + share, length - SUB)
         for half in range(halves):
-            starts = [spot(at, half, halves) for at in places]
-            rows = [q_ref[pl.ds(at, species, stride=length * halves), :] for at in starts]
-            rates = [with_damp(rates_ref[at : at + 1, :], (species, LANES)) for at in starts]
+
+            def start(at):
+                if at < 0:
+                    return below * halves + spot(at + SUB, half, halves)
+                if at >= share:
+                    return above * halves + spot(at - share, half, halves)
+                return first * halves + spot(at, half, halves)
+
+            reach = range(-BEHIND, share + AHEAD)
+            rows = [q_ref[pl.ds(start(at), species, stride=length * halves), :] for at in reach]
+            rates = [
+                with_damp(rates_ref[pl.ds(start(at), 1), :], (species, LANES)) for at in reach
+            ]
             for at, value in enumerate(two_sweeps(rows, rates)):
                 place = (at * halves + half) * LANES
-                out_ref[dest, :, place : place + LANES] = value.astype(jnp.bfloat16)
+                out_refs[k][:, place : place + LANES] = value.astype(jnp.bfloat16)
 
 
 def edge_kernel(
-    length, halves, even_ref, odd_ref, hits_ref, q_ref, rates_ref, inner_ref, out_ref,
-    to_even_ref, to_odd_ref, known_ref,
+    dests, length, halves, odd_ref, even_ref, hits_ref, q_ref, rates_ref, *refs
 ):
-    dests, species, cells = out_ref.shape
-    out_ref[...] = inner_ref[...]
+    in_refs, out_refs, (to_even_ref, to_odd_ref, known_ref) = (
+        refs[:dests], refs[dests : 2 * dests], refs[2 * dests :]
+    )
+    species, cells = out_refs[0].shape
+    me = lax.axis_index("spec")
     part = BEHIND * species + SUB
     reach = BEHIND + AHEAD
     even = lax.rem(lax.axis_index("tile"), 2) == 0
@@ -177,13 +190,23 @@
                 rates_of(own_rates(length - reach) + [after[j : j + 1] for j in range(AHEAD)]),
             )
         )
-    for half in range(halves):
-        for j, value in enumerate(tops[half]):
-            at = (j * halves + half) * LANES
-            out_ref[0, :, at : at + LANES] = value.astype(jnp.bfloat16)
-        for j, value in enumerate(bottoms[half]):
-            at = cells + ((j - AHEAD) * halves + half) * LANES
-            out_ref[dests - 1, :, at : at + LANES] = value.astype(jnp.bfloat16)
+    for k, (in_ref, out_ref) in enumerate(zip(in_refs, out_refs)):
+        dest = lax.rem(me + k, dests)
+        out_ref[...] = in_ref[...]
+
+        @pl.when(dest == 0)
+        def _():
+            for half in range(halves):
+                for j, value in enumerate(tops[half]):
+                    at = (j * halves + half) * LANES
+                    out_ref[:, at : at + LANES] = value.astype(jnp.bfloat16)
+
+        @pl.when(dest == dests - 1)
+        def _():
+            for half in range(halves):
+                for j, value in enumerate(bottoms[half]):
+                    at = cells + ((j - AHEAD) * halves + half) * LANES
+                    out_ref[:, at : at + LANES] = value.astype(jnp.bfloat16)
 
 
 def weight_kernel(w1_ref, w2_ref, list_ref, after_ref, w1_out, w2_out, list_out):
@@ -193,13 +216,15 @@
 
 
 def chemistry_kernel(
-    list_ref, w1_ref, w2_ref, w3_ref, known_ref, even_ref, odd_ref, cells_ref,
-    out_ref, share_ref, state_ref, picked_ref, held_ref, done,
+    groups, list_ref, w1_ref, w2_ref, w3_ref, known_ref, odd_ref, even_ref, *refs
 ):
-    groups, species, cells = state_ref.shape
+    parts, (out_ref, share_ref, state_ref, picked_ref, held_ref, done) = refs[:groups], refs[groups:]
+    species, cells = state_ref.shape[1:]
     slots = list_ref.shape[0]
     blocks = cells // BLK
-    state_ref[...] = cells_ref[...]
+    me = lax.axis_index("spec")
+    for k in range(groups):
+        state_ref[lax.rem(me - k + groups, groups)] = parts[k][...]
     hits = known_ref[...] + even_ref[...] + odd_ref[...]
     lane = lax.broadcasted_iota(jnp.int32, hits.shape, 1)
     mine = jnp.where(lane == lax.axis_index("tile"), hits, 0.0)
@@ -294,30 +319,33 @@
     evens = [(t, t ^ 1) for t in range(tiles)]
     odds = [(t, ((t + 1) ^ 1) - 1) for t in range(tiles)]
     odds = [(t, other % tiles) for t, other in odds]
+    from_odd = lax.ppermute(to_odd, "tile", odds)
     from_even = lax.ppermute(to_even, "tile", evens)
-    from_odd = lax.ppermute(to_odd, "tile", odds)
-    every = jax.ShapeDtypeStruct((dests, species, cells), bf16)
-    inner = pl.pallas_call(
+    block = jax.ShapeDtypeStruct((species, cells), bf16)
+    blocks = pl.pallas_call(
         functools.partial(inner_kernel, dests, length, halves),
-        out_shape=every,
+        out_shape=[block] * dests,
         in_specs=[vmem()] * 2,
-        out_specs=vmem(),
+        out_specs=[vmem()] * dests,
         compiler_params=params,
         cost_estimate=cost(1.0),
         name="inner_rows",
     )(field, rates)
-    swept, to_even, to_odd, known = pl.pallas_call(
-        functools.partial(edge_kernel, length, halves),
-        out_shape=[every] + [flag] * 3,
-        in_specs=[vmem()] * 6,
-        out_specs=[vmem()] * 4,
+    *blocks, to_even, to_odd, known = pl.pallas_call(
+        functools.partial(edge_kernel, dests, length, halves),
+        out_shape=[block] * dests + [flag] * 3,
+        in_specs=[vmem()] * (5 + dests),
+        out_specs=[vmem()] * (dests + 3),
         compiler_params=params,
         cost_estimate=cost(0.1),
         name="edge_rows",
-    )(from_even, from_odd, hits, field, rates, inner)
-    gathered = lax.all_to_all(swept, "spec", split_axis=0, concat_axis=0, tiled=True)
+    )(from_odd, from_even, hits, field, rates, *blocks)
+    received = [blocks[0]] + [
+        lax.ppermute(blocks[k], "spec", [(s, (s + k) % dests) for s in range(dests)])
+        for k in range(1, dests)
+    ]
+    from_odd = lax.ppermute(to_odd, "tile", odds)
     from_even = lax.ppermute(to_even, "tile", evens)
-    from_odd = lax.ppermute(to_odd, "tile", odds)
     w1, w2, listing = pl.pallas_call(
         weight_kernel,
         out_shape=[jax.ShapeDtypeStruct(w.shape[::-1], bf16) for w in (first_weight, middle_weight)]
@@ -329,9 +357,12 @@
         name="halved_weights",
     )(first_weight, middle_weight, active_blocks.reshape(1, slots), known)
     out, load_share = pl.pallas_call(
-        chemistry_kernel,
-        out_shape=[every, jax.ShapeDtypeStruct((1, 1), f32)],
-        in_specs=[pl.BlockSpec(memory_space=pltpu.SMEM)] + [vmem()] * 7,
+        functools.partial(chemistry_kernel, dests),
+        out_shape=[
+            jax.ShapeDtypeStruct((dests, species, cells), bf16),
+            jax.ShapeDtypeStruct((1, 1), f32),
+        ],
+        in_specs=[pl.BlockSpec(memory_space=pltpu.SMEM)] + [vmem()] * (6 + dests),
         out_specs=[anywhere()] * 2,
         scratch_shapes=[
             pltpu.VMEM((dests, species, cells), bf16),
@@ -348,9 +379,9 @@
         w2,
         last_weight.T,
         known,
+        from_odd,
         from_even,
-        from_odd,
-        gathered,
+        *received,
     )
     return out.reshape(dests * species, cells), load_share
 

time: 27 us -> 21.9 us (0.81)
  waiting for transfers between devices: 7 us -> 3.4 us
  Pallas kernels: 6.91 us -> 6.24 us
  starting transfers between devices: 11.4 us -> 10.8 us
    ppermute x0 -> x3, starting transfers between devices: none -> 6.7 us  [shards(): lax.ppermute(blocks[k], 'spec', [(s, (s + k) % dests) for s in range(dest...]
    all_to_all x1 -> x0, starting transfers between devices: 5.16 us -> none  [shards(): lax.all_to_all(swept, 'spec', split_axis=0, concat_axis=0, tiled=True)]
    all_to_all x1 -> x0, waiting for transfers between devices: 5.11 us -> none  [shards(): lax.all_to_all(swept, 'spec', split_axis=0, concat_axis=0, tiled=True)]
    ppermute x2, starting transfers between devices: 5.76 us -> 4.07 us  [shards(): from_odd = lax.ppermute(to_odd, 'tile', odds)]
    ppermute x2, waiting for transfers between devices: 1.88 us -> 3.39 us  [shards(): from_odd = lax.ppermute(to_odd, 'tile', odds)]
    pallas_call x2, Pallas kernels: 4.91 us -> 4.21 us  [the longest x1 4.06 us: shards(): pl.pallas_call(functools.partial(chemistry_kernel, dests), out_shape=[jax...]
    ppermute x2, starting transfers between devices: 0.52 us -> 0.01 us  [shards(): from_even = lax.ppermute(to_even, 'tile', evens)]
  transfers between devices with their start and end apart: 5 -> 7, of which waited for: 3 -> 2; matrix products, arithmetic and copies ran while one was open for 0% -> 0% of each run, Pallas kernels for 3% -> 4%
where the time goes in v5:
time: 21.9 us; the launch traced here: 21.8 us
  starting transfers between devices  10.8 us (49%)
  Pallas kernels  6.24 us (28%)
  waiting for transfers between devices  3.4 us (16%)
  between operations  0.7 us (3%)
  local copies, waits for them, and re-layouts  0.66 us (3%)
    ppermute x3, starting transfers between devices, shards(): lax.ppermute(blocks[k], 'spec', [(s, (s + k) % dests) for s in range(dest...  6.7 us
    ppermute x2, starting transfers between devices, shards(): from_odd = lax.ppermute(to_odd, 'tile', odds)  4.07 us
    pallas_call x1, Pallas kernels, shards(): pl.pallas_call(functools.partial(chemistry_kernel, dests), out_shape=[jax...  4.06 us
    ppermute x2, waiting for transfers between devices, shards(): from_odd = lax.ppermute(to_odd, 'tile', odds)  3.39 us
    pallas_call x1, Pallas kernels, shards(): pl.pallas_call(functools.partial(pack_kernel, length, halves, cells // BL...  1.11 us
    pallas_call x1, Pallas kernels, shards(): pl.pallas_call(functools.partial(inner_kernel, dests, length, halves), ou...  0.67 us
    unnamed x8, local copies, waits for them, and re-layouts  0.66 us
  transfers between devices with their start and end apart: 7, of which 2 were waited for; matrix products, arithmetic and copies ran while one was open for 0% of the time, Pallas kernels for 4%

profile of v5, /device:TPU:0, one launch (start us, length us, event | category | flops | bytes accessed | tf_op | source)
XLA Modules:
  0.0 21.8 jit_solution(4815425847485160521)
XLA Ops:
  0.6 1.1 %pack_edges.1 = (f32[88,128]{1,0:T(8,128)S(1)}, f32[88,128]{1,0:T(8,128)S(1)}, f32[8,128]{1,0:T(8,128)S(1)}, f32[1024,128]{1,0:T(8,128)S(1)}, f32[128,128]{1,0:T(8,128)S(1)}) custom-call(f32[1024,128]{1,0:T(8,128)} %bitcast.20, f32[128,128]{1,0:T(8,128)} %bitcast.21, s32[16]{0:T(128)} %bitcast.17, s32[16]{0:T(128)} %bitcast.22), custom_call_target="tpu_custom_call" | custom-call | flops 1000000000 | bytes 3000000 | tf_op jit(solution)/shard_map/pack_edges/pallas_call | solution.py:295
  1.8 3.4 %collective-permute-start = (f32[88,128]{1,0:T(8,128)S(1)}, f32[88,128]{1,0:T(8,128)S(1)}, u32[]{:S(2)}, u32[]{:S(2)}) collective-permute-start(f32[88,128]{1,0:T(8,128)S(1)} %get-tuple-element.23), channel_id=1, source_target_pairs={{0,28},{4,8},{8,4},{12,16},{16,12},{20,24},{24,20},{28,0},{1,29},{... | collective-permute-start | bytes 135176 | tf_op jit(solution)/shard_map/ppermute | solution.py:322
  5.1 0.0 collective-permute-start.1
  5.2 0.7 %inner_rows.1 = (bf16[8,4096]{1,0:T(8,128)(2,1)S(1)}, bf16[8,4096]{1,0:T(8,128)(2,1)S(1)}, bf16[8,4096]{1,0:T(8,128)(2,1)S(1)}, bf16[8,4096]{1,0:T(8,128)(2,1)S(1)}) custom-call(f32[1024,128]{1,0:T(8,128)S(1)} %get-tuple-element.26.q_ref, f32[128,128]{1,0:T(8,128)S(1)} %get-tuple-element.27.rates_ref), custom_call_target="tpu_custom_call" | custom-call | flops 1000000000 | bytes 3000000 | tf_op jit(solution)/shard_map/inner_rows/pallas_call | solution.py:325
  5.8 0.0 copy-start
  5.8 1.0 %collective-permute-done.odd_ref = f32[88,128]{1,0:T(8,128)S(1)} collective-permute-done((f32[88,128]{1,0:T(8,128)S(1)}, f32[88,128]{1,0:T(8,128)S(1)}, u32[]{:S(2)}, u32[]{:S(2)}) %collective-permute-start) | collective-permute-done | bytes 45088 | tf_op jit(solution)/shard_map/ppermute | solution.py:322
  6.9 0.0 collective-permute-done.1.even_ref
  6.9 0.0 copy-start.1
  6.9 0.2 edge_rows.1
  7.1 2.8 %collective-permute-start.4 = (bf16[8,4096]{1,0:T(8,128)(2,1)S(1)}, bf16[8,4096]{1,0:T(8,128)(2,1)S(1)}, u32[]{:S(2)}, u32[]{:S(2)}) collective-permute-start(bf16[8,4096]{1,0:T(8,128)(2,1)S(1)} %get-tuple-element.39), channel_id=1, source_target_pairs={{0,1},{1,2},{2,3},{3,0},{4,5},{5,6},{6,7},{7,4},{8,9},{9,10},{10,1... | collective-permute-start | bytes 196616 | tf_op jit(solution)/shard_map/ppermute | solution.py:344
  9.8 2.6 %collective-permute-start.5 = (bf16[8,4096]{1,0:T(8,128)(2,1)S(1)}, bf16[8,4096]{1,0:T(8,128)(2,1)S(1)}, u32[]{:S(2)}, u32[]{:S(2)}) collective-permute-start(bf16[8,4096]{1,0:T(8,128)(2,1)S(1)} %get-tuple-element.40), channel_id=1, source_target_pairs={{0,2},{1,3},{2,0},{3,1},{4,6},{5,7},{6,4},{7,5},{8,10},{9,11},{10,... | collective-permute-start | bytes 196616 | tf_op jit(solution)/shard_map/ppermute | solution.py:344
  12.4 1.3 %collective-permute-start.6 = (bf16[8,4096]{1,0:T(8,128)(2,1)S(1)}, bf16[8,4096]{1,0:T(8,128)(2,1)S(1)}, u32[]{:S(2)}, u32[]{:S(2)}) collective-permute-start(bf16[8,4096]{1,0:T(8,128)(2,1)S(1)} %get-tuple-element.41), channel_id=1, source_target_pairs={{0,3},{1,0},{2,1},{3,2},{4,7},{5,4},{6,5},{7,6},{8,11},{9,8},{10,9... | collective-permute-start | bytes 196616 | tf_op jit(solution)/shard_map/ppermute | solution.py:344
  13.7 0.7 %collective-permute-start.2 = (f32[8,128]{1,0:T(8,128)S(1)}, f32[8,128]{1,0:T(8,128)S(1)}, u32[]{:S(2)}, u32[]{:S(2)}) collective-permute-start(f32[8,128]{1,0:T(8,128)S(1)} %get-tuple-element.36), channel_id=1, source_target_pairs={{0,28},{4,8},{8,4},{12,16},{16,12},{20,24},{24,20},{28,0},{1,29},{... | collective-permute-start | bytes 12296 | tf_op jit(solution)/shard_map/ppermute | solution.py:347
  14.4 0.0 collective-permute-start.3
  14.4 0.0 copy-start.3
  14.4 0.0 copy-done
  14.4 0.0 copy-done.1
  14.4 0.6 %copy-done.3 = s32[1,1,16]{2,1,0:T(1,128)S(1)} copy-done((s32[1,1,16]{2,1,0:T(1,128)S(1)}, s32[1,1,16]{2,1,0:T(1,128)}, u32[]{:S(2)}) %copy-start.3) | copy-done | bytes 88
  15.1 0.0 copy-start.2
  15.1 0.2 %halved_weights.1 = (bf16[512,32]{1,0:T(8,128)(2,1)S(1)}, bf16[512,512]{1,0:T(8,128)(2,1)S(1)}, s32[1,16]{1,0:T(1,128)S(1)}) custom-call(bf16[32,512]{1,0:T(8,128)(2,1)S(1)} %copy-done.1, bf16[512,512]{1,0:T(8,128)(2,1)S(1)} %copy-done, s32[1,16]{1,0:T(1,128)S(1)} %bitcast.18, f32[8,128]{1,0:T(8,128)S(1)} %get-tuple-element.32.after_ref.known_ref), custom_call_target="tpu_custom_call" | custom-call | flops 500000000 | bytes 1500000 | tf_op jit(solution)/shard_map/halved_weights/pallas_call | solution.py:349
  15.3 2.4 %collective-permute-done.2.odd_ref = f32[8,128]{1,0:T(8,128)S(1)} collective-permute-done((f32[8,128]{1,0:T(8,128)S(1)}, f32[8,128]{1,0:T(8,128)S(1)}, u32[]{:S(2)}, u32[]{:S(2)}) %collective-permute-start.2) | collective-permute-done | bytes 4128 | tf_op jit(solution)/shard_map/ppermute | solution.py:347
  17.7 0.0 collective-permute-done.3.even_ref
  17.7 0.0 collective-permute-done.4.refs_1_
  17.7 0.0 collective-permute-done.5.refs_2_
  17.7 0.0 collective-permute-done.6.refs_3_
  17.7 0.0 copy-done.2
  17.7 4.1 %chemistry.1 = (bf16[4,8,4096]{2,1,0:T(8,128)(2,1)}, f32[1,1]{1,0:T(1,128)}) custom-call(s32[16]{0:T(128)S(1)} %bitcast.19, bf16[512,32]{1,0:T(8,128)(2,1)S(1)} %get-tuple-element.34.w1_ref, bf16[512,512]{1,0:T(8,128)(2,1)S(1)} %get-tuple-element.35.w2_ref, bf16[32,512]{1,0:T(8,128)(2,1)S(1)} %bitcast.16, ...), custom_call_target="tpu_custom_call" | custom-call | flops 4000000000 | bytes 12000000 | tf_op jit(solution)/shard_map/chemistry/pallas_call | solution.py:359
Async XLA Ops:
  1.8 5.1 %collective-permute-start = (f32[88,128]{1,0:T(8,128)S(1)}, f32[88,128]{1,0:T(8,128)S(1)}, u32[]{:S(2)}, u32[]{:S(2)}) collective-permute-start(f32[88,128]{1,0:T(8,128)S(1)} %get-tuple-element.23), channel_id=1, source_target_pairs={{0,28},{4,8},{8,4},{12,16},{16,12},{20,24},{24,20},{28,0},{1,29},{... | collective-permute-start | bytes 135176 | tf_op jit(solution)/shard_map/ppermute | solution.py:322
  5.1 1.7 %collective-permute-start.1 = (f32[88,128]{1,0:T(8,128)S(1)}, f32[88,128]{1,0:T(8,128)S(1)}, u32[]{:S(2)}, u32[]{:S(2)}) collective-permute-start(f32[88,128]{1,0:T(8,128)S(1)} %get-tuple-element.24), channel_id=1, source_target_pairs={{0,4},{4,0},{8,12},{12,8},{16,20},{20,16},{24,28},{28,24},{1,5},{5... | collective-permute-start | bytes 135176 | tf_op jit(solution)/shard_map/ppermute | solution.py:323
  5.8 8.6 %copy-start = (bf16[512,512]{1,0:T(8,128)(2,1)S(1)}, bf16[512,512]{1,0:T(8,128)(2,1)}, u32[]{:S(2)}) copy-start(bf16[512,512]{1,0:T(8,128)(2,1)} %w2_ref.1) | copy-start | bytes 1572868
  6.9 7.5 %copy-start.1 = (bf16[32,512]{1,0:T(8,128)(2,1)S(1)}, bf16[32,512]{1,0:T(8,128)(2,1)}, u32[]{:S(2)}) copy-start(bf16[32,512]{1,0:T(8,128)(2,1)} %w1_ref.1) | copy-start | bytes 98308
  7.1 10.6 %collective-permute-start.4 = (bf16[8,4096]{1,0:T(8,128)(2,1)S(1)}, bf16[8,4096]{1,0:T(8,128)(2,1)S(1)}, u32[]{:S(2)}, u32[]{:S(2)}) collective-permute-start(bf16[8,4096]{1,0:T(8,128)(2,1)S(1)} %get-tuple-element.39), channel_id=1, source_target_pairs={{0,1},{1,2},{2,3},{3,0},{4,5},{5,6},{6,7},{7,4},{8,9},{9,10},{10,1... | collective-permute-start | bytes 196616 | tf_op jit(solution)/shard_map/ppermute | solution.py:344
  9.8 7.9 %collective-permute-start.5 = (bf16[8,4096]{1,0:T(8,128)(2,1)S(1)}, bf16[8,4096]{1,0:T(8,128)(2,1)S(1)}, u32[]{:S(2)}, u32[]{:S(2)}) collective-permute-start(bf16[8,4096]{1,0:T(8,128)(2,1)S(1)} %get-tuple-element.40), channel_id=1, source_target_pairs={{0,2},{1,3},{2,0},{3,1},{4,6},{5,7},{6,4},{7,5},{8,10},{9,11},{10,... | collective-permute-start | bytes 196616 | tf_op jit(solution)/shard_map/ppermute | solution.py:344
  12.4 5.3 %collective-permute-start.6 = (bf16[8,4096]{1,0:T(8,128)(2,1)S(1)}, bf16[8,4096]{1,0:T(8,128)(2,1)S(1)}, u32[]{:S(2)}, u32[]{:S(2)}) collective-permute-start(bf16[8,4096]{1,0:T(8,128)(2,1)S(1)} %get-tuple-element.41), channel_id=1, source_target_pairs={{0,3},{1,0},{2,1},{3,2},{4,7},{5,4},{6,5},{7,6},{8,11},{9,8},{10,9... | collective-permute-start | bytes 196616 | tf_op jit(solution)/shard_map/ppermute | solution.py:344
  13.7 3.9 %collective-permute-start.2 = (f32[8,128]{1,0:T(8,128)S(1)}, f32[8,128]{1,0:T(8,128)S(1)}, u32[]{:S(2)}, u32[]{:S(2)}) collective-permute-start(f32[8,128]{1,0:T(8,128)S(1)} %get-tuple-element.36), channel_id=1, source_target_pairs={{0,28},{4,8},{8,4},{12,16},{16,12},{20,24},{24,20},{28,0},{1,29},{... | collective-permute-start | bytes 12296 | tf_op jit(solution)/shard_map/ppermute | solution.py:347
  14.4 3.3 %collective-permute-start.3 = (f32[8,128]{1,0:T(8,128)S(1)}, f32[8,128]{1,0:T(8,128)S(1)}, u32[]{:S(2)}, u32[]{:S(2)}) collective-permute-start(f32[8,128]{1,0:T(8,128)S(1)} %get-tuple-element.37), channel_id=1, source_target_pairs={{0,4},{4,0},{8,12},{12,8},{16,20},{20,16},{24,28},{28,24},{1,5},{5... | collective-permute-start | bytes 12296 | tf_op jit(solution)/shard_map/ppermute | solution.py:348
  14.4 0.7 %copy-start.3 = (s32[1,1,16]{2,1,0:T(1,128)S(1)}, s32[1,1,16]{2,1,0:T(1,128)}, u32[]{:S(2)}) copy-start(s32[1,1,16]{2,1,0:T(1,128)} %param.12) | copy-start | bytes 196
  15.1 2.6 %copy-start.2 = (bf16[512,32]{0,1:T(8,128)(2,1)S(1)}, bf16[512,32]{0,1:T(8,128)(2,1)}, u32[]{:S(2)}) copy-start(bf16[512,32]{0,1:T(8,128)(2,1)} %param.11) | copy-start | bytes 98308

commit v6 on v5

--- a/solution.py
+++ b/solution.py
@@ -74,8 +74,8 @@
 
     copies[2].wait()
     copies[3].wait()
-    lane = lax.broadcasted_iota(jnp.int32, (SUB, LANES), 1)
-    hits = jnp.zeros((SUB, LANES), jnp.float32)
+    lane = lax.broadcasted_iota(jnp.int32, hits_ref.shape, 1)
+    hits = jnp.zeros(hits_ref.shape, jnp.float32)
     for j in range(list_ref.shape[0]):
         target = jnp.where(list_ref[j] < blocks, dest_ref[j], -1)
         hits = hits + jnp.where(lane == target, 1.0, 0.0)
@@ -99,8 +99,6 @@
             high, low = spot(length - SUB, half, halves), spot(0, half, halves)
             up_ref[start + BEHIND * species : start + part, :] = rates_ref[high : high + SUB, :]
             down_ref[start + BEHIND * species : start + part, :] = rates_ref[low : low + SUB, :]
-        up_ref[halves * part :, :] = hits
-        down_ref[halves * part :, :] = hits
 
     even = lax.rem(lax.axis_index("tile"), 2) == 0
 
@@ -140,21 +138,15 @@
                 out_refs[k][:, place : place + LANES] = value.astype(jnp.bfloat16)
 
 
-def edge_kernel(
-    dests, length, halves, odd_ref, even_ref, hits_ref, q_ref, rates_ref, *refs
-):
-    in_refs, out_refs, (to_even_ref, to_odd_ref, known_ref) = (
-        refs[:dests], refs[dests : 2 * dests], refs[2 * dests :]
+def edge_kernel(dests, early, late, length, halves, odd_ref, even_ref, q_ref, rates_ref, *refs):
+    in_refs, out_refs, small_refs = (
+        refs[: len(late)], refs[len(late) : 2 * len(late)], refs[2 * len(late) :]
     )
     species, cells = out_refs[0].shape
     me = lax.axis_index("spec")
     part = BEHIND * species + SUB
     reach = BEHIND + AHEAD
     even = lax.rem(lax.axis_index("tile"), 2) == 0
-    own, from_even, from_odd = hits_ref[...], even_ref[halves * part :, :], odd_ref[halves * part :, :]
-    known_ref[...] = own + from_even + from_odd
-    to_even_ref[...] = from_odd
-    to_odd_ref[...] = from_even
 
     def message(behind, at, size):
         a, b = odd_ref[at : at + size, :], even_ref[at : at + size, :]
@@ -190,7 +182,16 @@
                 rates_of(own_rates(length - reach) + [after[j : j + 1] for j in range(AHEAD)]),
             )
         )
-    for k, (in_ref, out_ref) in enumerate(zip(in_refs, out_refs)):
+    for k, small_ref in zip(early, small_refs):
+        low = lax.rem(me + k, dests) == 0
+        for half in range(halves):
+            for j in range(BEHIND):
+                value = tops[half][j]
+                if j >= BEHIND - AHEAD:
+                    value = jnp.where(low, value, bottoms[half][j - BEHIND + AHEAD])
+                at = (j * halves + half) * LANES
+                small_ref[:, at : at + LANES] = value.astype(jnp.bfloat16)
+    for k, in_ref, out_ref in zip(late, in_refs, out_refs):
         dest = lax.rem(me + k, dests)
         out_ref[...] = in_ref[...]
 
@@ -215,22 +216,34 @@
     w2_out[...] = (0.5 * w2_ref[...].astype(jnp.float32)).T.astype(jnp.bfloat16)
 
 
-def chemistry_kernel(
-    groups, list_ref, w1_ref, w2_ref, w3_ref, known_ref, odd_ref, even_ref, *refs
-):
-    parts, (out_ref, share_ref, state_ref, picked_ref, held_ref, done) = refs[:groups], refs[groups:]
+def chemistry_kernel(groups, early, list_ref, w1_ref, w2_ref, w3_ref, hits_in, *refs):
+    parts, edges, refs = refs[:groups], refs[groups : groups + len(early)], refs[groups + len(early) :]
+    out_ref, share_ref, state_ref, picked_ref, hits_ref, held_ref, done = refs
     species, cells = state_ref.shape[1:]
     slots = list_ref.shape[0]
     blocks = cells // BLK
     me = lax.axis_index("spec")
+
+    def source(k):
+        return lax.rem(me - k + groups, groups)
+
     for k in range(groups):
-        state_ref[lax.rem(me - k + groups, groups)] = parts[k][...]
-    hits = known_ref[...] + even_ref[...] + odd_ref[...]
-    lane = lax.broadcasted_iota(jnp.int32, hits.shape, 1)
-    mine = jnp.where(lane == lax.axis_index("tile"), hits, 0.0)
-    held_ref[...] = jnp.sum(mine[0:1], axis=1, keepdims=True) / RECV
-    share = pltpu.make_async_copy(held_ref, share_ref, done.at[0])
-    share.start()
+        state_ref[source(k)] = parts[k][...]
+    wide = edges[0].shape[1]
+    narrow = wide // BEHIND * AHEAD
+
+    @pl.when(me == 0)
+    def _():
+        for k, edge in zip(early, edges):
+            state_ref[source(k), :, 0:wide] = edge[...]
+
+    @pl.when(me == groups - 1)
+    def _():
+        for k, edge in zip(early, edges):
+            state_ref[source(k), :, cells - narrow :] = edge[:, wide - narrow :]
+
+    naming = pltpu.make_async_copy(hits_in, hits_ref, done.at[2])
+    naming.start()
 
     def place(j):
         return pl.ds(pl.multiple_of(jnp.minimum(list_ref[j], blocks - 1) * BLK, BLK), BLK)
@@ -258,6 +271,13 @@
             state_ref[g, :, place(j)] = jnp.where(valid, fresh, now).astype(jnp.bfloat16)
     whole = pltpu.make_async_copy(state_ref, out_ref, done.at[1])
     whole.start()
+    naming.wait()
+    lane = lax.broadcasted_iota(jnp.int32, hits_ref.shape, 1)
+    mine = jnp.where(lane == lax.axis_index("tile"), hits_ref[...], 0.0)
+    mine = jnp.sum(mine, axis=0, keepdims=True)
+    held_ref[...] = jnp.sum(mine, axis=1, keepdims=True) / RECV
+    share = pltpu.make_async_copy(held_ref, share_ref, done.at[0])
+    share.start()
     share.wait()
     whole.wait()
 
@@ -289,8 +309,8 @@
     halves = cols // LANES
     f32, bf16 = jnp.float32, jnp.bfloat16
     params = pltpu.CompilerParams(vmem_limit_bytes=VMEM_BYTES)
-    size = halves * (BEHIND * species + SUB) + SUB
-    flag = jax.ShapeDtypeStruct((SUB, LANES), f32)
+    size = halves * (BEHIND * species + SUB)
+    flag = jax.ShapeDtypeStruct((1, LANES), f32)
 
     to_even, to_odd, hits, field, rates = pl.pallas_call(
         functools.partial(pack_kernel, length, halves, cells // BLK),
@@ -331,21 +351,25 @@
         cost_estimate=cost(1.0),
         name="inner_rows",
     )(field, rates)
-    *blocks, to_even, to_odd, known = pl.pallas_call(
-        functools.partial(edge_kernel, dests, length, halves),
-        out_shape=[block] * dests + [flag] * 3,
-        in_specs=[vmem()] * (5 + dests),
-        out_specs=[vmem()] * (dests + 3),
+    def ring(k, x):
+        return lax.ppermute(x, "spec", [(s, (s + k) % dests) for s in range(dests)])
+
+    early, late = [1], [0] + list(range(2, dests))
+    edge = jax.ShapeDtypeStruct((species, BEHIND * cols), bf16)
+    whole = pl.pallas_call(
+        functools.partial(edge_kernel, dests, early, late, length, halves),
+        out_shape=[block] * len(late) + [edge] * len(early),
+        in_specs=[vmem()] * (4 + len(late)),
+        out_specs=[vmem()] * dests,
         compiler_params=params,
         cost_estimate=cost(0.1),
         name="edge_rows",
-    )(from_odd, from_even, hits, field, rates, *blocks)
-    received = [blocks[0]] + [
-        lax.ppermute(blocks[k], "spec", [(s, (s + k) % dests) for s in range(dests)])
-        for k in range(1, dests)
-    ]
-    from_odd = lax.ppermute(to_odd, "tile", odds)
-    from_even = lax.ppermute(to_even, "tile", evens)
+    )(from_odd, from_even, field, rates, *[blocks[k] for k in late])
+    full, edges = whole[: len(late)], whole[len(late) :]
+    received = {k: ring(k, blocks[k]) for k in early}
+    received |= {k: ring(k, x) if k else x for k, x in zip(late, full)}
+    edges = [ring(k, x) for k, x in zip(early, edges)]
+    hits = lax.all_gather(hits, "tile", axis=0, tiled=True)
     w1, w2, listing = pl.pallas_call(
         weight_kernel,
         out_shape=[jax.ShapeDtypeStruct(w.shape[::-1], bf16) for w in (first_weight, middle_weight)]
@@ -355,20 +379,24 @@
         compiler_params=params,
         cost_estimate=cost(0.5),
         name="halved_weights",
-    )(first_weight, middle_weight, active_blocks.reshape(1, slots), known)
+    )(first_weight, middle_weight, active_blocks.reshape(1, slots), full[0])
     out, load_share = pl.pallas_call(
-        functools.partial(chemistry_kernel, dests),
+        functools.partial(chemistry_kernel, dests, early),
         out_shape=[
             jax.ShapeDtypeStruct((dests, species, cells), bf16),
             jax.ShapeDtypeStruct((1, 1), f32),
         ],
-        in_specs=[pl.BlockSpec(memory_space=pltpu.SMEM)] + [vmem()] * (6 + dests),
+        in_specs=[pl.BlockSpec(memory_space=pltpu.SMEM)]
+        + [vmem()] * 3
+        + [anywhere()]
+        + [vmem()] * (dests + len(early)),
         out_specs=[anywhere()] * 2,
         scratch_shapes=[
             pltpu.VMEM((dests, species, cells), bf16),
             pltpu.VMEM((dests * species, slots * BLK), f32),
+            pltpu.VMEM((tiles, LANES), f32),
             pltpu.VMEM((1, 1), f32),
-            pltpu.SemaphoreType.DMA((2,)),
+            pltpu.SemaphoreType.DMA((3,)),
         ],
         compiler_params=params,
         cost_estimate=cost(4.0),
@@ -378,10 +406,9 @@
         w1,
         w2,
         last_weight.T,
-        known,
-        from_odd,
-        from_even,
-        *received,
+        from_hbm(hits),
+        *[received[k] for k in range(dests)],
+        *edges,
     )
     return out.reshape(dests * species, cells), load_share
 

time: 21.9 us -> 31 us (1.42)
  blocking collectives: 0 us -> 9.08 us
  starting transfers between devices: 10.8 us -> 10.2 us
  waiting for transfers between devices: 3.4 us -> 3.97 us
    all_gather x0 -> x1, blocking collectives: none -> 9.08 us  [shards(): hits = lax.all_gather(hits, 'tile', axis=0, tiled=True)]
    ppermute x3 -> x4, waiting for transfers between devices: 0.01 us -> 3.96 us  [ring(): return lax.ppermute(x, 'spec', [(s, (s + k) % dests) for s in range(dests)])]
    ppermute x2 -> x1, waiting for transfers between devices: 3.39 us -> 0.01 us  [shards(): from_odd = lax.ppermute(to_odd, 'tile', odds)]
    ppermute x2 -> x1, starting transfers between devices: 4.07 us -> 3.4 us  [shards(): from_odd = lax.ppermute(to_odd, 'tile', odds)]
    ppermute x3 -> x4, starting transfers between devices: 6.7 us -> 6.75 us  [ring(): return lax.ppermute(x, 'spec', [(s, (s + k) % dests) for s in range(dests)])]
  transfers between devices with their start and end apart: 7 -> 6, of which waited for: 2 -> 1; matrix products, arithmetic and copies ran while one was open for 0% -> 0% of each run, Pallas kernels for 4% -> 3%
where the time goes in v6:
time: 31 us; the launch traced here: 30.8 us
  starting transfers between devices  10.2 us (33%)
  blocking collectives  9.08 us (29%)
  Pallas kernels  6.27 us (20%)
  waiting for transfers between devices  3.97 us (13%)
  between operations  0.69 us (2%)
  local copies, waits for them, and re-layouts  0.66 us (2%)
    all_gather x1, blocking collectives, shards(): hits = lax.all_gather(hits, 'tile', axis=0, tiled=True)  9.08 us
    ppermute x4, starting transfers between devices, ring(): return lax.ppermute(x, 'spec', [(s, (s + k) % dests) for s in range(dests)])  6.75 us
    pallas_call x1, Pallas kernels, shards(): pl.pallas_call(functools.partial(chemistry_kernel, dests, early), out_sha...  4.09 us
    ppermute x4, waiting for transfers between devices, ring(): return lax.ppermute(x, 'spec', [(s, (s + k) % dests) for s in range(dests)])  3.96 us
    ppermute x1, starting transfers between devices, shards(): from_odd = lax.ppermute(to_odd, 'tile', odds)  3.4 us
    pallas_call x1, Pallas kernels, shards(): pl.pallas_call(functools.partial(pack_kernel, length, halves, cells // BL...  1.11 us
    pallas_call x1, Pallas kernels, shards(): pl.pallas_call(functools.partial(inner_kernel, dests, length, halves), ou...  0.67 us
    unnamed x8, local copies, waits for them, and re-layouts  0.66 us
  transfers between devices with their start and end apart: 6, of which 1 were waited for; matrix products, arithmetic and copies ran while one was open for 0% of the time, Pallas kernels for 3%

profile of v6, /device:TPU:0, one launch (start us, length us, event | category | flops | bytes accessed | tf_op | source)
XLA Modules:
  0.0 30.8 jit_solution(10435279251712925623)
XLA Ops:
  0.6 1.1 %pack_edges.1 = (f32[80,128]{1,0:T(8,128)S(1)}, f32[80,128]{1,0:T(8,128)S(1)}, f32[1,128]{1,0:T(1,128)S(1)}, f32[1024,128]{1,0:T(8,128)S(1)}, f32[128,128]{1,0:T(8,128)S(1)}) custom-call(f32[1024,128]{1,0:T(8,128)} %bitcast.24, f32[128,128]{1,0:T(8,128)} %bitcast.25, s32[16]{0:T(128)} %bitcast.20, s32[16]{0:T(128)} %bitcast.26), custom_call_target="tpu_custom_call" | custom-call | flops 1000000000 | bytes 3000000 | tf_op jit(solution)/shard_map/pack_edges/pallas_call | solution.py:315
  1.7 3.4 %collective-permute-start = (f32[80,128]{1,0:T(8,128)S(1)}, f32[80,128]{1,0:T(8,128)S(1)}, u32[]{:S(2)}, u32[]{:S(2)}) collective-permute-start(f32[80,128]{1,0:T(8,128)S(1)} %get-tuple-element.20), channel_id=1, source_target_pairs={{0,28},{4,8},{8,4},{12,16},{16,12},{20,24},{24,20},{28,0},{1,29},{... | collective-permute-start | bytes 122888 | tf_op jit(solution)/shard_map/ppermute | solution.py:342
  5.1 0.0 collective-permute-start.1
  5.2 0.7 %inner_rows.1 = (bf16[8,4096]{1,0:T(8,128)(2,1)S(1)}, bf16[8,4096]{1,0:T(8,128)(2,1)S(1)}, bf16[8,4096]{1,0:T(8,128)(2,1)S(1)}, bf16[8,4096]{1,0:T(8,128)(2,1)S(1)}) custom-call(f32[1024,128]{1,0:T(8,128)S(1)} %get-tuple-element.22.q_ref, f32[128,128]{1,0:T(8,128)S(1)} %get-tuple-element.23.rates_ref), custom_call_target="tpu_custom_call" | custom-call | flops 1000000000 | bytes 3000000 | tf_op jit(solution)/shard_map/inner_rows/pallas_call | solution.py:345
  5.8 0.0 copy-start
  5.8 1.6 %collective-permute-start.2 = (bf16[8,4096]{1,0:T(8,128)(2,1)S(1)}, bf16[8,4096]{1,0:T(8,128)(2,1)S(1)}, u32[]{:S(2)}, u32[]{:S(2)}) collective-permute-start(bf16[8,4096]{1,0:T(8,128)(2,1)S(1)} %get-tuple-element.32), channel_id=1, source_target_pairs={{0,1},{1,2},{2,3},{3,0},{4,5},{5,6},{6,7},{7,4},{8,9},{9,10},{10,1... | collective-permute-start | bytes 196616 | tf_op jit(solution)/shard_map/ppermute | solution.py:355
  7.5 0.0 collective-permute-done.odd_ref
  7.5 0.0 collective-permute-done.1.even_ref
  7.5 0.0 copy-start.1
  7.5 0.2 edge_rows.1
  7.6 3.1 %collective-permute-start.3 = (bf16[8,4096]{1,0:T(8,128)(2,1)S(1)}, bf16[8,4096]{1,0:T(8,128)(2,1)S(1)}, u32[]{:S(2)}, u32[]{:S(2)}) collective-permute-start(bf16[8,4096]{1,0:T(8,128)(2,1)S(1)} %get-tuple-element.33), channel_id=1, source_target_pairs={{0,2},{1,3},{2,0},{3,1},{4,6},{5,7},{6,4},{7,5},{8,10},{9,11},{10,... | collective-permute-start | bytes 196616 | tf_op jit(solution)/shard_map/ppermute | solution.py:355
  10.7 1.3 %collective-permute-start.4 = (bf16[8,4096]{1,0:T(8,128)(2,1)S(1)}, bf16[8,4096]{1,0:T(8,128)(2,1)S(1)}, u32[]{:S(2)}, u32[]{:S(2)}) collective-permute-start(bf16[8,4096]{1,0:T(8,128)(2,1)S(1)} %get-tuple-element.34), channel_id=1, source_target_pairs={{0,3},{1,0},{2,1},{3,2},{4,7},{5,4},{6,5},{7,6},{8,11},{9,8},{10,9... | collective-permute-start | bytes 196616 | tf_op jit(solution)/shard_map/ppermute | solution.py:355
  12.1 9.1 %all-gather = f32[8,1,128]{2,1,0:T(1,128)} all-gather(f32[1,1,128]{2,1,0:T(1,128)S(1)} %bitcast.18), channel_id=1, replica_groups=mesh['tile'=8,'spec'=4] {'tile'}, dimensions={0}, use_global_device_ids=true | all-gather | bytes 4608 | tf_op jit(solution)/shard_map/all_gather | solution.py:372
  21.2 0.7 %collective-permute-start.5 = (bf16[8,1024]{1,0:T(8,128)(2,1)S(1)}, bf16[8,1024]{1,0:T(8,128)(2,1)S(1)}, u32[]{:S(2)}, u32[]{:S(2)}) collective-permute-start(bf16[8,1024]{1,0:T(8,128)(2,1)S(1)} %get-tuple-element.35), channel_id=1, source_target_pairs={{0,1},{1,2},{2,3},{3,0},{4,5},{5,6},{6,7},{7,4},{8,9},{9,10},{10,1... | collective-permute-start | bytes 49160 | tf_op jit(solution)/shard_map/ppermute | solution.py:355
  21.8 0.0 copy-start.3
  21.8 0.0 copy-done
  21.9 0.0 copy-done.1
  21.9 0.6 %copy-done.3 = s32[1,1,16]{2,1,0:T(1,128)S(1)} copy-done((s32[1,1,16]{2,1,0:T(1,128)S(1)}, s32[1,1,16]{2,1,0:T(1,128)}, u32[]{:S(2)}) %copy-start.3) | copy-done | bytes 88
  22.5 0.0 copy-start.2
  22.5 0.2 halved_weights.1
  22.8 4.0 %collective-permute-done.5.refs_4_ = bf16[8,1024]{1,0:T(8,128)(2,1)S(1)} collective-permute-done((bf16[8,1024]{1,0:T(8,128)(2,1)S(1)}, bf16[8,1024]{1,0:T(8,128)(2,1)S(1)}, u32[]{:S(2)}, u32[]{:S(2)}) %collective-permute-start.5) | collective-permute-done | bytes 16416 | tf_op jit(solution)/shard_map/ppermute | solution.py:355
  26.7 0.0 collective-permute-done.2.refs_1_
  26.7 0.0 collective-permute-done.3.refs_2_
  26.7 0.0 collective-permute-done.4.refs_3_
  26.7 0.0 copy-done.2
  26.7 4.1 %chemistry.1 = (bf16[4,8,4096]{2,1,0:T(8,128)(2,1)}, f32[1,1]{1,0:T(1,128)}) custom-call(s32[16]{0:T(128)S(1)} %bitcast.22, bf16[512,32]{1,0:T(8,128)(2,1)S(1)} %get-tuple-element.29.w1_ref, bf16[512,512]{1,0:T(8,128)(2,1)S(1)} %get-tuple-element.30.w2_ref, bf16[32,512]{1,0:T(8,128)(2,1)S(1)} %bitcast.19, f32[8,128]{1,0:T(8,128)} %bitcast.23, ...), custom_call_target="tpu_custom_call" | custom-call | flops 4000000000 | bytes 12000000 | tf_op jit(solution)/shard_map/chemistry/pallas_call | solution.py:383
Async XLA Ops:
  1.7 5.7 %collective-permute-start = (f32[80,128]{1,0:T(8,128)S(1)}, f32[80,128]{1,0:T(8,128)S(1)}, u32[]{:S(2)}, u32[]{:S(2)}) collective-permute-start(f32[80,128]{1,0:T(8,128)S(1)} %get-tuple-element.20), channel_id=1, source_target_pairs={{0,28},{4,8},{8,4},{12,16},{16,12},{20,24},{24,20},{28,0},{1,29},{... | collective-permute-start | bytes 122888 | tf_op jit(solution)/shard_map/ppermute | solution.py:342
  5.1 2.3 %collective-permute-start.1 = (f32[80,128]{1,0:T(8,128)S(1)}, f32[80,128]{1,0:T(8,128)S(1)}, u32[]{:S(2)}, u32[]{:S(2)}) collective-permute-start(f32[80,128]{1,0:T(8,128)S(1)} %get-tuple-element.21), channel_id=1, source_target_pairs={{0,4},{4,0},{8,12},{12,8},{16,20},{20,16},{24,28},{28,24},{1,5},{5... | collective-permute-start | bytes 122888 | tf_op jit(solution)/shard_map/ppermute | solution.py:343
  5.8 16.0 %copy-start = (bf16[512,512]{1,0:T(8,128)(2,1)S(1)}, bf16[512,512]{1,0:T(8,128)(2,1)}, u32[]{:S(2)}) copy-start(bf16[512,512]{1,0:T(8,128)(2,1)} %w2_ref.1) | copy-start | bytes 1572868
  5.8 20.9 %collective-permute-start.2 = (bf16[8,4096]{1,0:T(8,128)(2,1)S(1)}, bf16[8,4096]{1,0:T(8,128)(2,1)S(1)}, u32[]{:S(2)}, u32[]{:S(2)}) collective-permute-start(bf16[8,4096]{1,0:T(8,128)(2,1)S(1)} %get-tuple-element.32), channel_id=1, source_target_pairs={{0,1},{1,2},{2,3},{3,0},{4,5},{5,6},{6,7},{7,4},{8,9},{9,10},{10,1... | collective-permute-start | bytes 196616 | tf_op jit(solution)/shard_map/ppermute | solution.py:355
  7.5 14.4 %copy-start.1 = (bf16[32,512]{1,0:T(8,128)(2,1)S(1)}, bf16[32,512]{1,0:T(8,128)(2,1)}, u32[]{:S(2)}) copy-start(bf16[32,512]{1,0:T(8,128)(2,1)} %w1_ref.1) | copy-start | bytes 98308
  7.6 19.1 %collective-permute-start.3 = (bf16[8,4096]{1,0:T(8,128)(2,1)S(1)}, bf16[8,4096]{1,0:T(8,128)(2,1)S(1)}, u32[]{:S(2)}, u32[]{:S(2)}) collective-permute-start(bf16[8,4096]{1,0:T(8,128)(2,1)S(1)} %get-tuple-element.33), channel_id=1, source_target_pairs={{0,2},{1,3},{2,0},{3,1},{4,6},{5,7},{6,4},{7,5},{8,10},{9,11},{10,... | collective-permute-start | bytes 196616 | tf_op jit(solution)/shard_map/ppermute | solution.py:355
  10.7 16.0 %collective-permute-start.4 = (bf16[8,4096]{1,0:T(8,128)(2,1)S(1)}, bf16[8,4096]{1,0:T(8,128)(2,1)S(1)}, u32[]{:S(2)}, u32[]{:S(2)}) collective-permute-start(bf16[8,4096]{1,0:T(8,128)(2,1)S(1)} %get-tuple-element.34), channel_id=1, source_target_pairs={{0,3},{1,0},{2,1},{3,2},{4,7},{5,4},{6,5},{7,6},{8,11},{9,8},{10,9... | collective-permute-start | bytes 196616 | tf_op jit(solution)/shard_map/ppermute | solution.py:355
  21.2 5.5 %collective-permute-start.5 = (bf16[8,1024]{1,0:T(8,128)(2,1)S(1)}, bf16[8,1024]{1,0:T(8,128)(2,1)S(1)}, u32[]{:S(2)}, u32[]{:S(2)}) collective-permute-start(bf16[8,1024]{1,0:T(8,128)(2,1)S(1)} %get-tuple-element.35), channel_id=1, source_target_pairs={{0,1},{1,2},{2,3},{3,0},{4,5},{5,6},{6,7},{7,4},{8,9},{9,10},{10,1... | collective-permute-start | bytes 49160 | tf_op jit(solution)/shard_map/ppermute | solution.py:355
  21.8 0.7 %copy-start.3 = (s32[1,1,16]{2,1,0:T(1,128)S(1)}, s32[1,1,16]{2,1,0:T(1,128)}, u32[]{:S(2)}) copy-start(s32[1,1,16]{2,1,0:T(1,128)} %param.12) | copy-start | bytes 196
  22.5 4.2 %copy-start.2 = (bf16[512,32]{0,1:T(8,128)(2,1)S(1)}, bf16[512,32]{0,1:T(8,128)(2,1)}, u32[]{:S(2)}) copy-start(bf16[512,32]{0,1:T(8,128)(2,1)} %param.11) | copy-start | bytes 98308

commit v7 on v6

--- a/solution.py
+++ b/solution.py
@@ -55,33 +55,35 @@
     return (at // SUB * halves + half) * SUB + at % SUB
 
 
-def pack_kernel(
-    length, halves, blocks, q_in, rates_in, list_in, dest_in,
-    even_ref, odd_ref, hits_ref, q_ref, rates_ref, list_ref, dest_ref, arrived,
-):
-    pairs = [(q_in, q_ref), (rates_in, rates_ref), (list_in, list_ref), (dest_in, dest_ref)]
+def load_kernel(*refs):
+    *refs, arrived = refs
+    count = len(refs) // 2
     copies = [
-        pltpu.make_async_copy(source, target, arrived.at[i])
-        for i, (source, target) in enumerate(pairs)
+        pltpu.make_async_copy(refs[i], refs[count + i], arrived.at[i]) for i in range(count)
     ]
     for copy in copies:
         copy.start()
+    for copy in copies:
+        copy.wait()
+
+
+def pack_kernel(
+    length, halves, blocks, q_ref, rates_ref, list_ref, dest_ref, other_list_ref, other_dest_ref,
+    even_ref, odd_ref, hits_ref,
+):
     species = q_ref.shape[0] // (length * halves)
     part = BEHIND * species + SUB
 
     def row(at, half):
         return q_ref[pl.ds(spot(at, half, halves), species, stride=length * halves), :]
 
-    copies[2].wait()
-    copies[3].wait()
-    lane = lax.broadcasted_iota(jnp.int32, hits_ref.shape, 1)
-    hits = jnp.zeros(hits_ref.shape, jnp.float32)
-    for j in range(list_ref.shape[0]):
-        target = jnp.where(list_ref[j] < blocks, dest_ref[j], -1)
-        hits = hits + jnp.where(lane == target, 1.0, 0.0)
+    tile = lax.broadcasted_iota(jnp.int32, (hits_ref.shape[0], list_ref.shape[1]), 0)
+    named = jnp.zeros(tile.shape, jnp.float32)
+    for listed_ref, target_ref in ((list_ref, dest_ref), (other_list_ref, other_dest_ref)):
+        target = jnp.where(listed_ref[...] < blocks, target_ref[...], -1)
+        named = named + jnp.where(tile == target, 1.0, 0.0)
+    hits = jnp.broadcast_to(jnp.sum(named, axis=1, keepdims=True), hits_ref.shape)
     hits_ref[...] = hits
-    copies[1].wait()
-    copies[0].wait()
 
     def write(up_ref, down_ref):
         for half in range(halves):
@@ -99,6 +101,8 @@
             high, low = spot(length - SUB, half, halves), spot(0, half, halves)
             up_ref[start + BEHIND * species : start + part, :] = rates_ref[high : high + SUB, :]
             down_ref[start + BEHIND * species : start + part, :] = rates_ref[low : low + SUB, :]
+        up_ref[halves * part :, :] = hits
+        down_ref[halves * part :, :] = hits
 
     even = lax.rem(lax.axis_index("tile"), 2) == 0
 
@@ -138,15 +142,18 @@
                 out_refs[k][:, place : place + LANES] = value.astype(jnp.bfloat16)
 
 
-def edge_kernel(dests, early, late, length, halves, odd_ref, even_ref, q_ref, rates_ref, *refs):
-    in_refs, out_refs, small_refs = (
-        refs[: len(late)], refs[len(late) : 2 * len(late)], refs[2 * len(late) :]
-    )
+def edge_kernel(
+    dests, early, late, length, halves, odd_ref, even_ref, hits_ref, q_ref, rates_ref, *refs
+):
+    in_refs, out_refs, refs = refs[: len(late)], refs[len(late) : 2 * len(late)], refs[2 * len(late) :]
+    *small_refs, known_ref, to_even_ref = refs
     species, cells = out_refs[0].shape
     me = lax.axis_index("spec")
     part = BEHIND * species + SUB
     reach = BEHIND + AHEAD
     even = lax.rem(lax.axis_index("tile"), 2) == 0
+    known_ref[...] = hits_ref[...] + odd_ref[halves * part :, :]
+    to_even_ref[...] = odd_ref[halves * part :, :]
 
     def message(behind, at, size):
         a, b = odd_ref[at : at + size, :], even_ref[at : at + size, :]
@@ -210,15 +217,16 @@
                     out_ref[:, at : at + LANES] = value.astype(jnp.bfloat16)
 
 
-def weight_kernel(w1_ref, w2_ref, list_ref, after_ref, w1_out, w2_out, list_out):
-    list_out[...] = list_ref[...]
+def weight_kernel(w1_ref, w2_ref, after_ref, w1_out, w2_out):
     w1_out[...] = (0.5 * w1_ref[...].astype(jnp.float32)).T.astype(jnp.bfloat16)
     w2_out[...] = (0.5 * w2_ref[...].astype(jnp.float32)).T.astype(jnp.bfloat16)
 
 
-def chemistry_kernel(groups, early, list_ref, w1_ref, w2_ref, w3_ref, hits_in, *refs):
+def chemistry_kernel(
+    groups, early, list_ref, w1_ref, w2_ref, w3_ref, known_ref, even_ref, *refs
+):
     parts, edges, refs = refs[:groups], refs[groups : groups + len(early)], refs[groups + len(early) :]
-    out_ref, share_ref, state_ref, picked_ref, hits_ref, held_ref, done = refs
+    out_ref, share_ref, state_ref, picked_ref, held_ref, done = refs
     species, cells = state_ref.shape[1:]
     slots = list_ref.shape[0]
     blocks = cells // BLK
@@ -241,9 +249,6 @@
     def _():
         for k, edge in zip(early, edges):
             state_ref[source(k), :, cells - narrow :] = edge[:, wide - narrow :]
-
-    naming = pltpu.make_async_copy(hits_in, hits_ref, done.at[2])
-    naming.start()
 
     def place(j):
         return pl.ds(pl.multiple_of(jnp.minimum(list_ref[j], blocks - 1) * BLK, BLK), BLK)
@@ -271,11 +276,10 @@
             state_ref[g, :, place(j)] = jnp.where(valid, fresh, now).astype(jnp.bfloat16)
     whole = pltpu.make_async_copy(state_ref, out_ref, done.at[1])
     whole.start()
-    naming.wait()
-    lane = lax.broadcasted_iota(jnp.int32, hits_ref.shape, 1)
-    mine = jnp.where(lane == lax.axis_index("tile"), hits_ref[...], 0.0)
-    mine = jnp.sum(mine, axis=0, keepdims=True)
-    held_ref[...] = jnp.sum(mine, axis=1, keepdims=True) / RECV
+    hits = known_ref[...] + even_ref[...]
+    tile = lax.broadcasted_iota(jnp.int32, hits.shape, 0)
+    mine = jnp.where(tile == lax.axis_index("tile"), hits, 0.0)
+    held_ref[...] = jnp.sum(mine, axis=0, keepdims=True)[:, 0:1] / RECV
     share = pltpu.make_async_copy(held_ref, share_ref, done.at[0])
     share.start()
     share.wait()
@@ -309,36 +313,46 @@
     halves = cols // LANES
     f32, bf16 = jnp.float32, jnp.bfloat16
     params = pltpu.CompilerParams(vmem_limit_bytes=VMEM_BYTES)
-    size = halves * (BEHIND * species + SUB)
-    flag = jax.ShapeDtypeStruct((1, LANES), f32)
-
-    to_even, to_odd, hits, field, rates = pl.pallas_call(
-        functools.partial(pack_kernel, length, halves, cells // BLK),
-        out_shape=[jax.ShapeDtypeStruct((size, LANES), f32)] * 2
-        + [
-            flag,
-            jax.ShapeDtypeStruct((species * length * halves, LANES), f32),
-            jax.ShapeDtypeStruct((length * halves, LANES), f32),
-        ],
-        in_specs=[anywhere()] * 4,
-        out_specs=[vmem()] * 5,
-        scratch_shapes=[
-            pltpu.SMEM((slots,), jnp.int32),
-            pltpu.SMEM((slots,), jnp.int32),
-            pltpu.SemaphoreType.DMA((4,)),
-        ],
-        compiler_params=params,
-        cost_estimate=cost(1.0),
-        name="pack_edges",
-    )(
-        from_hbm(tiled(concentrations, halves).reshape(species * length * halves, LANES)),
-        from_hbm(tiled(courant, halves)),
-        from_hbm(active_blocks.reshape(-1)),
-        from_hbm(dest_tile.reshape(-1)),
-    )
+    size = halves * (BEHIND * species + SUB) + tiles
+    flag = jax.ShapeDtypeStruct((tiles, LANES), f32)
+
     evens = [(t, t ^ 1) for t in range(tiles)]
     odds = [(t, ((t + 1) ^ 1) - 1) for t in range(tiles)]
     odds = [(t, other % tiles) for t, other in odds]
+    other_list = lax.ppermute(active_blocks, "tile", evens)
+    other_dest = lax.ppermute(dest_tile, "tile", evens)
+    sources = [
+        tiled(concentrations, halves).reshape(species * length * halves, LANES),
+        tiled(courant, halves),
+        active_blocks.reshape(1, slots),
+        dest_tile.reshape(1, slots),
+    ]
+    field, rates, listing, targets = pl.pallas_call(
+        load_kernel,
+        out_shape=[jax.ShapeDtypeStruct(x.shape, x.dtype) for x in sources],
+        in_specs=[anywhere()] * 4,
+        out_specs=[vmem()] * 4,
+        scratch_shapes=[pltpu.SemaphoreType.DMA((4,))],
+        compiler_params=params,
+        cost_estimate=cost(1.0),
+        name="load_operands",
+    )(*[from_hbm(x) for x in sources])
+    to_even, to_odd, hits = pl.pallas_call(
+        functools.partial(pack_kernel, length, halves, cells // BLK),
+        out_shape=[jax.ShapeDtypeStruct((size, LANES), f32)] * 2 + [flag],
+        in_specs=[vmem()] * 6,
+        out_specs=[vmem()] * 3,
+        compiler_params=params,
+        cost_estimate=cost(0.1),
+        name="pack_edges",
+    )(
+        field,
+        rates,
+        listing,
+        targets,
+        other_list.reshape(1, slots),
+        other_dest.reshape(1, slots),
+    )
     from_odd = lax.ppermute(to_odd, "tile", odds)
     from_even = lax.ppermute(to_even, "tile", evens)
     block = jax.ShapeDtypeStruct((species, cells), bf16)
@@ -358,45 +372,40 @@
     edge = jax.ShapeDtypeStruct((species, BEHIND * cols), bf16)
     whole = pl.pallas_call(
         functools.partial(edge_kernel, dests, early, late, length, halves),
-        out_shape=[block] * len(late) + [edge] * len(early),
-        in_specs=[vmem()] * (4 + len(late)),
-        out_specs=[vmem()] * dests,
+        out_shape=[block] * len(late) + [edge] * len(early) + [flag] * 2,
+        in_specs=[vmem()] * (5 + len(late)),
+        out_specs=[vmem()] * (dests + 2),
         compiler_params=params,
         cost_estimate=cost(0.1),
         name="edge_rows",
-    )(from_odd, from_even, field, rates, *[blocks[k] for k in late])
-    full, edges = whole[: len(late)], whole[len(late) :]
+    )(from_odd, from_even, hits, field, rates, *[blocks[k] for k in late])
+    full, edges, (known, to_even) = whole[: len(late)], whole[len(late) : dests], whole[dests:]
     received = {k: ring(k, blocks[k]) for k in early}
     received |= {k: ring(k, x) if k else x for k, x in zip(late, full)}
     edges = [ring(k, x) for k, x in zip(early, edges)]
-    hits = lax.all_gather(hits, "tile", axis=0, tiled=True)
-    w1, w2, listing = pl.pallas_call(
+    from_even = lax.ppermute(to_even, "tile", evens)
+    w1, w2 = pl.pallas_call(
         weight_kernel,
-        out_shape=[jax.ShapeDtypeStruct(w.shape[::-1], bf16) for w in (first_weight, middle_weight)]
-        + [jax.ShapeDtypeStruct((1, slots), jnp.int32)],
-        in_specs=[vmem()] * 3 + [anywhere()],
-        out_specs=[vmem()] * 3,
+        out_shape=[jax.ShapeDtypeStruct(w.shape[::-1], bf16) for w in (first_weight, middle_weight)],
+        in_specs=[vmem()] * 2 + [anywhere()],
+        out_specs=[vmem()] * 2,
         compiler_params=params,
         cost_estimate=cost(0.5),
         name="halved_weights",
-    )(first_weight, middle_weight, active_blocks.reshape(1, slots), full[0])
+    )(first_weight, middle_weight, full[0])
     out, load_share = pl.pallas_call(
         functools.partial(chemistry_kernel, dests, early),
         out_shape=[
             jax.ShapeDtypeStruct((dests, species, cells), bf16),
             jax.ShapeDtypeStruct((1, 1), f32),
         ],
-        in_specs=[pl.BlockSpec(memory_space=pltpu.SMEM)]
-        + [vmem()] * 3
-        + [anywhere()]
-        + [vmem()] * (dests + len(early)),
+        in_specs=[pl.BlockSpec(memory_space=pltpu.SMEM)] + [vmem()] * (5 + dests + len(early)),
         out_specs=[anywhere()] * 2,
         scratch_shapes=[
             pltpu.VMEM((dests, species, cells), bf16),
             pltpu.VMEM((dests * species, slots * BLK), f32),
-            pltpu.VMEM((tiles, LANES), f32),
             pltpu.VMEM((1, 1), f32),
-            pltpu.SemaphoreType.DMA((3,)),
+            pltpu.SemaphoreType.DMA((2,)),
         ],
         compiler_params=params,
         cost_estimate=cost(4.0),
@@ -406,7 +415,8 @@
         w1,
         w2,
         last_weight.T,
-        from_hbm(hits),
+        known,
+        from_even,
         *[received[k] for k in range(dests)],
         *edges,
     )

time: 31 us -> 22.5 us (0.73)
  blocking collectives: 9.08 us -> 0 us
  waiting for transfers between devices: 3.97 us -> 4.69 us
  local copies, waits for them, and re-layouts: 0.66 us -> 0.01 us
  starting transfers between devices: 10.2 us -> 10.6 us
    all_gather x1 -> x0, blocking collectives: 9.08 us -> none  [shards(): hits = lax.all_gather(hits, 'tile', axis=0, tiled=True)]
    pallas_call x0 -> x1, Pallas kernels: none -> 1.08 us  [shards(): pl.pallas_call(load_kernel, out_shape=[jax.ShapeDtypeStruct(x.shape, x.dt...]
    pallas_call x1, Pallas kernels: 1.11 us -> 0.08 us  [shards(): pl.pallas_call(functools.partial(pack_kernel, length, halves, cells // BL...]
    unnamed x8 -> x6, local copies, waits for them, and re-layouts: 0.66 us -> 0.01 us
    ppermute x0 -> x2, starting transfers between devices: none -> 0.6 us  [the longest x1 0.52 us: shards(): other_list = lax.ppermute(active_blocks, 'tile', evens)]
    ppermute x4, starting transfers between devices: 6.75 us -> 6.31 us  [ring(): return lax.ppermute(x, 'spec', [(s, (s + k) % dests) for s in range(dests)])]
    ppermute x4, waiting for transfers between devices: 3.96 us -> 4.38 us  [ring(): return lax.ppermute(x, 'spec', [(s, (s + k) % dests) for s in range(dests)])]
  transfers between devices with their start and end apart: 6 -> 9, of which waited for: 1 -> 3; matrix products, arithmetic and copies ran while one was open for 0% -> 0% of each run, Pallas kernels for 3% -> 10%
where the time goes in v7:
time: 22.5 us; the launch traced here: 22.3 us
  starting transfers between devices  10.6 us (47%)
  Pallas kernels  6.33 us (28%)
  waiting for transfers between devices  4.69 us (21%)
  between operations  0.7 us (3%)
    ppermute x4, starting transfers between devices, ring(): return lax.ppermute(x, 'spec', [(s, (s + k) % dests) for s in range(dests)])  6.31 us
    ppermute x4, waiting for transfers between devices, ring(): return lax.ppermute(x, 'spec', [(s, (s + k) % dests) for s in range(dests)])  4.38 us
    pallas_call x1, Pallas kernels, shards(): pl.pallas_call(functools.partial(chemistry_kernel, dests, early), out_sha...  4.09 us
    ppermute x1, starting transfers between devices, shards(): from_odd = lax.ppermute(to_odd, 'tile', odds)  3.66 us
    pallas_call x1, Pallas kernels, shards(): pl.pallas_call(load_kernel, out_shape=[jax.ShapeDtypeStruct(x.shape, x.dt...  1.08 us
    pallas_call x1, Pallas kernels, shards(): pl.pallas_call(functools.partial(inner_kernel, dests, length, halves), ou...  0.67 us
    ppermute x1, starting transfers between devices, shards(): other_list = lax.ppermute(active_blocks, 'tile', evens)  0.52 us
  transfers between devices with their start and end apart: 9, of which 3 were waited for; matrix products, arithmetic and copies ran while one was open for 0% of the time, Pallas kernels for 10%

profile of v7, /device:TPU:0, one launch (start us, length us, event | category | flops | bytes accessed | tf_op | source)
XLA Modules:
  0.0 22.3 jit_solution(5075580369837966291)
XLA Ops:
  0.6 0.5 %collective-permute-start = (s32[1,1,16]{2,1,0:T(1,128)}, s32[1,1,16]{2,1,0:T(1,128)S(1)}, u32[]{:S(2)}, u32[]{:S(2)}) collective-permute-start(s32[1,1,16]{2,1,0:T(1,128)} %param.12), channel_id=1, source_target_pairs={{0,4},{4,0},{8,12},{12,8},{16,20},{20,16},{24,28},{28,24},{1,5},{5... | collective-permute-start | bytes 200 | tf_op jit(solution)/shard_map/ppermute | solution.py:322
  1.1 0.1 collective-permute-start.1
  1.2 1.1 %load_operands.1 = (f32[1024,128]{1,0:T(8,128)S(1)}, f32[128,128]{1,0:T(8,128)S(1)}, s32[1,16]{1,0:T(1,128)S(1)}, s32[1,16]{1,0:T(1,128)S(1)}) custom-call(f32[1024,128]{1,0:T(8,128)} %bitcast.21, f32[128,128]{1,0:T(8,128)} %bitcast.22, s32[1,16]{1,0:T(1,128)} %bitcast.23, s32[1,16]{1,0:T(1,128)} %bitcast.24), custom_call_target="tpu_custom_call" | custom-call | flops 1000000000 | bytes 3000000 | tf_op jit(solution)/shard_map/load_operands/pallas_call | solution.py:330
  2.3 0.0 collective-permute-done
  2.3 0.1 collective-permute-done.1
  2.4 0.1 pack_edges.1
  2.5 3.7 %collective-permute-start.2 = (f32[88,128]{1,0:T(8,128)S(1)}, f32[88,128]{1,0:T(8,128)S(1)}, u32[]{:S(2)}, u32[]{:S(2)}) collective-permute-start(f32[88,128]{1,0:T(8,128)S(1)} %get-tuple-element.27), channel_id=1, source_target_pairs={{0,28},{4,8},{8,4},{12,16},{16,12},{20,24},{24,20},{28,0},{1,29},{... | collective-permute-start | bytes 135176 | tf_op jit(solution)/shard_map/ppermute | solution.py:356
  6.1 0.0 collective-permute-start.3
  6.2 0.7 %inner_rows.1 = (bf16[8,4096]{1,0:T(8,128)(2,1)S(1)}, bf16[8,4096]{1,0:T(8,128)(2,1)S(1)}, bf16[8,4096]{1,0:T(8,128)(2,1)S(1)}, bf16[8,4096]{1,0:T(8,128)(2,1)S(1)}) custom-call(f32[1024,128]{1,0:T(8,128)S(1)} %get-tuple-element.24.q_ref, f32[128,128]{1,0:T(8,128)S(1)} %get-tuple-element.25.rates_ref), custom_call_target="tpu_custom_call" | custom-call | flops 1000000000 | bytes 3000000 | tf_op jit(solution)/shard_map/inner_rows/pallas_call | solution.py:359
  6.8 0.0 copy-start
  6.8 1.6 %collective-permute-start.5 = (bf16[8,4096]{1,0:T(8,128)(2,1)S(1)}, bf16[8,4096]{1,0:T(8,128)(2,1)S(1)}, u32[]{:S(2)}, u32[]{:S(2)}) collective-permute-start(bf16[8,4096]{1,0:T(8,128)(2,1)S(1)} %get-tuple-element.38), channel_id=1, source_target_pairs={{0,1},{1,2},{2,3},{3,0},{4,5},{5,6},{6,7},{7,4},{8,9},{9,10},{10,1... | collective-permute-start | bytes 196616 | tf_op jit(solution)/shard_map/ppermute | solution.py:369
  8.5 0.0 collective-permute-done.2.odd_ref
  8.5 0.0 collective-permute-done.3.even_ref
  8.5 0.0 copy-start.1
  8.5 0.2 edge_rows.1
  8.6 2.7 %collective-permute-start.6 = (bf16[8,4096]{1,0:T(8,128)(2,1)S(1)}, bf16[8,4096]{1,0:T(8,128)(2,1)S(1)}, u32[]{:S(2)}, u32[]{:S(2)}) collective-permute-start(bf16[8,4096]{1,0:T(8,128)(2,1)S(1)} %get-tuple-element.39), channel_id=1, source_target_pairs={{0,2},{1,3},{2,0},{3,1},{4,6},{5,7},{6,4},{7,5},{8,10},{9,11},{10,... | collective-permute-start | bytes 196616 | tf_op jit(solution)/shard_map/ppermute | solution.py:369
  11.3 1.3 %collective-permute-start.7 = (bf16[8,4096]{1,0:T(8,128)(2,1)S(1)}, bf16[8,4096]{1,0:T(8,128)(2,1)S(1)}, u32[]{:S(2)}, u32[]{:S(2)}) collective-permute-start(bf16[8,4096]{1,0:T(8,128)(2,1)S(1)} %get-tuple-element.40), channel_id=1, source_target_pairs={{0,3},{1,0},{2,1},{3,2},{4,7},{5,4},{6,5},{7,6},{8,11},{9,8},{10,9... | collective-permute-start | bytes 196616 | tf_op jit(solution)/shard_map/ppermute | solution.py:369
  12.6 0.0 collective-permute-start.4
  12.6 0.7 %collective-permute-start.8 = (bf16[8,1024]{1,0:T(8,128)(2,1)S(1)}, bf16[8,1024]{1,0:T(8,128)(2,1)S(1)}, u32[]{:S(2)}, u32[]{:S(2)}) collective-permute-start(bf16[8,1024]{1,0:T(8,128)(2,1)S(1)} %get-tuple-element.41), channel_id=1, source_target_pairs={{0,1},{1,2},{2,3},{3,0},{4,5},{5,6},{6,7},{7,4},{8,9},{9,10},{10,1... | collective-permute-start | bytes 49160 | tf_op jit(solution)/shard_map/ppermute | solution.py:369
  13.3 0.0 copy-done
  13.3 0.0 copy-done.1
  13.3 0.0 copy-start.2
  13.3 0.2 %halved_weights.1 = (bf16[512,32]{1,0:T(8,128)(2,1)S(1)}, bf16[512,512]{1,0:T(8,128)(2,1)S(1)}) custom-call(bf16[32,512]{1,0:T(8,128)(2,1)S(1)} %copy-done.1, bf16[512,512]{1,0:T(8,128)(2,1)S(1)} %copy-done, bf16[8,4096]{1,0:T(8,128)(2,1)S(1)} %get-tuple-element.33.after_ref.refs_0_), custom_call_target="tpu_custom_call" | custom-call | flops 500000000 | bytes 1500000 | tf_op jit(solution)/shard_map/halved_weights/pallas_call | solution.py:387
  13.6 0.2 %collective-permute-done.4.even_ref = f32[8,128]{1,0:T(8,128)S(1)} collective-permute-done((f32[8,128]{1,0:T(8,128)S(1)}, f32[8,128]{1,0:T(8,128)S(1)}, u32[]{:S(2)}, u32[]{:S(2)}) %collective-permute-start.4) | collective-permute-done | bytes 4128 | tf_op jit(solution)/shard_map/ppermute | solution.py:386
  13.8 4.4 %collective-permute-done.8.refs_4_ = bf16[8,1024]{1,0:T(8,128)(2,1)S(1)} collective-permute-done((bf16[8,1024]{1,0:T(8,128)(2,1)S(1)}, bf16[8,1024]{1,0:T(8,128)(2,1)S(1)}, u32[]{:S(2)}, u32[]{:S(2)}) %collective-permute-start.8) | collective-permute-done | bytes 16416 | tf_op jit(solution)/shard_map/ppermute | solution.py:369
  18.2 0.0 collective-permute-done.5.refs_1_
  18.2 0.0 collective-permute-done.6.refs_2_
  18.2 0.0 collective-permute-done.7.refs_3_
  18.2 0.0 copy-done.2
  18.2 4.1 %chemistry.1 = (bf16[4,8,4096]{2,1,0:T(8,128)(2,1)}, f32[1,1]{1,0:T(1,128)}) custom-call(s32[16]{0:T(128)S(1)} %bitcast.17, bf16[512,32]{1,0:T(8,128)(2,1)S(1)} %get-tuple-element.34.w1_ref, bf16[512,512]{1,0:T(8,128)(2,1)S(1)} %get-tuple-element.35.w2_ref, bf16[32,512]{1,0:T(8,128)(2,1)S(1)} %bitcast.20, f32[8,128]{1,0:T(8,128)S(1)} %get-tuple-element.36.known_ref, ...), custom_call_target="tpu_custom_call" | custom-call | flops 4000000000 | bytes 12000000 | tf_op jit(solution)/shard_map/chemistry/pallas_call | solution.py:396
Async XLA Ops:
  0.6 1.7 %collective-permute-start = (s32[1,1,16]{2,1,0:T(1,128)}, s32[1,1,16]{2,1,0:T(1,128)S(1)}, u32[]{:S(2)}, u32[]{:S(2)}) collective-permute-start(s32[1,1,16]{2,1,0:T(1,128)} %param.12), channel_id=1, source_target_pairs={{0,4},{4,0},{8,12},{12,8},{16,20},{20,16},{24,28},{28,24},{1,5},{5... | collective-permute-start | bytes 200 | tf_op jit(solution)/shard_map/ppermute | solution.py:322
  1.1 1.3 %collective-permute-start.1 = (s32[1,1,16]{2,1,0:T(1,128)}, s32[1,1,16]{2,1,0:T(1,128)S(1)}, u32[]{:S(2)}, u32[]{:S(2)}) collective-permute-start(s32[1,1,16]{2,1,0:T(1,128)} %param.13), channel_id=1, source_target_pairs={{0,4},{4,0},{8,12},{12,8},{16,20},{20,16},{24,28},{28,24},{1,5},{5... | collective-permute-start | bytes 200 | tf_op jit(solution)/shard_map/ppermute | solution.py:323
  2.5 6.0 %collective-permute-start.2 = (f32[88,128]{1,0:T(8,128)S(1)}, f32[88,128]{1,0:T(8,128)S(1)}, u32[]{:S(2)}, u32[]{:S(2)}) collective-permute-start(f32[88,128]{1,0:T(8,128)S(1)} %get-tuple-element.27), channel_id=1, source_target_pairs={{0,28},{4,8},{8,4},{12,16},{16,12},{20,24},{24,20},{28,0},{1,29},{... | collective-permute-start | bytes 135176 | tf_op jit(solution)/shard_map/ppermute | solution.py:356
  6.1 2.3 %collective-permute-start.3 = (f32[88,128]{1,0:T(8,128)S(1)}, f32[88,128]{1,0:T(8,128)S(1)}, u32[]{:S(2)}, u32[]{:S(2)}) collective-permute-start(f32[88,128]{1,0:T(8,128)S(1)} %get-tuple-element.28), channel_id=1, source_target_pairs={{0,4},{4,0},{8,12},{12,8},{16,20},{20,16},{24,28},{28,24},{1,5},{5... | collective-permute-start | bytes 135176 | tf_op jit(solution)/shard_map/ppermute | solution.py:357
  6.8 6.5 %copy-start = (bf16[512,512]{1,0:T(8,128)(2,1)S(1)}, bf16[512,512]{1,0:T(8,128)(2,1)}, u32[]{:S(2)}) copy-start(bf16[512,512]{1,0:T(8,128)(2,1)} %w2_ref.1) | copy-start | bytes 1572868
  6.8 11.3 %collective-permute-start.5 = (bf16[8,4096]{1,0:T(8,128)(2,1)S(1)}, bf16[8,4096]{1,0:T(8,128)(2,1)S(1)}, u32[]{:S(2)}, u32[]{:S(2)}) collective-permute-start(bf16[8,4096]{1,0:T(8,128)(2,1)S(1)} %get-tuple-element.38), channel_id=1, source_target_pairs={{0,1},{1,2},{2,3},{3,0},{4,5},{5,6},{6,7},{7,4},{8,9},{9,10},{10,1... | collective-permute-start | bytes 196616 | tf_op jit(solution)/shard_map/ppermute | solution.py:369
  8.5 4.9 %copy-start.1 = (bf16[32,512]{1,0:T(8,128)(2,1)S(1)}, bf16[32,512]{1,0:T(8,128)(2,1)}, u32[]{:S(2)}) copy-start(bf16[32,512]{1,0:T(8,128)(2,1)} %w1_ref.1) | copy-start | bytes 98308
  8.6 9.5 %collective-permute-start.6 = (bf16[8,4096]{1,0:T(8,128)(2,1)S(1)}, bf16[8,4096]{1,0:T(8,128)(2,1)S(1)}, u32[]{:S(2)}, u32[]{:S(2)}) collective-permute-start(bf16[8,4096]{1,0:T(8,128)(2,1)S(1)} %get-tuple-element.39), channel_id=1, source_target_pairs={{0,2},{1,3},{2,0},{3,1},{4,6},{5,7},{6,4},{7,5},{8,10},{9,11},{10,... | collective-permute-start | bytes 196616 | tf_op jit(solution)/shard_map/ppermute | solution.py:369
  11.3 6.9 %collective-permute-start.7 = (bf16[8,4096]{1,0:T(8,128)(2,1)S(1)}, bf16[8,4096]{1,0:T(8,128)(2,1)S(1)}, u32[]{:S(2)}, u32[]{:S(2)}) collective-permute-start(bf16[8,4096]{1,0:T(8,128)(2,1)S(1)} %get-tuple-element.40), channel_id=1, source_target_pairs={{0,3},{1,0},{2,1},{3,2},{4,7},{5,4},{6,5},{7,6},{8,11},{9,8},{10,9... | collective-permute-start | bytes 196616 | tf_op jit(solution)/shard_map/ppermute | solution.py:369
  12.6 1.2 %collective-permute-start.4 = (f32[8,128]{1,0:T(8,128)S(1)}, f32[8,128]{1,0:T(8,128)S(1)}, u32[]{:S(2)}, u32[]{:S(2)}) collective-permute-start(f32[8,128]{1,0:T(8,128)S(1)} %get-tuple-element.37), channel_id=1, source_target_pairs={{0,4},{4,0},{8,12},{12,8},{16,20},{20,16},{24,28},{28,24},{1,5},{5... | collective-permute-start | bytes 12296 | tf_op jit(solution)/shard_map/ppermute | solution.py:386
  12.6 5.5 %collective-permute-start.8 = (bf16[8,1024]{1,0:T(8,128)(2,1)S(1)}, bf16[8,1024]{1,0:T(8,128)(2,1)S(1)}, u32[]{:S(2)}, u32[]{:S(2)}) collective-permute-start(bf16[8,1024]{1,0:T(8,128)(2,1)S(1)} %get-tuple-element.41), channel_id=1, source_target_pairs={{0,1},{1,2},{2,3},{3,0},{4,5},{5,6},{6,7},{7,4},{8,9},{9,10},{10,1... | collective-permute-start | bytes 49160 | tf_op jit(solution)/shard_map/ppermute | solution.py:369
  13.3 4.9 %copy-start.2 = (bf16[512,32]{0,1:T(8,128)(2,1)S(1)}, bf16[512,32]{0,1:T(8,128)(2,1)}, u32[]{:S(2)}) copy-start(bf16[512,32]{0,1:T(8,128)(2,1)} %param.11) | copy-start | bytes 98308

commit v8 on v5

--- a/solution.py
+++ b/solution.py
@@ -17,6 +17,7 @@
 
 
 def silu_of_half(half):
+    half = half.astype(jnp.bfloat16)
     return half + half * jnp.tanh(half)
 
 
@@ -57,48 +58,53 @@
 
 def pack_kernel(
     length, halves, blocks, q_in, rates_in, list_in, dest_in,
-    even_ref, odd_ref, hits_ref, q_ref, rates_ref, list_ref, dest_ref, arrived,
+    even_ref, odd_ref, hits_ref, low_ref, high_ref, rates_ref, list_ref, dest_ref, arrived,
 ):
-    pairs = [(q_in, q_ref), (rates_in, rates_ref), (list_in, list_ref), (dest_in, dest_ref)]
+    species, rows = q_in.shape[:2]
+    tile = halves * SUB
+    part = BEHIND * species + SUB
+    shape = (species, tile, LANES)
+    pairs = [
+        (q_in.at[:, rows - tile :], high_ref.reshape(shape)),
+        (q_in.at[:, :tile], low_ref.reshape(shape)),
+        (rates_in.at[rows - tile :], rates_ref.at[tile:]),
+        (rates_in.at[:tile], rates_ref.at[:tile]),
+        (list_in, list_ref),
+        (dest_in, dest_ref),
+    ]
     copies = [
         pltpu.make_async_copy(source, target, arrived.at[i])
         for i, (source, target) in enumerate(pairs)
     ]
     for copy in copies:
         copy.start()
-    species = q_ref.shape[0] // (length * halves)
-    part = BEHIND * species + SUB
-
-    def row(at, half):
-        return q_ref[pl.ds(spot(at, half, halves), species, stride=length * halves), :]
-
-    copies[2].wait()
-    copies[3].wait()
+    copies[4].wait()
+    copies[5].wait()
     lane = lax.broadcasted_iota(jnp.int32, (SUB, LANES), 1)
     hits = jnp.zeros((SUB, LANES), jnp.float32)
     for j in range(list_ref.shape[0]):
         target = jnp.where(list_ref[j] < blocks, dest_ref[j], -1)
         hits = hits + jnp.where(lane == target, 1.0, 0.0)
     hits_ref[...] = hits
-    copies[1].wait()
-    copies[0].wait()
+    for copy in copies[:4]:
+        copy.wait()
 
     def write(up_ref, down_ref):
         for half in range(halves):
             start = half * part
             for j in range(BEHIND):
-                up_ref[start + j * species : start + (j + 1) * species, :] = row(
-                    length - BEHIND + j, half
-                )
-            for j in range(AHEAD):
-                down_ref[start + j * species : start + (j + 1) * species, :] = row(j, half)
-            for j in range(AHEAD, BEHIND):
-                down_ref[start + j * species : start + (j + 1) * species, :] = jnp.zeros(
-                    (species, LANES), jnp.float32
-                )
-            high, low = spot(length - SUB, half, halves), spot(0, half, halves)
-            up_ref[start + BEHIND * species : start + part, :] = rates_ref[high : high + SUB, :]
-            down_ref[start + BEHIND * species : start + part, :] = rates_ref[low : low + SUB, :]
+                at = start + j * species
+                up_ref[at : at + species, :] = high_ref[
+                    pl.ds(half * SUB + SUB - BEHIND + j, species, stride=tile), :
+                ]
+                if j < AHEAD:
+                    value = low_ref[pl.ds(half * SUB + j, species, stride=tile), :]
+                else:
+                    value = jnp.zeros((species, LANES), jnp.float32)
+                down_ref[at : at + species, :] = value
+            at = start + BEHIND * species
+            up_ref[at : at + SUB, :] = rates_ref[tile + half * SUB : tile + (half + 1) * SUB, :]
+            down_ref[at : at + SUB, :] = rates_ref[half * SUB : (half + 1) * SUB, :]
         up_ref[halves * part :, :] = hits
         down_ref[halves * part :, :] = hits
 
@@ -244,9 +250,9 @@
     for first in range(0, slots, each):
         x = picked_ref[:, first * BLK : (first + each) * BLK]
         hidden = jnp.dot(w1_ref[...], x.astype(jnp.bfloat16), preferred_element_type=jnp.float32)
-        hidden = silu_of_half(hidden).astype(jnp.bfloat16)
+        hidden = silu_of_half(hidden)
         hidden = jnp.dot(w2_ref[...], hidden, preferred_element_type=jnp.float32)
-        hidden = silu_of_half(hidden).astype(jnp.bfloat16)
+        hidden = silu_of_half(hidden)
         picked_ref[:, first * BLK : (first + each) * BLK] = x + jnp.dot(
             w3_ref[...], hidden, preferred_element_type=jnp.float32
         )
@@ -292,30 +298,30 @@
     size = halves * (BEHIND * species + SUB) + SUB
     flag = jax.ShapeDtypeStruct((SUB, LANES), f32)
 
-    to_even, to_odd, hits, field, rates = pl.pallas_call(
+    field, rates = tiled(concentrations, halves), tiled(courant, halves)
+    to_even, to_odd, hits = pl.pallas_call(
         functools.partial(pack_kernel, length, halves, cells // BLK),
-        out_shape=[jax.ShapeDtypeStruct((size, LANES), f32)] * 2
-        + [
-            flag,
-            jax.ShapeDtypeStruct((species * length * halves, LANES), f32),
-            jax.ShapeDtypeStruct((length * halves, LANES), f32),
-        ],
+        out_shape=[jax.ShapeDtypeStruct((size, LANES), f32)] * 2 + [flag],
         in_specs=[anywhere()] * 4,
-        out_specs=[vmem()] * 5,
+        out_specs=[vmem()] * 3,
         scratch_shapes=[
+            pltpu.VMEM((species * halves * SUB, LANES), f32),
+            pltpu.VMEM((species * halves * SUB, LANES), f32),
+            pltpu.VMEM((2 * halves * SUB, LANES), f32),
             pltpu.SMEM((slots,), jnp.int32),
             pltpu.SMEM((slots,), jnp.int32),
-            pltpu.SemaphoreType.DMA((4,)),
+            pltpu.SemaphoreType.DMA((6,)),
         ],
         compiler_params=params,
         cost_estimate=cost(1.0),
         name="pack_edges",
     )(
-        from_hbm(tiled(concentrations, halves).reshape(species * length * halves, LANES)),
-        from_hbm(tiled(courant, halves)),
+        from_hbm(field),
+        from_hbm(rates),
         from_hbm(active_blocks.reshape(-1)),
         from_hbm(dest_tile.reshape(-1)),
     )
+    field = field.reshape(species * length * halves, LANES)
     evens = [(t, t ^ 1) for t in range(tiles)]
     odds = [(t, ((t + 1) ^ 1) - 1) for t in range(tiles)]
     odds = [(t, other % tiles) for t, other in odds]

time: 21.9 us -> 21.9 us (level)
    unnamed x8 -> x12, local copies, waits for them, and re-layouts: 0.66 us -> 0.67 us
where the time goes in v8:
time: 21.9 us; the launch traced here: 21.7 us
  starting transfers between devices  10.8 us (49%)
  Pallas kernels  6.15 us (28%)
  waiting for transfers between devices  3.38 us (15%)
  between operations  0.72 us (3%)
  local copies, waits for them, and re-layouts  0.67 us (3%)
    ppermute x3, starting transfers between devices, shards(): lax.ppermute(blocks[k], 'spec', [(s, (s + k) % dests) for s in range(dest...  6.7 us
    ppermute x2, starting transfers between devices, shards(): from_odd = lax.ppermute(to_odd, 'tile', odds)  4.07 us
    pallas_call x1, Pallas kernels, shards(): pl.pallas_call(functools.partial(chemistry_kernel, dests), out_shape=[jax...  4.06 us
    ppermute x2, waiting for transfers between devices, shards(): from_odd = lax.ppermute(to_odd, 'tile', odds)  3.37 us
    pallas_call x1, Pallas kernels, shards(): pl.pallas_call(functools.partial(pack_kernel, length, halves, cells // BL...  1.01 us
    pallas_call x1, Pallas kernels, shards(): pl.pallas_call(functools.partial(inner_kernel, dests, length, halves), ou...  0.69 us
    unnamed x12, local copies, waits for them, and re-layouts  0.67 us
  transfers between devices with their start and end apart: 7, of which 2 were waited for; matrix products, arithmetic and copies ran while one was open for 0% of the time, Pallas kernels for 4%

profile of v8, /device:TPU:0, one launch (start us, length us, event | category | flops | bytes accessed | tf_op | source)
XLA Modules:
  0.0 21.7 jit_solution(8045497672303650344)
XLA Ops:
  0.6 0.0 copy-start
  0.6 0.0 copy-start.1
  0.6 1.0 %pack_edges.1 = (f32[88,128]{1,0:T(8,128)S(1)}, f32[88,128]{1,0:T(8,128)S(1)}, f32[8,128]{1,0:T(8,128)S(1)}) custom-call(f32[8,128,128]{2,1,0:T(8,128)} %bitcast.18, f32[128,128]{1,0:T(8,128)} %bitcast.21, s32[16]{0:T(128)} %bitcast.25, s32[16]{0:T(128)} %bitcast.28), custom_call_target="tpu_custom_call" | custom-call | flops 1000000000 | bytes 3000000 | tf_op jit(solution)/shard_map/pack_edges/pallas_call | solution.py:302
  1.7 3.4 %collective-permute-start = (f32[88,128]{1,0:T(8,128)S(1)}, f32[88,128]{1,0:T(8,128)S(1)}, u32[]{:S(2)}, u32[]{:S(2)}) collective-permute-start(f32[88,128]{1,0:T(8,128)S(1)} %get-tuple-element.21), channel_id=1, source_target_pairs={{0,28},{4,8},{8,4},{12,16},{16,12},{20,24},{24,20},{28,0},{1,29},{... | collective-permute-start | bytes 135176 | tf_op jit(solution)/shard_map/ppermute | solution.py:328
  5.1 0.0 collective-permute-start.1
  5.1 0.0 copy-done
  5.1 0.0 copy-done.1
  5.1 0.7 %inner_rows.1 = (bf16[8,4096]{1,0:T(8,128)(2,1)S(1)}, bf16[8,4096]{1,0:T(8,128)(2,1)S(1)}, bf16[8,4096]{1,0:T(8,128)(2,1)S(1)}, bf16[8,4096]{1,0:T(8,128)(2,1)S(1)}) custom-call(f32[1024,128]{1,0:T(8,128)S(1)} %bitcast.19, f32[128,128]{1,0:T(8,128)S(1)} %bitcast.22), custom_call_target="tpu_custom_call" | custom-call | flops 1000000000 | bytes 3000000 | tf_op jit(solution)/shard_map/inner_rows/pallas_call | solution.py:331
  5.8 0.0 copy-start.2
  5.8 1.0 %collective-permute-done.odd_ref = f32[88,128]{1,0:T(8,128)S(1)} collective-permute-done((f32[88,128]{1,0:T(8,128)S(1)}, f32[88,128]{1,0:T(8,128)S(1)}, u32[]{:S(2)}, u32[]{:S(2)}) %collective-permute-start) | collective-permute-done | bytes 45088 | tf_op jit(solution)/shard_map/ppermute | solution.py:328
  6.8 0.0 collective-permute-done.1.even_ref
  6.8 0.0 copy-start.3
  6.8 0.2 edge_rows.1
  7.0 2.8 %collective-permute-start.4 = (bf16[8,4096]{1,0:T(8,128)(2,1)S(1)}, bf16[8,4096]{1,0:T(8,128)(2,1)S(1)}, u32[]{:S(2)}, u32[]{:S(2)}) collective-permute-start(bf16[8,4096]{1,0:T(8,128)(2,1)S(1)} %get-tuple-element.35), channel_id=1, source_target_pairs={{0,1},{1,2},{2,3},{3,0},{4,5},{5,6},{6,7},{7,4},{8,9},{9,10},{10,1... | collective-permute-start | bytes 196616 | tf_op jit(solution)/shard_map/ppermute | solution.py:350
  9.7 2.6 %collective-permute-start.5 = (bf16[8,4096]{1,0:T(8,128)(2,1)S(1)}, bf16[8,4096]{1,0:T(8,128)(2,1)S(1)}, u32[]{:S(2)}, u32[]{:S(2)}) collective-permute-start(bf16[8,4096]{1,0:T(8,128)(2,1)S(1)} %get-tuple-element.36), channel_id=1, source_target_pairs={{0,2},{1,3},{2,0},{3,1},{4,6},{5,7},{6,4},{7,5},{8,10},{9,11},{10,... | collective-permute-start | bytes 196616 | tf_op jit(solution)/shard_map/ppermute | solution.py:350
  12.3 1.3 %collective-permute-start.6 = (bf16[8,4096]{1,0:T(8,128)(2,1)S(1)}, bf16[8,4096]{1,0:T(8,128)(2,1)S(1)}, u32[]{:S(2)}, u32[]{:S(2)}) collective-permute-start(bf16[8,4096]{1,0:T(8,128)(2,1)S(1)} %get-tuple-element.37), channel_id=1, source_target_pairs={{0,3},{1,0},{2,1},{3,2},{4,7},{5,4},{6,5},{7,6},{8,11},{9,8},{10,9... | collective-permute-start | bytes 196616 | tf_op jit(solution)/shard_map/ppermute | solution.py:350
  13.7 0.7 %collective-permute-start.2 = (f32[8,128]{1,0:T(8,128)S(1)}, f32[8,128]{1,0:T(8,128)S(1)}, u32[]{:S(2)}, u32[]{:S(2)}) collective-permute-start(f32[8,128]{1,0:T(8,128)S(1)} %get-tuple-element.32), channel_id=1, source_target_pairs={{0,28},{4,8},{8,4},{12,16},{16,12},{20,24},{24,20},{28,0},{1,29},{... | collective-permute-start | bytes 12296 | tf_op jit(solution)/shard_map/ppermute | solution.py:353
  14.3 0.0 collective-permute-start.3
  14.3 0.0 copy-start.5
  14.3 0.0 copy-done.2
  14.3 0.0 copy-done.3
  14.3 0.6 %copy-done.5 = s32[1,1,16]{2,1,0:T(1,128)S(1)} copy-done((s32[1,1,16]{2,1,0:T(1,128)S(1)}, s32[1,1,16]{2,1,0:T(1,128)}, u32[]{:S(2)}) %copy-start.5) | copy-done | bytes 88
  15.0 0.0 copy-start.4
  15.0 0.2 %halved_weights.1 = (bf16[512,32]{1,0:T(8,128)(2,1)S(1)}, bf16[512,512]{1,0:T(8,128)(2,1)S(1)}, s32[1,16]{1,0:T(1,128)S(1)}) custom-call(bf16[32,512]{1,0:T(8,128)(2,1)S(1)} %copy-done.3, bf16[512,512]{1,0:T(8,128)(2,1)S(1)} %copy-done.2, s32[1,16]{1,0:T(1,128)S(1)} %bitcast.26, f32[8,128]{1,0:T(8,128)S(1)} %get-tuple-element.28.after_ref.known_ref), custom_call_target="tpu_custom_call" | custom-call | flops 500000000 | bytes 1500000 | tf_op jit(solution)/shard_map/halved_weights/pallas_call | solution.py:355
  15.2 2.4 %collective-permute-done.2.odd_ref = f32[8,128]{1,0:T(8,128)S(1)} collective-permute-done((f32[8,128]{1,0:T(8,128)S(1)}, f32[8,128]{1,0:T(8,128)S(1)}, u32[]{:S(2)}, u32[]{:S(2)}) %collective-permute-start.2) | collective-permute-done | bytes 4128 | tf_op jit(solution)/shard_map/ppermute | solution.py:353
  17.6 0.0 collective-permute-done.3.even_ref
  17.6 0.0 collective-permute-done.4.refs_1_
  17.6 0.0 collective-permute-done.5.refs_2_
  17.6 0.0 collective-permute-done.6.refs_3_
  17.6 0.0 copy-done.4
  17.6 4.1 %chemistry.1 = (bf16[4,8,4096]{2,1,0:T(8,128)(2,1)}, f32[1,1]{1,0:T(1,128)}) custom-call(s32[16]{0:T(128)S(1)} %bitcast.27, bf16[512,32]{1,0:T(8,128)(2,1)S(1)} %get-tuple-element.30.w1_ref, bf16[512,512]{1,0:T(8,128)(2,1)S(1)} %get-tuple-element.31.w2_ref, bf16[32,512]{1,0:T(8,128)(2,1)S(1)} %bitcast.24, ...), custom_call_target="tpu_custom_call" | custom-call | flops 4000000000 | bytes 12000000 | tf_op jit(solution)/shard_map/chemistry/pallas_call | solution.py:365
Async XLA Ops:
  0.6 4.4 %copy-start = (f32[8,64,256]{2,1,0:T(8,128)S(1)}, f32[8,64,256]{2,1,0:T(8,128)}, u32[]{:S(2)}) copy-start(f32[8,64,256]{2,1,0:T(8,128)} %param.7) | copy-start | bytes 1572868
  0.6 4.4 %copy-start.1 = (f32[64,256]{1,0:T(8,128)S(1)}, f32[64,256]{1,0:T(8,128)}, u32[]{:S(2)}) copy-start(f32[64,256]{1,0:T(8,128)} %param.8) | copy-start | bytes 196612
  1.7 5.1 %collective-permute-start = (f32[88,128]{1,0:T(8,128)S(1)}, f32[88,128]{1,0:T(8,128)S(1)}, u32[]{:S(2)}, u32[]{:S(2)}) collective-permute-start(f32[88,128]{1,0:T(8,128)S(1)} %get-tuple-element.21), channel_id=1, source_target_pairs={{0,28},{4,8},{8,4},{12,16},{16,12},{20,24},{24,20},{28,0},{1,29},{... | collective-permute-start | bytes 135176 | tf_op jit(solution)/shard_map/ppermute | solution.py:328
  5.1 1.7 %collective-permute-start.1 = (f32[88,128]{1,0:T(8,128)S(1)}, f32[88,128]{1,0:T(8,128)S(1)}, u32[]{:S(2)}, u32[]{:S(2)}) collective-permute-start(f32[88,128]{1,0:T(8,128)S(1)} %get-tuple-element.22), channel_id=1, source_target_pairs={{0,4},{4,0},{8,12},{12,8},{16,20},{20,16},{24,28},{28,24},{1,5},{5... | collective-permute-start | bytes 135176 | tf_op jit(solution)/shard_map/ppermute | solution.py:329
  5.8 8.6 %copy-start.2 = (bf16[512,512]{1,0:T(8,128)(2,1)S(1)}, bf16[512,512]{1,0:T(8,128)(2,1)}, u32[]{:S(2)}) copy-start(bf16[512,512]{1,0:T(8,128)(2,1)} %w2_ref.1) | copy-start | bytes 1572868
  6.8 7.5 %copy-start.3 = (bf16[32,512]{1,0:T(8,128)(2,1)S(1)}, bf16[32,512]{1,0:T(8,128)(2,1)}, u32[]{:S(2)}) copy-start(bf16[32,512]{1,0:T(8,128)(2,1)} %w1_ref.1) | copy-start | bytes 98308
  7.0 10.6 %collective-permute-start.4 = (bf16[8,4096]{1,0:T(8,128)(2,1)S(1)}, bf16[8,4096]{1,0:T(8,128)(2,1)S(1)}, u32[]{:S(2)}, u32[]{:S(2)}) collective-permute-start(bf16[8,4096]{1,0:T(8,128)(2,1)S(1)} %get-tuple-element.35), channel_id=1, source_target_pairs={{0,1},{1,2},{2,3},{3,0},{4,5},{5,6},{6,7},{7,4},{8,9},{9,10},{10,1... | collective-permute-start | bytes 196616 | tf_op jit(solution)/shard_map/ppermute | solution.py:350
  9.7 7.9 %collective-permute-start.5 = (bf16[8,4096]{1,0:T(8,128)(2,1)S(1)}, bf16[8,4096]{1,0:T(8,128)(2,1)S(1)}, u32[]{:S(2)}, u32[]{:S(2)}) collective-permute-start(bf16[8,4096]{1,0:T(8,128)(2,1)S(1)} %get-tuple-element.36), channel_id=1, source_target_pairs={{0,2},{1,3},{2,0},{3,1},{4,6},{5,7},{6,4},{7,5},{8,10},{9,11},{10,... | collective-permute-start | bytes 196616 | tf_op jit(solution)/shard_map/ppermute | solution.py:350
  12.3 5.3 %collective-permute-start.6 = (bf16[8,4096]{1,0:T(8,128)(2,1)S(1)}, bf16[8,4096]{1,0:T(8,128)(2,1)S(1)}, u32[]{:S(2)}, u32[]{:S(2)}) collective-permute-start(bf16[8,4096]{1,0:T(8,128)(2,1)S(1)} %get-tuple-element.37), channel_id=1, source_target_pairs={{0,3},{1,0},{2,1},{3,2},{4,7},{5,4},{6,5},{7,6},{8,11},{9,8},{10,9... | collective-permute-start | bytes 196616 | tf_op jit(solution)/shard_map/ppermute | solution.py:350
  13.7 3.9 %collective-permute-start.2 = (f32[8,128]{1,0:T(8,128)S(1)}, f32[8,128]{1,0:T(8,128)S(1)}, u32[]{:S(2)}, u32[]{:S(2)}) collective-permute-start(f32[8,128]{1,0:T(8,128)S(1)} %get-tuple-element.32), channel_id=1, source_target_pairs={{0,28},{4,8},{8,4},{12,16},{16,12},{20,24},{24,20},{28,0},{1,29},{... | collective-permute-start | bytes 12296 | tf_op jit(solution)/shard_map/ppermute | solution.py:353
  14.3 3.3 %collective-permute-start.3 = (f32[8,128]{1,0:T(8,128)S(1)}, f32[8,128]{1,0:T(8,128)S(1)}, u32[]{:S(2)}, u32[]{:S(2)}) collective-permute-start(f32[8,128]{1,0:T(8,128)S(1)} %get-tuple-element.33), channel_id=1, source_target_pairs={{0,4},{4,0},{8,12},{12,8},{16,20},{20,16},{24,28},{28,24},{1,5},{5... | collective-permute-start | bytes 12296 | tf_op jit(solution)/shard_map/ppermute | solution.py:354
  14.3 0.7 %copy-start.5 = (s32[1,1,16]{2,1,0:T(1,128)S(1)}, s32[1,1,16]{2,1,0:T(1,128)}, u32[]{:S(2)}) copy-start(s32[1,1,16]{2,1,0:T(1,128)} %param.12) | copy-start | bytes 196
  15.0 2.6 %copy-start.4 = (bf16[512,32]{0,1:T(8,128)(2,1)S(1)}, bf16[512,32]{0,1:T(8,128)(2,1)}, u32[]{:S(2)}) copy-start(bf16[512,32]{0,1:T(8,128)(2,1)} %param.11) | copy-start | bytes 98308

commit v9 on v8

--- a/solution.py
+++ b/solution.py
@@ -17,7 +17,6 @@
 
 
 def silu_of_half(half):
-    half = half.astype(jnp.bfloat16)
     return half + half * jnp.tanh(half)
 
 
@@ -215,8 +214,17 @@
                     out_ref[:, at : at + LANES] = value.astype(jnp.bfloat16)
 
 
-def weight_kernel(w1_ref, w2_ref, list_ref, after_ref, w1_out, w2_out, list_out):
-    list_out[...] = list_ref[...]
+def weight_kernel(blocks, w1_ref, w2_ref, list_ref, after_ref, w1_out, w2_out, listed_out):
+    slots = list_ref.shape[0]
+    for j in range(slots + 1):
+        listed_out[j] = blocks
+    count = jnp.int32(0)
+    for j in range(slots):
+        block = list_ref[j]
+        listed_out[count] = block
+        count = count + jnp.where(block < blocks, 1, 0)
+    listed_out[count] = blocks
+    listed_out[slots] = count
     w1_out[...] = (0.5 * w1_ref[...].astype(jnp.float32)).T.astype(jnp.bfloat16)
     w2_out[...] = (0.5 * w2_ref[...].astype(jnp.float32)).T.astype(jnp.bfloat16)
 
@@ -226,7 +234,7 @@
 ):
     parts, (out_ref, share_ref, state_ref, picked_ref, held_ref, done) = refs[:groups], refs[groups:]
     species, cells = state_ref.shape[1:]
-    slots = list_ref.shape[0]
+    slots = list_ref.shape[0] - 1
     blocks = cells // BLK
     me = lax.axis_index("spec")
     for k in range(groups):
@@ -241,27 +249,34 @@
     def place(j):
         return pl.ds(pl.multiple_of(jnp.minimum(list_ref[j], blocks - 1) * BLK, BLK), BLK)
 
-    for j in range(slots):
-        for g in range(groups):
-            picked_ref[g * species : (g + 1) * species, j * BLK : (j + 1) * BLK] = state_ref[
-                g, :, place(j)
-            ].astype(jnp.float32)
+    count = list_ref[slots]
     each = 4
     for first in range(0, slots, each):
-        x = picked_ref[:, first * BLK : (first + each) * BLK]
-        hidden = jnp.dot(w1_ref[...], x.astype(jnp.bfloat16), preferred_element_type=jnp.float32)
-        hidden = silu_of_half(hidden)
-        hidden = jnp.dot(w2_ref[...], hidden, preferred_element_type=jnp.float32)
-        hidden = silu_of_half(hidden)
-        picked_ref[:, first * BLK : (first + each) * BLK] = x + jnp.dot(
-            w3_ref[...], hidden, preferred_element_type=jnp.float32
-        )
-    for j in range(slots):
-        valid = list_ref[j] < blocks
-        for g in range(groups):
-            fresh = picked_ref[g * species : (g + 1) * species, j * BLK : (j + 1) * BLK]
-            now = state_ref[g, :, place(j)].astype(jnp.float32)
-            state_ref[g, :, place(j)] = jnp.where(valid, fresh, now).astype(jnp.bfloat16)
+
+        @pl.when(first < count)
+        def _():
+            for j in range(each):
+                for g in range(groups):
+                    picked_ref[g * species : (g + 1) * species, j * BLK : (j + 1) * BLK] = state_ref[
+                        g, :, place(first + j)
+                    ].astype(jnp.float32)
+            x = picked_ref[...]
+            hidden = jnp.dot(
+                w1_ref[...], x.astype(jnp.bfloat16), preferred_element_type=jnp.float32
+            )
+            hidden = silu_of_half(hidden).astype(jnp.bfloat16)
+            hidden = jnp.dot(w2_ref[...], hidden, preferred_element_type=jnp.float32)
+            hidden = silu_of_half(hidden).astype(jnp.bfloat16)
+            fresh = x + jnp.dot(w3_ref[...], hidden, preferred_element_type=jnp.float32)
+            for j in range(each):
+                valid = first + j < count
+                for g in range(groups):
+                    now = state_ref[g, :, place(first + j)].astype(jnp.float32)
+                    new = fresh[g * species : (g + 1) * species, j * BLK : (j + 1) * BLK]
+                    state_ref[g, :, place(first + j)] = jnp.where(valid, new, now).astype(
+                        jnp.bfloat16
+                    )
+
     whole = pltpu.make_async_copy(state_ref, out_ref, done.at[1])
     whole.start()
     share.wait()
@@ -353,15 +368,15 @@
     from_odd = lax.ppermute(to_odd, "tile", odds)
     from_even = lax.ppermute(to_even, "tile", evens)
     w1, w2, listing = pl.pallas_call(
-        weight_kernel,
+        functools.partial(weight_kernel, cells // BLK),
         out_shape=[jax.ShapeDtypeStruct(w.shape[::-1], bf16) for w in (first_weight, middle_weight)]
-        + [jax.ShapeDtypeStruct((1, slots), jnp.int32)],
-        in_specs=[vmem()] * 3 + [anywhere()],
-        out_specs=[vmem()] * 3,
+        + [jax.ShapeDtypeStruct((slots + 1,), jnp.int32)],
+        in_specs=[vmem()] * 2 + [pl.BlockSpec(memory_space=pltpu.SMEM), anywhere()],
+        out_specs=[vmem()] * 2 + [pl.BlockSpec(memory_space=pltpu.SMEM)],
         compiler_params=params,
         cost_estimate=cost(0.5),
         name="halved_weights",
-    )(first_weight, middle_weight, active_blocks.reshape(1, slots), known)
+    )(first_weight, middle_weight, active_blocks.reshape(-1), known)
     out, load_share = pl.pallas_call(
         functools.partial(chemistry_kernel, dests),
         out_shape=[
@@ -372,7 +387,7 @@
         out_specs=[anywhere()] * 2,
         scratch_shapes=[
             pltpu.VMEM((dests, species, cells), bf16),
-            pltpu.VMEM((dests * species, slots * BLK), f32),
+            pltpu.VMEM((dests * species, 4 * BLK), f32),
             pltpu.VMEM((1, 1), f32),
             pltpu.SemaphoreType.DMA((2,)),
         ],
@@ -380,7 +395,7 @@
         cost_estimate=cost(4.0),
         name="chemistry",
     )(
-        listing.reshape(-1),
+        listing,
         w1,
         w2,
         last_weight.T,

time: 21.9 us -> 20.6 us (0.941)
  waiting for transfers between devices: 3.38 us -> 2.31 us
    pallas_call x1, Pallas kernels: 4.06 us -> 2.95 us  [shards(): pl.pallas_call(functools.partial(chemistry_kernel, dests), out_shape=[jax...]
    pallas_call x1, Pallas kernels: 0.24 us -> 1.31 us  [shards(): pl.pallas_call(functools.partial(weight_kernel, cells // BLK), out_shape=...]
    ppermute x2, waiting for transfers between devices: 3.37 us -> 2.3 us  [shards(): from_odd = lax.ppermute(to_odd, 'tile', odds)]
  transfers between devices with their start and end apart: 7 -> 7, of which waited for: 2 -> 2; matrix products, arithmetic and copies ran while one was open for 0% -> 0% of each run, Pallas kernels for 4% -> 10%
where the time goes in v9:
time: 20.6 us
  starting transfers between devices  10.8 us (52%)
  Pallas kernels  6.11 us (30%)
  waiting for transfers between devices  2.31 us (11%)
  between operations  0.72 us (3%)
  local copies, waits for them, and re-layouts  0.67 us (3%)
    ppermute x3, starting transfers between devices, shards(): lax.ppermute(blocks[k], 'spec', [(s, (s + k) % dests) for s in range(dest...  6.7 us
    ppermute x2, starting transfers between devices, shards(): from_odd = lax.ppermute(to_odd, 'tile', odds)  4.07 us
    pallas_call x1, Pallas kernels, shards(): pl.pallas_call(functools.partial(chemistry_kernel, dests), out_shape=[jax...  2.95 us
    ppermute x2, waiting for transfers between devices, shards(): from_odd = lax.ppermute(to_odd, 'tile', odds)  2.3 us
    pallas_call x1, Pallas kernels, shards(): pl.pallas_call(functools.partial(weight_kernel, cells // BLK), out_shape=...  1.31 us
    pallas_call x1, Pallas kernels, shards(): pl.pallas_call(functools.partial(pack_kernel, length, halves, cells // BL...  1.01 us
    pallas_call x1, Pallas kernels, shards(): pl.pallas_call(functools.partial(inner_kernel, dests, length, halves), ou...  0.69 us
    unnamed x12, local copies, waits for them, and re-layouts  0.67 us
  transfers between devices with their start and end apart: 7, of which 2 were waited for; matrix products, arithmetic and copies ran while one was open for 0% of the time, Pallas kernels for 10%

profile of v9, /device:TPU:0, one launch (start us, length us, event | category | flops | bytes accessed | tf_op | source)
XLA Modules:
  0.0 20.6 jit_solution(15780627038775305348)
XLA Ops:
  0.6 0.0 copy-start
  0.6 0.0 copy-start.1
  0.6 1.0 %pack_edges.1 = (f32[88,128]{1,0:T(8,128)S(1)}, f32[88,128]{1,0:T(8,128)S(1)}, f32[8,128]{1,0:T(8,128)S(1)}) custom-call(f32[8,128,128]{2,1,0:T(8,128)} %bitcast.16, f32[128,128]{1,0:T(8,128)} %bitcast.19, s32[16]{0:T(128)} %bitcast.23, s32[16]{0:T(128)} %bitcast.25), custom_call_target="tpu_custom_call" | custom-call | flops 1000000000 | bytes 3000000 | tf_op jit(solution)/shard_map/pack_edges/pallas_call | solution.py:317
  1.7 3.4 %collective-permute-start = (f32[88,128]{1,0:T(8,128)S(1)}, f32[88,128]{1,0:T(8,128)S(1)}, u32[]{:S(2)}, u32[]{:S(2)}) collective-permute-start(f32[88,128]{1,0:T(8,128)S(1)} %get-tuple-element.21), channel_id=1, source_target_pairs={{0,28},{4,8},{8,4},{12,16},{16,12},{20,24},{24,20},{28,0},{1,29},{... | collective-permute-start | bytes 135176 | tf_op jit(solution)/shard_map/ppermute | solution.py:343
  5.1 0.0 collective-permute-start.1
  5.1 0.0 copy-done
  5.1 0.0 copy-done.1
  5.1 0.7 %inner_rows.1 = (bf16[8,4096]{1,0:T(8,128)(2,1)S(1)}, bf16[8,4096]{1,0:T(8,128)(2,1)S(1)}, bf16[8,4096]{1,0:T(8,128)(2,1)S(1)}, bf16[8,4096]{1,0:T(8,128)(2,1)S(1)}) custom-call(f32[1024,128]{1,0:T(8,128)S(1)} %bitcast.17, f32[128,128]{1,0:T(8,128)S(1)} %bitcast.20), custom_call_target="tpu_custom_call" | custom-call | flops 1000000000 | bytes 3000000 | tf_op jit(solution)/shard_map/inner_rows/pallas_call | solution.py:346
  5.8 0.0 copy-start.2
  5.8 1.0 %collective-permute-done.odd_ref = f32[88,128]{1,0:T(8,128)S(1)} collective-permute-done((f32[88,128]{1,0:T(8,128)S(1)}, f32[88,128]{1,0:T(8,128)S(1)}, u32[]{:S(2)}, u32[]{:S(2)}) %collective-permute-start) | collective-permute-done | bytes 45088 | tf_op jit(solution)/shard_map/ppermute | solution.py:343
  6.8 0.0 collective-permute-done.1.even_ref
  6.8 0.0 copy-start.3
  6.8 0.2 edge_rows.1
  7.0 2.8 %collective-permute-start.4 = (bf16[8,4096]{1,0:T(8,128)(2,1)S(1)}, bf16[8,4096]{1,0:T(8,128)(2,1)S(1)}, u32[]{:S(2)}, u32[]{:S(2)}) collective-permute-start(bf16[8,4096]{1,0:T(8,128)(2,1)S(1)} %get-tuple-element.35), channel_id=1, source_target_pairs={{0,1},{1,2},{2,3},{3,0},{4,5},{5,6},{6,7},{7,4},{8,9},{9,10},{10,1... | collective-permute-start | bytes 196616 | tf_op jit(solution)/shard_map/ppermute | solution.py:365
  9.7 2.6 %collective-permute-start.5 = (bf16[8,4096]{1,0:T(8,128)(2,1)S(1)}, bf16[8,4096]{1,0:T(8,128)(2,1)S(1)}, u32[]{:S(2)}, u32[]{:S(2)}) collective-permute-start(bf16[8,4096]{1,0:T(8,128)(2,1)S(1)} %get-tuple-element.36), channel_id=1, source_target_pairs={{0,2},{1,3},{2,0},{3,1},{4,6},{5,7},{6,4},{7,5},{8,10},{9,11},{10,... | collective-permute-start | bytes 196616 | tf_op jit(solution)/shard_map/ppermute | solution.py:365
  12.3 1.3 %collective-permute-start.6 = (bf16[8,4096]{1,0:T(8,128)(2,1)S(1)}, bf16[8,4096]{1,0:T(8,128)(2,1)S(1)}, u32[]{:S(2)}, u32[]{:S(2)}) collective-permute-start(bf16[8,4096]{1,0:T(8,128)(2,1)S(1)} %get-tuple-element.37), channel_id=1, source_target_pairs={{0,3},{1,0},{2,1},{3,2},{4,7},{5,4},{6,5},{7,6},{8,11},{9,8},{10,9... | collective-permute-start | bytes 196616 | tf_op jit(solution)/shard_map/ppermute | solution.py:365
  13.7 0.7 %collective-permute-start.2 = (f32[8,128]{1,0:T(8,128)S(1)}, f32[8,128]{1,0:T(8,128)S(1)}, u32[]{:S(2)}, u32[]{:S(2)}) collective-permute-start(f32[8,128]{1,0:T(8,128)S(1)} %get-tuple-element.32), channel_id=1, source_target_pairs={{0,28},{4,8},{8,4},{12,16},{16,12},{20,24},{24,20},{28,0},{1,29},{... | collective-permute-start | bytes 12296 | tf_op jit(solution)/shard_map/ppermute | solution.py:368
  14.3 0.0 copy-start.5
  14.3 0.0 collective-permute-start.3
  14.3 0.0 copy-done.2
  14.3 0.0 copy-done.3
  14.3 0.6 %copy-done.5 = s32[1,1,16]{2,1,0:T(1,128)S(1)} copy-done((s32[1,1,16]{2,1,0:T(1,128)S(1)}, s32[1,1,16]{2,1,0:T(1,128)}, u32[]{:S(2)}) %copy-start.5) | copy-done | bytes 88
  15.0 0.0 copy-start.4
  15.0 1.3 %halved_weights.1 = (bf16[512,32]{1,0:T(8,128)(2,1)S(1)}, bf16[512,512]{1,0:T(8,128)(2,1)S(1)}, s32[17]{0:T(128)S(1)}) custom-call(bf16[32,512]{1,0:T(8,128)(2,1)S(1)} %copy-done.3, bf16[512,512]{1,0:T(8,128)(2,1)S(1)} %copy-done.2, s32[16]{0:T(128)S(1)} %bitcast.24, f32[8,128]{1,0:T(8,128)S(1)} %get-tuple-element.28.after_ref.known_ref), custom_call_target="tpu_custom_call" | custom-call | flops 500000000 | bytes 1500000 | tf_op jit(solution)/shard_map/halved_weights/pallas_call | solution.py:370
  16.3 1.3 %collective-permute-done.2.odd_ref = f32[8,128]{1,0:T(8,128)S(1)} collective-permute-done((f32[8,128]{1,0:T(8,128)S(1)}, f32[8,128]{1,0:T(8,128)S(1)}, u32[]{:S(2)}, u32[]{:S(2)}) %collective-permute-start.2) | collective-permute-done | bytes 4128 | tf_op jit(solution)/shard_map/ppermute | solution.py:368
  17.6 0.0 collective-permute-done.3.even_ref
  17.6 0.0 collective-permute-done.4.refs_1_
  17.6 0.0 collective-permute-done.5.refs_2_
  17.6 0.0 collective-permute-done.6.refs_3_
  17.6 0.0 copy-done.4
  17.6 3.0 %chemistry.1 = (bf16[4,8,4096]{2,1,0:T(8,128)(2,1)}, f32[1,1]{1,0:T(1,128)}) custom-call(s32[17]{0:T(128)S(1)} %get-tuple-element.29.list_ref, bf16[512,32]{1,0:T(8,128)(2,1)S(1)} %get-tuple-element.30.w1_ref, bf16[512,512]{1,0:T(8,128)(2,1)S(1)} %get-tuple-element.31.w2_ref, bf16[32,512]{1,0:T(8,128)(2,1)S(1)} %bitcast.22, ...), custom_call_target="tpu_custom_call" | custom-call | flops 4000000000 | bytes 12000000 | tf_op jit(solution)/shard_map/chemistry/pallas_call | solution.py:380
Async XLA Ops:
  0.6 4.4 %copy-start = (f32[8,64,256]{2,1,0:T(8,128)S(1)}, f32[8,64,256]{2,1,0:T(8,128)}, u32[]{:S(2)}) copy-start(f32[8,64,256]{2,1,0:T(8,128)} %param.7) | copy-start | bytes 1572868
  0.6 4.4 %copy-start.1 = (f32[64,256]{1,0:T(8,128)S(1)}, f32[64,256]{1,0:T(8,128)}, u32[]{:S(2)}) copy-start(f32[64,256]{1,0:T(8,128)} %param.8) | copy-start | bytes 196612
  1.7 5.1 %collective-permute-start = (f32[88,128]{1,0:T(8,128)S(1)}, f32[88,128]{1,0:T(8,128)S(1)}, u32[]{:S(2)}, u32[]{:S(2)}) collective-permute-start(f32[88,128]{1,0:T(8,128)S(1)} %get-tuple-element.21), channel_id=1, source_target_pairs={{0,28},{4,8},{8,4},{12,16},{16,12},{20,24},{24,20},{28,0},{1,29},{... | collective-permute-start | bytes 135176 | tf_op jit(solution)/shard_map/ppermute | solution.py:343
  5.1 1.7 %collective-permute-start.1 = (f32[88,128]{1,0:T(8,128)S(1)}, f32[88,128]{1,0:T(8,128)S(1)}, u32[]{:S(2)}, u32[]{:S(2)}) collective-permute-start(f32[88,128]{1,0:T(8,128)S(1)} %get-tuple-element.22), channel_id=1, source_target_pairs={{0,4},{4,0},{8,12},{12,8},{16,20},{20,16},{24,28},{28,24},{1,5},{5... | collective-permute-start | bytes 135176 | tf_op jit(solution)/shard_map/ppermute | solution.py:344
  5.8 8.6 %copy-start.2 = (bf16[512,512]{1,0:T(8,128)(2,1)S(1)}, bf16[512,512]{1,0:T(8,128)(2,1)}, u32[]{:S(2)}) copy-start(bf16[512,512]{1,0:T(8,128)(2,1)} %w2_ref.1) | copy-start | bytes 1572868
  6.8 7.5 %copy-start.3 = (bf16[32,512]{1,0:T(8,128)(2,1)S(1)}, bf16[32,512]{1,0:T(8,128)(2,1)}, u32[]{:S(2)}) copy-start(bf16[32,512]{1,0:T(8,128)(2,1)} %w1_ref.1) | copy-start | bytes 98308
  7.0 10.6 %collective-permute-start.4 = (bf16[8,4096]{1,0:T(8,128)(2,1)S(1)}, bf16[8,4096]{1,0:T(8,128)(2,1)S(1)}, u32[]{:S(2)}, u32[]{:S(2)}) collective-permute-start(bf16[8,4096]{1,0:T(8,128)(2,1)S(1)} %get-tuple-element.35), channel_id=1, source_target_pairs={{0,1},{1,2},{2,3},{3,0},{4,5},{5,6},{6,7},{7,4},{8,9},{9,10},{10,1... | collective-permute-start | bytes 196616 | tf_op jit(solution)/shard_map/ppermute | solution.py:365
  9.7 7.9 %collective-permute-start.5 = (bf16[8,4096]{1,0:T(8,128)(2,1)S(1)}, bf16[8,4096]{1,0:T(8,128)(2,1)S(1)}, u32[]{:S(2)}, u32[]{:S(2)}) collective-permute-start(bf16[8,4096]{1,0:T(8,128)(2,1)S(1)} %get-tuple-element.36), channel_id=1, source_target_pairs={{0,2},{1,3},{2,0},{3,1},{4,6},{5,7},{6,4},{7,5},{8,10},{9,11},{10,... | collective-permute-start | bytes 196616 | tf_op jit(solution)/shard_map/ppermute | solution.py:365
  12.3 5.3 %collective-permute-start.6 = (bf16[8,4096]{1,0:T(8,128)(2,1)S(1)}, bf16[8,4096]{1,0:T(8,128)(2,1)S(1)}, u32[]{:S(2)}, u32[]{:S(2)}) collective-permute-start(bf16[8,4096]{1,0:T(8,128)(2,1)S(1)} %get-tuple-element.37), channel_id=1, source_target_pairs={{0,3},{1,0},{2,1},{3,2},{4,7},{5,4},{6,5},{7,6},{8,11},{9,8},{10,9... | collective-permute-start | bytes 196616 | tf_op jit(solution)/shard_map/ppermute | solution.py:365
  13.7 3.9 %collective-permute-start.2 = (f32[8,128]{1,0:T(8,128)S(1)}, f32[8,128]{1,0:T(8,128)S(1)}, u32[]{:S(2)}, u32[]{:S(2)}) collective-permute-start(f32[8,128]{1,0:T(8,128)S(1)} %get-tuple-element.32), channel_id=1, source_target_pairs={{0,28},{4,8},{8,4},{12,16},{16,12},{20,24},{24,20},{28,0},{1,29},{... | collective-permute-start | bytes 12296 | tf_op jit(solution)/shard_map/ppermute | solution.py:368
  14.3 0.7 %copy-start.5 = (s32[1,1,16]{2,1,0:T(1,128)S(1)}, s32[1,1,16]{2,1,0:T(1,128)}, u32[]{:S(2)}) copy-start(s32[1,1,16]{2,1,0:T(1,128)} %param.12) | copy-start | bytes 196
  14.3 3.3 %collective-permute-start.3 = (f32[8,128]{1,0:T(8,128)S(1)}, f32[8,128]{1,0:T(8,128)S(1)}, u32[]{:S(2)}, u32[]{:S(2)}) collective-permute-start(f32[8,128]{1,0:T(8,128)S(1)} %get-tuple-element.33), channel_id=1, source_target_pairs={{0,4},{4,0},{8,12},{12,8},{16,20},{20,16},{24,28},{28,24},{1,5},{5... | collective-permute-start | bytes 12296 | tf_op jit(solution)/shard_map/ppermute | solution.py:369
  15.0 2.6 %copy-start.4 = (bf16[512,32]{0,1:T(8,128)(2,1)S(1)}, bf16[512,32]{0,1:T(8,128)(2,1)}, u32[]{:S(2)}) copy-start(bf16[512,32]{0,1:T(8,128)(2,1)} %param.11) | copy-start | bytes 98308

commit v10 on v9

--- a/solution.py
+++ b/solution.py
@@ -11,6 +11,7 @@
 RECV = 8
 LANES = 128
 SUB = 8
+EACH = 4
 BEHIND = 4
 AHEAD = 2
 VMEM_BYTES = 16 * 1024 * 1024
@@ -232,55 +233,85 @@
 def chemistry_kernel(
     groups, list_ref, w1_ref, w2_ref, w3_ref, known_ref, odd_ref, even_ref, *refs
 ):
-    parts, (out_ref, share_ref, state_ref, picked_ref, held_ref, done) = refs[:groups], refs[groups:]
-    species, cells = state_ref.shape[1:]
+    parts, (out_ref, share_ref, picked_ref, fresh_ref, held_ref, done) = refs[:groups], refs[groups:]
+    species, cells = parts[0].shape
     slots = list_ref.shape[0] - 1
     blocks = cells // BLK
     me = lax.axis_index("spec")
-    for k in range(groups):
-        state_ref[lax.rem(me - k + groups, groups)] = parts[k][...]
-    hits = known_ref[...] + even_ref[...] + odd_ref[...]
+    sources = [lax.rem(me - k + groups, groups) for k in range(groups)]
+    copies = [
+        pltpu.make_async_copy(part, out_ref.at[source], done.at[k])
+        for k, (part, source) in enumerate(zip(parts, sources))
+    ]
+    for copy in copies:
+        copy.start()
+    hits = known_ref[...] + odd_ref[...] + even_ref[...]
     lane = lax.broadcasted_iota(jnp.int32, hits.shape, 1)
     mine = jnp.where(lane == lax.axis_index("tile"), hits, 0.0)
     held_ref[...] = jnp.sum(mine[0:1], axis=1, keepdims=True) / RECV
-    share = pltpu.make_async_copy(held_ref, share_ref, done.at[0])
-    share.start()
+    copies.append(pltpu.make_async_copy(held_ref, share_ref, done.at[groups]))
+    copies[groups].start()
+    count = list_ref[slots]
 
     def place(j):
         return pl.ds(pl.multiple_of(jnp.minimum(list_ref[j], blocks - 1) * BLK, BLK), BLK)
 
-    count = list_ref[slots]
-    each = 4
-    for first in range(0, slots, each):
-
-        @pl.when(first < count)
+    def integrate(first, number):
+        for j in range(number):
+            for part, source in zip(parts, sources):
+                rows = pl.ds(pl.multiple_of(source * species, species), species)
+                picked_ref[rows, j * BLK : (j + 1) * BLK] = part[:, place(first + j)].astype(
+                    jnp.float32
+                )
+        width = min(number, EACH) * BLK
+        spans = [slice(at, at + width) for at in range(0, number * BLK, width)]
+        x = [picked_ref[:, span] for span in spans]
+        hidden = [
+            jnp.dot(w1_ref[...], v.astype(jnp.bfloat16), preferred_element_type=jnp.float32)
+            for v in x
+        ]
+        hidden = [silu_of_half(v).astype(jnp.bfloat16) for v in hidden]
+        hidden = [jnp.dot(w2_ref[...], v, preferred_element_type=jnp.float32) for v in hidden]
+        hidden = [silu_of_half(v).astype(jnp.bfloat16) for v in hidden]
+        for i, (v, h) in enumerate(zip(x, hidden)):
+            v = v + jnp.dot(w3_ref[...], h, preferred_element_type=jnp.float32)
+            for j in range(width // BLK):
+                for g in range(groups):
+                    fresh_ref[first + i * width // BLK + j, g] = v[
+                        g * species : (g + 1) * species, j * BLK : (j + 1) * BLK
+                    ].astype(jnp.bfloat16)
+
+    for first in range(0, slots, 2 * EACH):
+        left = count - first
+
+        @pl.when((left > 0) & (left <= EACH))
         def _():
-            for j in range(each):
-                for g in range(groups):
-                    picked_ref[g * species : (g + 1) * species, j * BLK : (j + 1) * BLK] = state_ref[
-                        g, :, place(first + j)
-                    ].astype(jnp.float32)
-            x = picked_ref[...]
-            hidden = jnp.dot(
-                w1_ref[...], x.astype(jnp.bfloat16), preferred_element_type=jnp.float32
-            )
-            hidden = silu_of_half(hidden).astype(jnp.bfloat16)
-            hidden = jnp.dot(w2_ref[...], hidden, preferred_element_type=jnp.float32)
-            hidden = silu_of_half(hidden).astype(jnp.bfloat16)
-            fresh = x + jnp.dot(w3_ref[...], hidden, preferred_element_type=jnp.float32)
-            for j in range(each):
-                valid = first + j < count
-                for g in range(groups):
-                    now = state_ref[g, :, place(first + j)].astype(jnp.float32)
-                    new = fresh[g * species : (g + 1) * species, j * BLK : (j + 1) * BLK]
-                    state_ref[g, :, place(first + j)] = jnp.where(valid, new, now).astype(
-                        jnp.bfloat16
-                    )
-
-    whole = pltpu.make_async_copy(state_ref, out_ref, done.at[1])
-    whole.start()
-    share.wait()
-    whole.wait()
+            integrate(first, EACH)
+
+        @pl.when(left > EACH)
+        def _():
+            integrate(first, 2 * EACH)
+
+    for copy in copies:
+        copy.wait()
+
+    def for_listed(act):
+        for first in range(0, slots, EACH):
+
+            @pl.when(first < count)
+            def _():
+                for j in range(first, first + EACH):
+
+                    @pl.when(j < count)
+                    def _():
+                        act(
+                            pltpu.make_async_copy(
+                                fresh_ref.at[j], out_ref.at[:, :, place(j)], done.at[groups + 1 + j]
+                            )
+                        )
+
+    for_listed(lambda copy: copy.start())
+    for_listed(lambda copy: copy.wait())
 
 
 def vmem():
@@ -386,10 +417,10 @@
         in_specs=[pl.BlockSpec(memory_space=pltpu.SMEM)] + [vmem()] * (6 + dests),
         out_specs=[anywhere()] * 2,
         scratch_shapes=[
-            pltpu.VMEM((dests, species, cells), bf16),
-            pltpu.VMEM((dests * species, 4 * BLK), f32),
+            pltpu.VMEM((dests * species, 2 * EACH * BLK), f32),
+            pltpu.VMEM((slots, dests, species, BLK), bf16),
             pltpu.VMEM((1, 1), f32),
-            pltpu.SemaphoreType.DMA((2,)),
+            pltpu.SemaphoreType.DMA((dests + 1 + slots,)),
         ],
         compiler_params=params,
         cost_estimate=cost(4.0),

time: 20.6 us -> 20.8 us (level); the launches traced: 20.6 us -> 21 us
  Pallas kernels: 6.11 us -> 6.58 us
    pallas_call x1, Pallas kernels: 2.95 us -> 3.42 us  [shards(): pl.pallas_call(functools.partial(chemistry_kernel, dests), out_shape=[jax...]
where the time goes in v10:
time: 20.8 us; the launch traced here: 21 us
  starting transfers between devices  10.8 us (52%)
  Pallas kernels  6.58 us (32%)
  waiting for transfers between devices  2.31 us (11%)
  between operations  0.72 us (3%)
  local copies, waits for them, and re-layouts  0.67 us (3%)
    ppermute x3, starting transfers between devices, shards(): lax.ppermute(blocks[k], 'spec', [(s, (s + k) % dests) for s in range(dest...  6.7 us
    ppermute x2, starting transfers between devices, shards(): from_odd = lax.ppermute(to_odd, 'tile', odds)  4.07 us
    pallas_call x1, Pallas kernels, shards(): pl.pallas_call(functools.partial(chemistry_kernel, dests), out_shape=[jax...  3.42 us
    ppermute x2, waiting for transfers between devices, shards(): from_odd = lax.ppermute(to_odd, 'tile', odds)  2.3 us
    pallas_call x1, Pallas kernels, shards(): pl.pallas_call(functools.partial(weight_kernel, cells // BLK), out_shape=...  1.31 us
    pallas_call x1, Pallas kernels, shards(): pl.pallas_call(functools.partial(pack_kernel, length, halves, cells // BL...  1.01 us
    pallas_call x1, Pallas kernels, shards(): pl.pallas_call(functools.partial(inner_kernel, dests, length, halves), ou...  0.69 us
    unnamed x12, local copies, waits for them, and re-layouts  0.67 us
  transfers between devices with their start and end apart: 7, of which 2 were waited for; matrix products, arithmetic and copies ran while one was open for 0% of the time, Pallas kernels for 10%

profile of v10, /device:TPU:0, one launch (start us, length us, event | category | flops | bytes accessed | tf_op | source)
XLA Modules:
  0.0 21.0 jit_solution(11109417742618814967)
XLA Ops:
  0.6 0.0 copy-start
  0.6 0.0 copy-start.1
  0.6 1.0 %pack_edges.1 = (f32[88,128]{1,0:T(8,128)S(1)}, f32[88,128]{1,0:T(8,128)S(1)}, f32[8,128]{1,0:T(8,128)S(1)}) custom-call(f32[8,128,128]{2,1,0:T(8,128)} %bitcast.16, f32[128,128]{1,0:T(8,128)} %bitcast.19, s32[16]{0:T(128)} %bitcast.23, s32[16]{0:T(128)} %bitcast.25), custom_call_target="tpu_custom_call" | custom-call | flops 1000000000 | bytes 3000000 | tf_op jit(solution)/shard_map/pack_edges/pallas_call | solution.py:348
  1.7 3.4 %collective-permute-start = (f32[88,128]{1,0:T(8,128)S(1)}, f32[88,128]{1,0:T(8,128)S(1)}, u32[]{:S(2)}, u32[]{:S(2)}) collective-permute-start(f32[88,128]{1,0:T(8,128)S(1)} %get-tuple-element.21), channel_id=1, source_target_pairs={{0,28},{4,8},{8,4},{12,16},{16,12},{20,24},{24,20},{28,0},{1,29},{... | collective-permute-start | bytes 135176 | tf_op jit(solution)/shard_map/ppermute | solution.py:374
  5.1 0.0 collective-permute-start.1
  5.1 0.0 copy-done
  5.1 0.0 copy-done.1
  5.1 0.7 %inner_rows.1 = (bf16[8,4096]{1,0:T(8,128)(2,1)S(1)}, bf16[8,4096]{1,0:T(8,128)(2,1)S(1)}, bf16[8,4096]{1,0:T(8,128)(2,1)S(1)}, bf16[8,4096]{1,0:T(8,128)(2,1)S(1)}) custom-call(f32[1024,128]{1,0:T(8,128)S(1)} %bitcast.17, f32[128,128]{1,0:T(8,128)S(1)} %bitcast.20), custom_call_target="tpu_custom_call" | custom-call | flops 1000000000 | bytes 3000000 | tf_op jit(solution)/shard_map/inner_rows/pallas_call | solution.py:377
  5.8 0.0 copy-start.2
  5.8 1.0 %collective-permute-done.odd_ref = f32[88,128]{1,0:T(8,128)S(1)} collective-permute-done((f32[88,128]{1,0:T(8,128)S(1)}, f32[88,128]{1,0:T(8,128)S(1)}, u32[]{:S(2)}, u32[]{:S(2)}) %collective-permute-start) | collective-permute-done | bytes 45088 | tf_op jit(solution)/shard_map/ppermute | solution.py:374
  6.8 0.0 collective-permute-done.1.even_ref
  6.8 0.0 copy-start.3
  6.8 0.2 edge_rows.1
  7.0 2.8 %collective-permute-start.4 = (bf16[8,4096]{1,0:T(8,128)(2,1)S(1)}, bf16[8,4096]{1,0:T(8,128)(2,1)S(1)}, u32[]{:S(2)}, u32[]{:S(2)}) collective-permute-start(bf16[8,4096]{1,0:T(8,128)(2,1)S(1)} %get-tuple-element.35), channel_id=1, source_target_pairs={{0,1},{1,2},{2,3},{3,0},{4,5},{5,6},{6,7},{7,4},{8,9},{9,10},{10,1... | collective-permute-start | bytes 196616 | tf_op jit(solution)/shard_map/ppermute | solution.py:396
  9.7 2.6 %collective-permute-start.5 = (bf16[8,4096]{1,0:T(8,128)(2,1)S(1)}, bf16[8,4096]{1,0:T(8,128)(2,1)S(1)}, u32[]{:S(2)}, u32[]{:S(2)}) collective-permute-start(bf16[8,4096]{1,0:T(8,128)(2,1)S(1)} %get-tuple-element.36), channel_id=1, source_target_pairs={{0,2},{1,3},{2,0},{3,1},{4,6},{5,7},{6,4},{7,5},{8,10},{9,11},{10,... | collective-permute-start | bytes 196616 | tf_op jit(solution)/shard_map/ppermute | solution.py:396
  12.3 1.3 %collective-permute-start.6 = (bf16[8,4096]{1,0:T(8,128)(2,1)S(1)}, bf16[8,4096]{1,0:T(8,128)(2,1)S(1)}, u32[]{:S(2)}, u32[]{:S(2)}) collective-permute-start(bf16[8,4096]{1,0:T(8,128)(2,1)S(1)} %get-tuple-element.37), channel_id=1, source_target_pairs={{0,3},{1,0},{2,1},{3,2},{4,7},{5,4},{6,5},{7,6},{8,11},{9,8},{10,9... | collective-permute-start | bytes 196616 | tf_op jit(solution)/shard_map/ppermute | solution.py:396
  13.7 0.7 %collective-permute-start.2 = (f32[8,128]{1,0:T(8,128)S(1)}, f32[8,128]{1,0:T(8,128)S(1)}, u32[]{:S(2)}, u32[]{:S(2)}) collective-permute-start(f32[8,128]{1,0:T(8,128)S(1)} %get-tuple-element.32), channel_id=1, source_target_pairs={{0,28},{4,8},{8,4},{12,16},{16,12},{20,24},{24,20},{28,0},{1,29},{... | collective-permute-start | bytes 12296 | tf_op jit(solution)/shard_map/ppermute | solution.py:399
  14.3 0.0 copy-start.5
  14.3 0.0 collective-permute-start.3
  14.3 0.0 copy-done.2
  14.3 0.0 copy-done.3
  14.3 0.6 %copy-done.5 = s32[1,1,16]{2,1,0:T(1,128)S(1)} copy-done((s32[1,1,16]{2,1,0:T(1,128)S(1)}, s32[1,1,16]{2,1,0:T(1,128)}, u32[]{:S(2)}) %copy-start.5) | copy-done | bytes 88
  15.0 0.0 copy-start.4
  15.0 1.3 %halved_weights.1 = (bf16[512,32]{1,0:T(8,128)(2,1)S(1)}, bf16[512,512]{1,0:T(8,128)(2,1)S(1)}, s32[17]{0:T(128)S(1)}) custom-call(bf16[32,512]{1,0:T(8,128)(2,1)S(1)} %copy-done.3, bf16[512,512]{1,0:T(8,128)(2,1)S(1)} %copy-done.2, s32[16]{0:T(128)S(1)} %bitcast.24, f32[8,128]{1,0:T(8,128)S(1)} %get-tuple-element.28.after_ref.known_ref), custom_call_target="tpu_custom_call" | custom-call | flops 500000000 | bytes 1500000 | tf_op jit(solution)/shard_map/halved_weights/pallas_call | solution.py:401
  16.3 1.3 %collective-permute-done.2.odd_ref = f32[8,128]{1,0:T(8,128)S(1)} collective-permute-done((f32[8,128]{1,0:T(8,128)S(1)}, f32[8,128]{1,0:T(8,128)S(1)}, u32[]{:S(2)}, u32[]{:S(2)}) %collective-permute-start.2) | collective-permute-done | bytes 4128 | tf_op jit(solution)/shard_map/ppermute | solution.py:399
  17.6 0.0 collective-permute-done.3.even_ref
  17.6 0.0 collective-permute-done.4.refs_1_
  17.6 0.0 collective-permute-done.5.refs_2_
  17.6 0.0 collective-permute-done.6.refs_3_
  17.6 0.0 copy-done.4
  17.6 3.4 %chemistry.1 = (bf16[4,8,4096]{2,1,0:T(8,128)(2,1)}, f32[1,1]{1,0:T(1,128)}) custom-call(s32[17]{0:T(128)S(1)} %get-tuple-element.29.list_ref, bf16[512,32]{1,0:T(8,128)(2,1)S(1)} %get-tuple-element.30.w1_ref, bf16[512,512]{1,0:T(8,128)(2,1)S(1)} %get-tuple-element.31.w2_ref, bf16[32,512]{1,0:T(8,128)(2,1)S(1)} %bitcast.22, ...), custom_call_target="tpu_custom_call" | custom-call | flops 4000000000 | bytes 12000000 | tf_op jit(solution)/shard_map/chemistry/pallas_call | solution.py:411
Async XLA Ops:
  0.6 4.4 %copy-start = (f32[8,64,256]{2,1,0:T(8,128)S(1)}, f32[8,64,256]{2,1,0:T(8,128)}, u32[]{:S(2)}) copy-start(f32[8,64,256]{2,1,0:T(8,128)} %param.7) | copy-start | bytes 1572868
  0.6 4.4 %copy-start.1 = (f32[64,256]{1,0:T(8,128)S(1)}, f32[64,256]{1,0:T(8,128)}, u32[]{:S(2)}) copy-start(f32[64,256]{1,0:T(8,128)} %param.8) | copy-start | bytes 196612
  1.7 5.1 %collective-permute-start = (f32[88,128]{1,0:T(8,128)S(1)}, f32[88,128]{1,0:T(8,128)S(1)}, u32[]{:S(2)}, u32[]{:S(2)}) collective-permute-start(f32[88,128]{1,0:T(8,128)S(1)} %get-tuple-element.21), channel_id=1, source_target_pairs={{0,28},{4,8},{8,4},{12,16},{16,12},{20,24},{24,20},{28,0},{1,29},{... | collective-permute-start | bytes 135176 | tf_op jit(solution)/shard_map/ppermute | solution.py:374
  5.1 1.7 %collective-permute-start.1 = (f32[88,128]{1,0:T(8,128)S(1)}, f32[88,128]{1,0:T(8,128)S(1)}, u32[]{:S(2)}, u32[]{:S(2)}) collective-permute-start(f32[88,128]{1,0:T(8,128)S(1)} %get-tuple-element.22), channel_id=1, source_target_pairs={{0,4},{4,0},{8,12},{12,8},{16,20},{20,16},{24,28},{28,24},{1,5},{5... | collective-permute-start | bytes 135176 | tf_op jit(solution)/shard_map/ppermute | solution.py:375
  5.8 8.6 %copy-start.2 = (bf16[512,512]{1,0:T(8,128)(2,1)S(1)}, bf16[512,512]{1,0:T(8,128)(2,1)}, u32[]{:S(2)}) copy-start(bf16[512,512]{1,0:T(8,128)(2,1)} %w2_ref.1) | copy-start | bytes 1572868
  6.8 7.5 %copy-start.3 = (bf16[32,512]{1,0:T(8,128)(2,1)S(1)}, bf16[32,512]{1,0:T(8,128)(2,1)}, u32[]{:S(2)}) copy-start(bf16[32,512]{1,0:T(8,128)(2,1)} %w1_ref.1) | copy-start | bytes 98308
  7.0 10.6 %collective-permute-start.4 = (bf16[8,4096]{1,0:T(8,128)(2,1)S(1)}, bf16[8,4096]{1,0:T(8,128)(2,1)S(1)}, u32[]{:S(2)}, u32[]{:S(2)}) collective-permute-start(bf16[8,4096]{1,0:T(8,128)(2,1)S(1)} %get-tuple-element.35), channel_id=1, source_target_pairs={{0,1},{1,2},{2,3},{3,0},{4,5},{5,6},{6,7},{7,4},{8,9},{9,10},{10,1... | collective-permute-start | bytes 196616 | tf_op jit(solution)/shard_map/ppermute | solution.py:396
  9.7 7.9 %collective-permute-start.5 = (bf16[8,4096]{1,0:T(8,128)(2,1)S(1)}, bf16[8,4096]{1,0:T(8,128)(2,1)S(1)}, u32[]{:S(2)}, u32[]{:S(2)}) collective-permute-start(bf16[8,4096]{1,0:T(8,128)(2,1)S(1)} %get-tuple-element.36), channel_id=1, source_target_pairs={{0,2},{1,3},{2,0},{3,1},{4,6},{5,7},{6,4},{7,5},{8,10},{9,11},{10,... | collective-permute-start | bytes 196616 | tf_op jit(solution)/shard_map/ppermute | solution.py:396
  12.3 5.3 %collective-permute-start.6 = (bf16[8,4096]{1,0:T(8,128)(2,1)S(1)}, bf16[8,4096]{1,0:T(8,128)(2,1)S(1)}, u32[]{:S(2)}, u32[]{:S(2)}) collective-permute-start(bf16[8,4096]{1,0:T(8,128)(2,1)S(1)} %get-tuple-element.37), channel_id=1, source_target_pairs={{0,3},{1,0},{2,1},{3,2},{4,7},{5,4},{6,5},{7,6},{8,11},{9,8},{10,9... | collective-permute-start | bytes 196616 | tf_op jit(solution)/shard_map/ppermute | solution.py:396
  13.7 3.9 %collective-permute-start.2 = (f32[8,128]{1,0:T(8,128)S(1)}, f32[8,128]{1,0:T(8,128)S(1)}, u32[]{:S(2)}, u32[]{:S(2)}) collective-permute-start(f32[8,128]{1,0:T(8,128)S(1)} %get-tuple-element.32), channel_id=1, source_target_pairs={{0,28},{4,8},{8,4},{12,16},{16,12},{20,24},{24,20},{28,0},{1,29},{... | collective-permute-start | bytes 12296 | tf_op jit(solution)/shard_map/ppermute | solution.py:399
  14.3 0.7 %copy-start.5 = (s32[1,1,16]{2,1,0:T(1,128)S(1)}, s32[1,1,16]{2,1,0:T(1,128)}, u32[]{:S(2)}) copy-start(s32[1,1,16]{2,1,0:T(1,128)} %param.12) | copy-start | bytes 196
  14.3 3.3 %collective-permute-start.3 = (f32[8,128]{1,0:T(8,128)S(1)}, f32[8,128]{1,0:T(8,128)S(1)}, u32[]{:S(2)}, u32[]{:S(2)}) collective-permute-start(f32[8,128]{1,0:T(8,128)S(1)} %get-tuple-element.33), channel_id=1, source_target_pairs={{0,4},{4,0},{8,12},{12,8},{16,20},{20,16},{24,28},{28,24},{1,5},{5... | collective-permute-start | bytes 12296 | tf_op jit(solution)/shard_map/ppermute | solution.py:400
  15.0 2.6 %copy-start.4 = (bf16[512,32]{0,1:T(8,128)(2,1)S(1)}, bf16[512,32]{0,1:T(8,128)(2,1)}, u32[]{:S(2)}) copy-start(bf16[512,32]{0,1:T(8,128)(2,1)} %param.11) | copy-start | bytes 98308

commit v11 on v10

--- a/solution.py
+++ b/solution.py
@@ -12,6 +12,7 @@
 LANES = 128
 SUB = 8
 EACH = 4
+COPIES = 5
 BEHIND = 4
 AHEAD = 2
 VMEM_BYTES = 16 * 1024 * 1024
@@ -57,8 +58,8 @@
 
 
 def pack_kernel(
-    length, halves, blocks, q_in, rates_in, list_in, dest_in,
-    even_ref, odd_ref, hits_ref, low_ref, high_ref, rates_ref, list_ref, dest_ref, arrived,
+    length, halves, blocks, q_in, rates_in, list_in, dest_in, row_in,
+    even_ref, odd_ref, hits_ref, row_ref, low_ref, high_ref, rates_ref, list_ref, dest_ref, arrived,
 ):
     species, rows = q_in.shape[:2]
     tile = halves * SUB
@@ -71,6 +72,7 @@
         (rates_in.at[:tile], rates_ref.at[:tile]),
         (list_in, list_ref),
         (dest_in, dest_ref),
+        (row_in, row_ref),
     ]
     copies = [
         pltpu.make_async_copy(source, target, arrived.at[i])
@@ -86,7 +88,7 @@
         target = jnp.where(list_ref[j] < blocks, dest_ref[j], -1)
         hits = hits + jnp.where(lane == target, 1.0, 0.0)
     hits_ref[...] = hits
-    for copy in copies[:4]:
+    for copy in copies[:4] + copies[6:]:
         copy.wait()
 
     def write(up_ref, down_ref):
@@ -147,11 +149,10 @@
 
 
 def edge_kernel(
-    dests, length, halves, odd_ref, even_ref, hits_ref, q_ref, rates_ref, *refs
+    dests, early, late, length, halves, odd_ref, even_ref, hits_ref, q_ref, rates_ref, *refs
 ):
-    in_refs, out_refs, (to_even_ref, to_odd_ref, known_ref) = (
-        refs[:dests], refs[dests : 2 * dests], refs[2 * dests :]
-    )
+    in_refs, out_refs, refs = refs[: len(late)], refs[len(late) : 2 * len(late)], refs[2 * len(late) :]
+    *small_refs, to_even_ref, to_odd_ref, known_ref = refs
     species, cells = out_refs[0].shape
     me = lax.axis_index("spec")
     part = BEHIND * species + SUB
@@ -160,7 +161,7 @@
     own, from_even, from_odd = hits_ref[...], even_ref[halves * part :, :], odd_ref[halves * part :, :]
     known_ref[...] = own + from_even + from_odd
     to_even_ref[...] = from_odd
-    to_odd_ref[...] = from_even
+    to_odd_ref[...] = jnp.concatenate([from_even] * COPIES)
 
     def message(behind, at, size):
         a, b = odd_ref[at : at + size, :], even_ref[at : at + size, :]
@@ -196,7 +197,16 @@
                 rates_of(own_rates(length - reach) + [after[j : j + 1] for j in range(AHEAD)]),
             )
         )
-    for k, (in_ref, out_ref) in enumerate(zip(in_refs, out_refs)):
+    for k, small_ref in zip(early, small_refs):
+        low = lax.rem(me + k, dests) == 0
+        for half in range(halves):
+            for j in range(BEHIND):
+                value = tops[half][j]
+                if j >= BEHIND - AHEAD:
+                    value = jnp.where(low, value, bottoms[half][j - BEHIND + AHEAD])
+                at = (j * halves + half) * LANES
+                small_ref[:, at : at + LANES] = value.astype(jnp.bfloat16)
+    for k, in_ref, out_ref in zip(late, in_refs, out_refs):
         dest = lax.rem(me + k, dests)
         out_ref[...] = in_ref[...]
 
@@ -215,55 +225,69 @@
                     out_ref[:, at : at + LANES] = value.astype(jnp.bfloat16)
 
 
-def weight_kernel(blocks, w1_ref, w2_ref, list_ref, after_ref, w1_out, w2_out, listed_out):
-    slots = list_ref.shape[0]
-    for j in range(slots + 1):
-        listed_out[j] = blocks
-    count = jnp.int32(0)
-    for j in range(slots):
-        block = list_ref[j]
-        listed_out[count] = block
-        count = count + jnp.where(block < blocks, 1, 0)
-    listed_out[count] = blocks
-    listed_out[slots] = count
+def weight_kernel(w1_ref, w2_ref, after_ref, w1_out, w2_out):
     w1_out[...] = (0.5 * w1_ref[...].astype(jnp.float32)).T.astype(jnp.bfloat16)
     w2_out[...] = (0.5 * w2_ref[...].astype(jnp.float32)).T.astype(jnp.bfloat16)
 
 
 def chemistry_kernel(
-    groups, list_ref, w1_ref, w2_ref, w3_ref, known_ref, odd_ref, even_ref, *refs
+    groups, early, named_ref, w1_ref, w2_ref, w3_ref, *refs
 ):
-    parts, (out_ref, share_ref, picked_ref, fresh_ref, held_ref, done) = refs[:groups], refs[groups:]
+    parts, edges, refs = list(refs[:groups]), refs[groups : groups + len(early)], refs[groups + len(early) :]
+    (known_ref, odd_ref, even_ref), refs = refs[:3], refs[3:]
+    out_ref, share_ref, list_ref, whole_ref, picked_ref, fresh_ref, held_ref, done = refs
     species, cells = parts[0].shape
-    slots = list_ref.shape[0] - 1
+    slots = named_ref.shape[0]
     blocks = cells // BLK
     me = lax.axis_index("spec")
     sources = [lax.rem(me - k + groups, groups) for k in range(groups)]
+    wide = edges[0].shape[1]
+    narrow = wide // BEHIND * AHEAD
+    for i, k in enumerate(early):
+        whole_ref[i] = parts[k][...]
+        parts[k] = whole_ref.at[i]
+
+    @pl.when(me == 0)
+    def _():
+        for k, edge in zip(early, edges):
+            parts[k][:, :wide] = edge[...]
+
+    @pl.when(me == groups - 1)
+    def _():
+        for k, edge in zip(early, edges):
+            parts[k][:, cells - narrow :] = edge[:, wide - narrow :]
+
     copies = [
         pltpu.make_async_copy(part, out_ref.at[source], done.at[k])
         for k, (part, source) in enumerate(zip(parts, sources))
     ]
     for copy in copies:
         copy.start()
-    hits = known_ref[...] + odd_ref[...] + even_ref[...]
+    hits = known_ref[...] + odd_ref[:SUB] + even_ref[...]
     lane = lax.broadcasted_iota(jnp.int32, hits.shape, 1)
     mine = jnp.where(lane == lax.axis_index("tile"), hits, 0.0)
     held_ref[...] = jnp.sum(mine[0:1], axis=1, keepdims=True) / RECV
     copies.append(pltpu.make_async_copy(held_ref, share_ref, done.at[groups]))
     copies[groups].start()
-    count = list_ref[slots]
+    for j in range(slots):
+        list_ref[j] = blocks
+    count = jnp.int32(0)
+    for j in range(slots):
+        block = named_ref[j]
+        list_ref[count] = block
+        count = count + jnp.where(block < blocks, 1, 0)
 
     def place(j):
         return pl.ds(pl.multiple_of(jnp.minimum(list_ref[j], blocks - 1) * BLK, BLK), BLK)
 
-    def integrate(first, number):
+    def integrate(number):
         for j in range(number):
             for part, source in zip(parts, sources):
                 rows = pl.ds(pl.multiple_of(source * species, species), species)
-                picked_ref[rows, j * BLK : (j + 1) * BLK] = part[:, place(first + j)].astype(
+                picked_ref[rows, j * BLK : (j + 1) * BLK] = part[:, place(j)].astype(
                     jnp.float32
                 )
-        width = min(number, EACH) * BLK
+        width = EACH * BLK
         spans = [slice(at, at + width) for at in range(0, number * BLK, width)]
         x = [picked_ref[:, span] for span in spans]
         hidden = [
@@ -277,20 +301,15 @@
             v = v + jnp.dot(w3_ref[...], h, preferred_element_type=jnp.float32)
             for j in range(width // BLK):
                 for g in range(groups):
-                    fresh_ref[first + i * width // BLK + j, g] = v[
+                    fresh_ref[i * EACH + j, g] = v[
                         g * species : (g + 1) * species, j * BLK : (j + 1) * BLK
                     ].astype(jnp.bfloat16)
 
-    for first in range(0, slots, 2 * EACH):
-        left = count - first
-
-        @pl.when((left > 0) & (left <= EACH))
+    for number in range(EACH, slots + 1, EACH):
+
+        @pl.when((count > number - EACH) & (count <= number))
         def _():
-            integrate(first, EACH)
-
-        @pl.when(left > EACH)
-        def _():
-            integrate(first, 2 * EACH)
+            integrate(number)
 
     for copy in copies:
         copy.wait()
@@ -345,18 +364,19 @@
     flag = jax.ShapeDtypeStruct((SUB, LANES), f32)
 
     field, rates = tiled(concentrations, halves), tiled(courant, halves)
-    to_even, to_odd, hits = pl.pallas_call(
+    to_even, to_odd, hits, listing = pl.pallas_call(
         functools.partial(pack_kernel, length, halves, cells // BLK),
-        out_shape=[jax.ShapeDtypeStruct((size, LANES), f32)] * 2 + [flag],
-        in_specs=[anywhere()] * 4,
-        out_specs=[vmem()] * 3,
+        out_shape=[jax.ShapeDtypeStruct((size, LANES), f32)] * 2
+        + [flag, jax.ShapeDtypeStruct((1, slots), jnp.int32)],
+        in_specs=[anywhere()] * 5,
+        out_specs=[vmem()] * 4,
         scratch_shapes=[
             pltpu.VMEM((species * halves * SUB, LANES), f32),
             pltpu.VMEM((species * halves * SUB, LANES), f32),
             pltpu.VMEM((2 * halves * SUB, LANES), f32),
             pltpu.SMEM((slots,), jnp.int32),
             pltpu.SMEM((slots,), jnp.int32),
-            pltpu.SemaphoreType.DMA((6,)),
+            pltpu.SemaphoreType.DMA((7,)),
         ],
         compiler_params=params,
         cost_estimate=cost(1.0),
@@ -366,6 +386,7 @@
         from_hbm(rates),
         from_hbm(active_blocks.reshape(-1)),
         from_hbm(dest_tile.reshape(-1)),
+        from_hbm(active_blocks.reshape(1, slots)),
     )
     field = field.reshape(species * length * halves, LANES)
     evens = [(t, t ^ 1) for t in range(tiles)]
@@ -383,41 +404,50 @@
         cost_estimate=cost(1.0),
         name="inner_rows",
     )(field, rates)
-    *blocks, to_even, to_odd, known = pl.pallas_call(
-        functools.partial(edge_kernel, dests, length, halves),
-        out_shape=[block] * dests + [flag] * 3,
-        in_specs=[vmem()] * (5 + dests),
+    def ring(k, x):
+        return lax.ppermute(x, "spec", [(s, (s + k) % dests) for s in range(dests)])
+
+    early = [dests // 2]
+    late = [k for k in range(dests) if k not in early]
+    edge = jax.ShapeDtypeStruct((species, BEHIND * cols), bf16)
+    whole = pl.pallas_call(
+        functools.partial(edge_kernel, dests, early, late, length, halves),
+        out_shape=[block] * len(late)
+        + [edge] * len(early)
+        + [flag, jax.ShapeDtypeStruct((COPIES * SUB, LANES), f32), flag],
+        in_specs=[vmem()] * (5 + len(late)),
         out_specs=[vmem()] * (dests + 3),
         compiler_params=params,
         cost_estimate=cost(0.1),
         name="edge_rows",
-    )(from_odd, from_even, hits, field, rates, *blocks)
-    received = [blocks[0]] + [
-        lax.ppermute(blocks[k], "spec", [(s, (s + k) % dests) for s in range(dests)])
-        for k in range(1, dests)
-    ]
+    )(from_odd, from_even, hits, field, rates, *[blocks[k] for k in late])
+    full, edges, (to_even, to_odd, known) = whole[: len(late)], whole[len(late) : dests], whole[dests:]
+    received = {k: ring(k, blocks[k]) for k in early}
+    received |= {k: ring(k, x) if k else x for k, x in zip(late, full)}
+    edges = [ring(k, x) for k, x in zip(early, edges)]
     from_odd = lax.ppermute(to_odd, "tile", odds)
     from_even = lax.ppermute(to_even, "tile", evens)
-    w1, w2, listing = pl.pallas_call(
-        functools.partial(weight_kernel, cells // BLK),
-        out_shape=[jax.ShapeDtypeStruct(w.shape[::-1], bf16) for w in (first_weight, middle_weight)]
-        + [jax.ShapeDtypeStruct((slots + 1,), jnp.int32)],
-        in_specs=[vmem()] * 2 + [pl.BlockSpec(memory_space=pltpu.SMEM), anywhere()],
-        out_specs=[vmem()] * 2 + [pl.BlockSpec(memory_space=pltpu.SMEM)],
+    w1, w2 = pl.pallas_call(
+        weight_kernel,
+        out_shape=[jax.ShapeDtypeStruct(w.shape[::-1], bf16) for w in (first_weight, middle_weight)],
+        in_specs=[vmem()] * 2 + [anywhere()],
+        out_specs=[vmem()] * 2,
         compiler_params=params,
         cost_estimate=cost(0.5),
         name="halved_weights",
-    )(first_weight, middle_weight, active_blocks.reshape(-1), known)
+    )(first_weight, middle_weight, known)
     out, load_share = pl.pallas_call(
-        functools.partial(chemistry_kernel, dests),
+        functools.partial(chemistry_kernel, dests, early),
         out_shape=[
             jax.ShapeDtypeStruct((dests, species, cells), bf16),
             jax.ShapeDtypeStruct((1, 1), f32),
         ],
-        in_specs=[pl.BlockSpec(memory_space=pltpu.SMEM)] + [vmem()] * (6 + dests),
+        in_specs=[pl.BlockSpec(memory_space=pltpu.SMEM)] + [vmem()] * (6 + dests + len(early)),
         out_specs=[anywhere()] * 2,
         scratch_shapes=[
-            pltpu.VMEM((dests * species, 2 * EACH * BLK), f32),
+            pltpu.SMEM((slots + 1,), jnp.int32),
+            pltpu.VMEM((len(early), species, cells), bf16),
+            pltpu.VMEM((dests * species, slots * BLK), f32),
             pltpu.VMEM((slots, dests, species, BLK), bf16),
             pltpu.VMEM((1, 1), f32),
             pltpu.SemaphoreType.DMA((dests + 1 + slots,)),
@@ -426,14 +456,15 @@
         cost_estimate=cost(4.0),
         name="chemistry",
     )(
-        listing,
+        listing.reshape(-1),
         w1,
         w2,
         last_weight.T,
+        *[received[k] for k in range(dests)],
+        *edges,
         known,
         from_odd,
         from_even,
-        *received,
     )
     return out.reshape(dests * species, cells), load_share
 

time: 20.8 us -> 20.5 us (0.986); the launches traced: 21 us -> 20.2 us
  Pallas kernels: 6.58 us -> 4.34 us
  waiting for transfers between devices: 2.31 us -> 3.96 us
  local copies, waits for them, and re-layouts: 0.67 us -> 0.02 us
  starting transfers between devices: 10.8 us -> 11.1 us
    ppermute x3 -> x4, waiting for transfers between devices: 0.01 us -> 2.32 us  [ring(): return lax.ppermute(x, 'spec', [(s, (s + k) % dests) for s in range(dests)])]
    pallas_call x3, Pallas kernels: 4.89 us -> 2.64 us  [the longest x1 2.24 us: shards(): pl.pallas_call(functools.partial(chemistry_kernel, dests, early), out_sha...]
    ppermute x2, waiting for transfers between devices: 2.3 us -> 0.75 us  [shards(): from_odd = lax.ppermute(to_odd, 'tile', odds)]
    ppermute x2, waiting for transfers between devices: 0.01 us -> 0.89 us  [shards(): from_even = lax.ppermute(to_even, 'tile', evens)]
    unnamed x12 -> x10, local copies, waits for them, and re-layouts: 0.67 us -> 0.02 us
    ppermute x2, starting transfers between devices: 4.07 us -> 4.3 us  [shards(): from_odd = lax.ppermute(to_odd, 'tile', odds)]
    ppermute x3 -> x4, starting transfers between devices: 6.7 us -> 6.8 us  [ring(): return lax.ppermute(x, 'spec', [(s, (s + k) % dests) for s in range(dests)])]
  transfers between devices with their start and end apart: 7 -> 8, of which waited for: 2 -> 3; matrix products, arithmetic and copies ran while one was open for 0% -> 0% of each run, Pallas kernels for 10% -> 5%
where the time goes in v11:
time: 20.5 us; the launch traced here: 20.2 us
  starting transfers between devices  11.1 us (54%)
  Pallas kernels  4.34 us (21%)
  waiting for transfers between devices  3.96 us (19%)
  between operations  0.71 us (3%)
    ppermute x4, starting transfers between devices, ring(): return lax.ppermute(x, 'spec', [(s, (s + k) % dests) for s in range(dests)])  6.8 us
    ppermute x2, starting transfers between devices, shards(): from_odd = lax.ppermute(to_odd, 'tile', odds)  4.3 us
    ppermute x4, waiting for transfers between devices, ring(): return lax.ppermute(x, 'spec', [(s, (s + k) % dests) for s in range(dests)])  2.32 us
    pallas_call x1, Pallas kernels, shards(): pl.pallas_call(functools.partial(chemistry_kernel, dests, early), out_sha...  2.24 us
    pallas_call x1, Pallas kernels, shards(): pl.pallas_call(functools.partial(pack_kernel, length, halves, cells // BL...  1.02 us
    ppermute x2, waiting for transfers between devices, shards(): from_even = lax.ppermute(to_even, 'tile', evens)  0.89 us
    ppermute x2, waiting for transfers between devices, shards(): from_odd = lax.ppermute(to_odd, 'tile', odds)  0.75 us
    pallas_call x1, Pallas kernels, shards(): pl.pallas_call(functools.partial(inner_kernel, dests, length, halves), ou...  0.69 us
  transfers between devices with their start and end apart: 8, of which 3 were waited for; matrix products, arithmetic and copies ran while one was open for 0% of the time, Pallas kernels for 5%

profile of v11, /device:TPU:0, one launch (start us, length us, event | category | flops | bytes accessed | tf_op | source)
XLA Modules:
  0.0 20.2 jit_solution(5821438238920598371)
XLA Ops:
  0.6 0.0 copy-start
  0.6 0.0 copy-start.1
  0.7 1.0 %pack_edges.1 = (f32[88,128]{1,0:T(8,128)S(1)}, f32[88,128]{1,0:T(8,128)S(1)}, f32[8,128]{1,0:T(8,128)S(1)}, s32[1,16]{1,0:T(1,128)S(1)}) custom-call(f32[8,128,128]{2,1,0:T(8,128)} %bitcast.18, f32[128,128]{1,0:T(8,128)} %bitcast.21, s32[16]{0:T(128)} %bitcast.26, s32[16]{0:T(128)} %bitcast.28, s32[1,16]{1,0:T(1,128)} %bitcast.27), custom_call_target="tpu_custom_call" | custom-call | flops 1000000000 | bytes 3000000 | tf_op jit(solution)/shard_map/pack_edges/pallas_call | solution.py:367
  1.7 3.4 %collective-permute-start = (f32[88,128]{1,0:T(8,128)S(1)}, f32[88,128]{1,0:T(8,128)S(1)}, u32[]{:S(2)}, u32[]{:S(2)}) collective-permute-start(f32[88,128]{1,0:T(8,128)S(1)} %get-tuple-element.22), channel_id=1, source_target_pairs={{0,28},{4,8},{8,4},{12,16},{16,12},{20,24},{24,20},{28,0},{1,29},{... | collective-permute-start | bytes 135176 | tf_op jit(solution)/shard_map/ppermute | solution.py:395
  5.1 0.0 collective-permute-start.1
  5.1 0.0 copy-done
  5.1 0.0 copy-done.1
  5.1 0.7 %inner_rows.1 = (bf16[8,4096]{1,0:T(8,128)(2,1)S(1)}, bf16[8,4096]{1,0:T(8,128)(2,1)S(1)}, bf16[8,4096]{1,0:T(8,128)(2,1)S(1)}, bf16[8,4096]{1,0:T(8,128)(2,1)S(1)}) custom-call(f32[1024,128]{1,0:T(8,128)S(1)} %bitcast.19, f32[128,128]{1,0:T(8,128)S(1)} %bitcast.22), custom_call_target="tpu_custom_call" | custom-call | flops 1000000000 | bytes 3000000 | tf_op jit(solution)/shard_map/inner_rows/pallas_call | solution.py:398
  5.8 0.0 copy-start.2
  5.8 2.7 %collective-permute-start.3 = (bf16[8,4096]{1,0:T(8,128)(2,1)S(1)}, bf16[8,4096]{1,0:T(8,128)(2,1)S(1)}, u32[]{:S(2)}, u32[]{:S(2)}) collective-permute-start(bf16[8,4096]{1,0:T(8,128)(2,1)S(1)} %get-tuple-element.33), channel_id=1, source_target_pairs={{0,2},{1,3},{2,0},{3,1},{4,6},{5,7},{6,4},{7,5},{8,10},{9,11},{10,... | collective-permute-start | bytes 196616 | tf_op jit(solution)/shard_map/ppermute | solution.py:408
  8.4 0.0 collective-permute-done.odd_ref
  8.4 0.0 collective-permute-done.1.even_ref
  8.5 0.0 copy-start.3
  8.5 0.2 edge_rows.1
  8.6 1.6 %collective-permute-start.2 = (bf16[8,4096]{1,0:T(8,128)(2,1)S(1)}, bf16[8,4096]{1,0:T(8,128)(2,1)S(1)}, u32[]{:S(2)}, u32[]{:S(2)}) collective-permute-start(bf16[8,4096]{1,0:T(8,128)(2,1)S(1)} %get-tuple-element.32), channel_id=1, source_target_pairs={{0,1},{1,2},{2,3},{3,0},{4,5},{5,6},{6,7},{7,4},{8,9},{9,10},{10,1... | collective-permute-start | bytes 196616 | tf_op jit(solution)/shard_map/ppermute | solution.py:408
  10.3 2.2 %collective-permute-start.4 = (bf16[8,4096]{1,0:T(8,128)(2,1)S(1)}, bf16[8,4096]{1,0:T(8,128)(2,1)S(1)}, u32[]{:S(2)}, u32[]{:S(2)}) collective-permute-start(bf16[8,4096]{1,0:T(8,128)(2,1)S(1)} %get-tuple-element.34), channel_id=1, source_target_pairs={{0,3},{1,0},{2,1},{3,2},{4,7},{5,4},{6,5},{7,6},{8,11},{9,8},{10,9... | collective-permute-start | bytes 196616 | tf_op jit(solution)/shard_map/ppermute | solution.py:408
  12.5 0.0 collective-permute-start.7
  12.5 0.3 %collective-permute-start.5 = (bf16[8,1024]{1,0:T(8,128)(2,1)S(1)}, bf16[8,1024]{1,0:T(8,128)(2,1)S(1)}, u32[]{:S(2)}, u32[]{:S(2)}) collective-permute-start(bf16[8,1024]{1,0:T(8,128)(2,1)S(1)} %get-tuple-element.35), channel_id=1, source_target_pairs={{0,2},{1,3},{2,0},{3,1},{4,6},{5,7},{6,4},{7,5},{8,10},{9,11},{10,... | collective-permute-start | bytes 49160 | tf_op jit(solution)/shard_map/ppermute | solution.py:408
  12.8 0.9 %collective-permute-done.7.refs_7_ = f32[8,128]{1,0:T(8,128)S(1)} collective-permute-done((f32[8,128]{1,0:T(8,128)S(1)}, f32[8,128]{1,0:T(8,128)S(1)}, u32[]{:S(2)}, u32[]{:S(2)}) %collective-permute-start.7) | collective-permute-done | bytes 4128 | tf_op jit(solution)/shard_map/ppermute | solution.py:429
  13.7 0.9 %collective-permute-start.6 = (f32[40,128]{1,0:T(8,128)S(1)}, f32[40,128]{1,0:T(8,128)S(1)}, u32[]{:S(2)}, u32[]{:S(2)}) collective-permute-start(f32[40,128]{1,0:T(8,128)S(1)} %get-tuple-element.36), channel_id=1, source_target_pairs={{0,28},{4,8},{8,4},{12,16},{16,12},{20,24},{24,20},{28,0},{1,29},{... | collective-permute-start | bytes 61448 | tf_op jit(solution)/shard_map/ppermute | solution.py:428
  14.6 0.0 copy-done.2
  14.6 0.0 copy-done.3
  14.6 0.0 copy-start.4
  14.6 0.2 %halved_weights.1 = (bf16[512,32]{1,0:T(8,128)(2,1)S(1)}, bf16[512,512]{1,0:T(8,128)(2,1)S(1)}) custom-call(bf16[32,512]{1,0:T(8,128)(2,1)S(1)} %copy-done.3, bf16[512,512]{1,0:T(8,128)(2,1)S(1)} %copy-done.2, f32[8,128]{1,0:T(8,128)S(1)} %get-tuple-element.28.after_ref.refs_5_), custom_call_target="tpu_custom_call" | custom-call | flops 500000000 | bytes 1500000 | tf_op jit(solution)/shard_map/halved_weights/pallas_call | solution.py:430
  14.8 2.3 %collective-permute-done.5.refs_4_ = bf16[8,1024]{1,0:T(8,128)(2,1)S(1)} collective-permute-done((bf16[8,1024]{1,0:T(8,128)(2,1)S(1)}, bf16[8,1024]{1,0:T(8,128)(2,1)S(1)}, u32[]{:S(2)}, u32[]{:S(2)}) %collective-permute-start.5) | collective-permute-done | bytes 16416 | tf_op jit(solution)/shard_map/ppermute | solution.py:408
  17.1 0.7 %collective-permute-done.6.refs_6_ = f32[40,128]{1,0:T(8,128)S(1)} collective-permute-done((f32[40,128]{1,0:T(8,128)S(1)}, f32[40,128]{1,0:T(8,128)S(1)}, u32[]{:S(2)}, u32[]{:S(2)}) %collective-permute-start.6) | collective-permute-done | bytes 20512 | tf_op jit(solution)/shard_map/ppermute | solution.py:428
  17.9 0.0 collective-permute-done.3.refs_2_
  17.9 0.0 collective-permute-done.2.refs_1_
  17.9 0.0 collective-permute-done.4.refs_3_
  17.9 0.0 copy-done.4
  17.9 2.2 %chemistry.1 = (bf16[4,8,4096]{2,1,0:T(8,128)(2,1)}, f32[1,1]{1,0:T(1,128)}) custom-call(s32[16]{0:T(128)S(1)} %bitcast.25, bf16[512,32]{1,0:T(8,128)(2,1)S(1)} %get-tuple-element.29.w1_ref, bf16[512,512]{1,0:T(8,128)(2,1)S(1)} %get-tuple-element.30.w2_ref, bf16[32,512]{1,0:T(8,128)(2,1)S(1)} %bitcast.24, bf16[8,4096]{1,0:T(8,128)(2,1)S(1)} %get-tuple-element.31.refs_0_, ...), custom_call_target="tpu_custom_call" | custom-call | flops 4000000000 | bytes 12000000 | tf_op jit(solution)/shard_map/chemistry/pallas_call | solution.py:439
Async XLA Ops:
  0.6 4.5 %copy-start = (f32[8,64,256]{2,1,0:T(8,128)S(1)}, f32[8,64,256]{2,1,0:T(8,128)}, u32[]{:S(2)}) copy-start(f32[8,64,256]{2,1,0:T(8,128)} %param.7) | copy-start | bytes 1572868
  0.6 4.4 %copy-start.1 = (f32[64,256]{1,0:T(8,128)S(1)}, f32[64,256]{1,0:T(8,128)}, u32[]{:S(2)}) copy-start(f32[64,256]{1,0:T(8,128)} %param.8) | copy-start | bytes 196612
  1.7 6.8 %collective-permute-start = (f32[88,128]{1,0:T(8,128)S(1)}, f32[88,128]{1,0:T(8,128)S(1)}, u32[]{:S(2)}, u32[]{:S(2)}) collective-permute-start(f32[88,128]{1,0:T(8,128)S(1)} %get-tuple-element.22), channel_id=1, source_target_pairs={{0,28},{4,8},{8,4},{12,16},{16,12},{20,24},{24,20},{28,0},{1,29},{... | collective-permute-start | bytes 135176 | tf_op jit(solution)/shard_map/ppermute | solution.py:395
  5.1 3.4 %collective-permute-start.1 = (f32[88,128]{1,0:T(8,128)S(1)}, f32[88,128]{1,0:T(8,128)S(1)}, u32[]{:S(2)}, u32[]{:S(2)}) collective-permute-start(f32[88,128]{1,0:T(8,128)S(1)} %get-tuple-element.23), channel_id=1, source_target_pairs={{0,4},{4,0},{8,12},{12,8},{16,20},{20,16},{24,28},{28,24},{1,5},{5... | collective-permute-start | bytes 135176 | tf_op jit(solution)/shard_map/ppermute | solution.py:396
  5.8 8.8 %copy-start.2 = (bf16[512,512]{1,0:T(8,128)(2,1)S(1)}, bf16[512,512]{1,0:T(8,128)(2,1)}, u32[]{:S(2)}) copy-start(bf16[512,512]{1,0:T(8,128)(2,1)} %w2_ref.1) | copy-start | bytes 1572868
  5.8 12.1 %collective-permute-start.3 = (bf16[8,4096]{1,0:T(8,128)(2,1)S(1)}, bf16[8,4096]{1,0:T(8,128)(2,1)S(1)}, u32[]{:S(2)}, u32[]{:S(2)}) collective-permute-start(bf16[8,4096]{1,0:T(8,128)(2,1)S(1)} %get-tuple-element.33), channel_id=1, source_target_pairs={{0,2},{1,3},{2,0},{3,1},{4,6},{5,7},{6,4},{7,5},{8,10},{9,11},{10,... | collective-permute-start | bytes 196616 | tf_op jit(solution)/shard_map/ppermute | solution.py:408
  8.5 6.1 %copy-start.3 = (bf16[32,512]{1,0:T(8,128)(2,1)S(1)}, bf16[32,512]{1,0:T(8,128)(2,1)}, u32[]{:S(2)}) copy-start(bf16[32,512]{1,0:T(8,128)(2,1)} %w1_ref.1) | copy-start | bytes 98308
  8.6 9.3 %collective-permute-start.2 = (bf16[8,4096]{1,0:T(8,128)(2,1)S(1)}, bf16[8,4096]{1,0:T(8,128)(2,1)S(1)}, u32[]{:S(2)}, u32[]{:S(2)}) collective-permute-start(bf16[8,4096]{1,0:T(8,128)(2,1)S(1)} %get-tuple-element.32), channel_id=1, source_target_pairs={{0,1},{1,2},{2,3},{3,0},{4,5},{5,6},{6,7},{7,4},{8,9},{9,10},{10,1... | collective-permute-start | bytes 196616 | tf_op jit(solution)/shard_map/ppermute | solution.py:408
  10.3 7.6 %collective-permute-start.4 = (bf16[8,4096]{1,0:T(8,128)(2,1)S(1)}, bf16[8,4096]{1,0:T(8,128)(2,1)S(1)}, u32[]{:S(2)}, u32[]{:S(2)}) collective-permute-start(bf16[8,4096]{1,0:T(8,128)(2,1)S(1)} %get-tuple-element.34), channel_id=1, source_target_pairs={{0,3},{1,0},{2,1},{3,2},{4,7},{5,4},{6,5},{7,6},{8,11},{9,8},{10,9... | collective-permute-start | bytes 196616 | tf_op jit(solution)/shard_map/ppermute | solution.py:408
  12.5 1.2 %collective-permute-start.7 = (f32[8,128]{1,0:T(8,128)S(1)}, f32[8,128]{1,0:T(8,128)S(1)}, u32[]{:S(2)}, u32[]{:S(2)}) collective-permute-start(f32[8,128]{1,0:T(8,128)S(1)} %get-tuple-element.37), channel_id=1, source_target_pairs={{0,4},{4,0},{8,12},{12,8},{16,20},{20,16},{24,28},{28,24},{1,5},{5... | collective-permute-start | bytes 12296 | tf_op jit(solution)/shard_map/ppermute | solution.py:429
  12.5 4.6 %collective-permute-start.5 = (bf16[8,1024]{1,0:T(8,128)(2,1)S(1)}, bf16[8,1024]{1,0:T(8,128)(2,1)S(1)}, u32[]{:S(2)}, u32[]{:S(2)}) collective-permute-start(bf16[8,1024]{1,0:T(8,128)(2,1)S(1)} %get-tuple-element.35), channel_id=1, source_target_pairs={{0,2},{1,3},{2,0},{3,1},{4,6},{5,7},{6,4},{7,5},{8,10},{9,11},{10,... | collective-permute-start | bytes 49160 | tf_op jit(solution)/shard_map/ppermute | solution.py:408
  13.7 4.2 %collective-permute-start.6 = (f32[40,128]{1,0:T(8,128)S(1)}, f32[40,128]{1,0:T(8,128)S(1)}, u32[]{:S(2)}, u32[]{:S(2)}) collective-permute-start(f32[40,128]{1,0:T(8,128)S(1)} %get-tuple-element.36), channel_id=1, source_target_pairs={{0,28},{4,8},{8,4},{12,16},{16,12},{20,24},{24,20},{28,0},{1,29},{... | collective-permute-start | bytes 61448 | tf_op jit(solution)/shard_map/ppermute | solution.py:428
  14.6 3.3 %copy-start.4 = (bf16[512,32]{0,1:T(8,128)(2,1)S(1)}, bf16[512,32]{0,1:T(8,128)(2,1)}, u32[]{:S(2)}) copy-start(bf16[512,32]{0,1:T(8,128)(2,1)} %param.11) | copy-start | bytes 98308
